TPU v7x, 512 devices: a whole 4x4x16 slice. The times are simulated.
512 devices in a mesh: dp: 16 (over y, x_hi, core), mp: 32 (over z, x_lo).
Axes of the slice: x: 4 (x_hi: 2, x_lo: 2; x = x_hi * 2 + x_lo), y: 4, z: 16, core: 2. Of those that a mesh axis runs over, the one named last changes fastest.
Arguments:
- hidden: bfloat16 [2048, 2048], P('dp')
- head_weight: bfloat16 [126976, 2048], P('mp', 'dp')
- targets: int32 [2048], P('dp'), may hold values from 0 to 126975
- segments: int32 [2048], P('dp'), may hold values from 0 to 63, never falling along the last dimension, each value on 1 to 64 neighbouring positions
- loss_mask: int32 [2048], P('dp'), may hold values 0 or 1
- row_state: float32 [126976], P('mp'), may hold values from 1e-20 to 1e-06
- column_state: float32 [2048], P('dp'), may hold values from 1e-12 to 1e-08
Outputs:
- update_step: bfloat16 [126976, 2048], P('mp', 'dp')
- total_loss: float32 [], replicated
Inputs may be any that keep to these rules, and one draw needn't show every extreme that they name: `segments`: segment ids never fall along the tokens; a segment covers 1 to 64 tokens.
All inputs are finite; a program needn't handle non-finite values. No bound on the sum of `loss_mask` on one device may be relied on, other than what follows from the above.
Results may differ from a plain program's by a relative error of at most 0.0039.
Values may be sent and summed in bfloat16 or wider, within the bound.
No kernel may reach another device: no remote copies, remote signals or barrier semaphores. Data moves between devices by JAX's collectives and lax.ppermute only.
A program may use at most 128 MiB of HBM per device.

v0:
```python
import jax
import jax.numpy as jnp
from jax import lax
from jax.sharding import PartitionSpec as P

D = 2048
V = 126976


penalty = 0.25
decay_rate = 1.0 - 16.0 ** (-0.8)
clip_limit = 1.0


def per_device(hidden, head_weight, targets, segments, loss_mask, row_state, column_state):
    tok_rows = hidden.shape[0]
    voc_rows, col_count = head_weight.shape
    seg_count = tok_rows * lax.axis_size("dp") // 32
    voc_start = lax.axis_index("mp") * voc_rows
    mask_value = loss_mask.astype(jnp.float32)
    member = (segments[:, None] == jnp.arange(seg_count, dtype=jnp.int32)[None, :]).astype(
        jnp.float32
    )
    counts = lax.psum(jnp.sum(member * mask_value[:, None], axis=0), "dp")
    tok_weight = (
        mask_value / jnp.maximum(jnp.sum(member * counts[None, :], axis=1), 1.0) / seg_count
    )
    token_columns = lax.all_to_all(hidden, "dp", split_axis=1, concat_axis=0, tiled=True)
    section = hidden
    logits = lax.dot_general(
        section,
        lax.all_gather(head_weight, "dp", axis=1, tiled=True),
        (((1,), (1,)), ((), ())),
        preferred_element_type=jnp.float32,
    )
    target_hit = jnp.arange(voc_rows, dtype=jnp.int32)[None, :] + voc_start == targets[:, None]
    row_max = lax.pmax(jnp.max(logits, axis=1), "mp")
    shifted = jnp.exp(logits - row_max[:, None])
    exp_sum, exp_dot, target_logit = lax.psum(
        (
            jnp.sum(shifted, axis=1),
            jnp.sum(shifted * logits, axis=1),
            jnp.sum(jnp.where(target_hit, logits, 0.0), axis=1),
        ),
        "mp",
    )
    log_total = row_max + jnp.log(exp_sum)
    entropy = log_total - exp_dot / exp_sum
    token_loss = log_total - target_logit - penalty * entropy
    local_loss = jnp.sum(tok_weight * token_loss)
    total_loss = lax.psum(local_loss, "dp")
    probability = jnp.exp(logits - log_total[:, None])
    score_grad = (
        tok_weight[:, None]
        * (
            probability
            - target_hit.astype(jnp.float32)
            + penalty * probability * (logits - log_total[:, None] + entropy[:, None])
        )
    ).astype(jnp.bfloat16)
    section = token_columns
    head_grad = lax.dot_general(
        lax.all_gather(score_grad, "dp", axis=0, tiled=True),
        section,
        (((0,), (0,)), ((), ())),
        preferred_element_type=jnp.float32,
    )
    squared = head_grad * head_grad
    row_part = jnp.sum(squared, axis=1)
    row_sums = lax.psum(row_part, "dp")
    row_new = decay_rate * row_state + (1.0 - decay_rate) * (row_sums / D)
    column_sums, row_total = lax.psum((jnp.sum(squared, axis=0), jnp.sum(row_new)), "mp")
    column_new = decay_rate * column_state + (1.0 - decay_rate) * (column_sums / V)
    row_mean = row_total / V
    unclipped = (
        head_grad
        * lax.rsqrt(row_new)[:, None]
        * (jnp.sqrt(row_mean) * lax.rsqrt(column_new))[None, :]
    )
    square_total = lax.psum(jnp.sum(unclipped * unclipped), ("dp", "mp"))
    update_rms = jnp.sqrt(square_total / (V * D))
    update_step = (unclipped / jnp.maximum(1.0, update_rms / clip_limit)).astype(jnp.bfloat16)
    return (update_step, total_loss)


def solution(mesh):
    return jax.shard_map(
        per_device,
        mesh=mesh,
        in_specs=(P("dp", None), P("mp", "dp"), P("dp"), P("dp"), P("dp"), P("mp"), P("dp")),
        out_specs=(P("mp", "dp"), P()),
        check_vma=False,
    )
```

profile of v0, /device:TPU:1, one launch (start us, length us, event | category | flops | bytes accessed | tf_op | source)
XLA Modules:
  0.0 690.4 jit_solution(6801189515636697517)
XLA Ops:
  7.2 0.7 all-gather.3.cloned.1.call-update
  7.9 0.7 convert_element_type.13
  8.6 0.8 select_reduce_fusion.1
  9.4 39.7 %psum.63 = f32[64]{0:T(128)S(1)} all-reduce(f32[64]{0:T(128)S(1)} %select_reduce_fusion.1), channel_id=1, replica_groups=mesh['dp'=16,'mp'=32] {'dp'}, use_global_device_ids=true, to_apply=%region_1.0 | all-reduce | flops 64 | bytes 512 | tf_op jit(solution)/shard_map/psum | solution.py:24
  49.0 0.7 select_reduce_fusion
  49.8 0.7 fusion.8
  50.4 98.3 %all-gather.3.cloned.1.call-done = bf16[3968,2048]{1,0:T(8,128)(2,1)} async-done(((bf16[3968,128]{1,0:T(8,128)(2,1)}), bf16[3968,2048]{1,0:T(8,128)(2,1)}) %all-gather.3.cloned.1.call-update) | async-done | bytes 16252944 | tf_op jit(solution)/shard_map/all_gather | solution.py:32
  148.7 11.3 %fusion.9 = (f32[128]{0:T(128)S(1)}, f32[128,3968]{1,0:T(8,128)S(1)}) fusion(bf16[128,2048]{1,0:T(8,128)(2,1)} %param.7, bf16[3968,2048]{1,0:T(8,128)(2,1)} %all-gather.3.cloned.1.call-done), kind=kOutput, calls=%fused_computation.28 | convolution fusion | flops 2080882560 | bytes 18809344 | tf_op jit(solution)/shard_map/dot_general | solution.py:30
  160.0 50.0 %pmax.7 = f32[128]{0:T(128)S(1)} all-reduce(f32[128]{0:T(128)S(1)} %get-tuple-element.16), channel_id=1, replica_groups=mesh['dp'=16,'mp'=32] {'mp'}, use_global_device_ids=true, to_apply=%region_4.0 | all-reduce | flops 128 | bytes 1024 | tf_op jit(solution)/shard_map/pmax | solution.py:37
  210.0 0.8 multiply_reduce_fusion.1
  210.8 46.0 %all-reduce.1 = (f32[128]{0:T(128)S(1)}, f32[128]{0:T(128)S(1)}) all-reduce(f32[128]{0:T(128)S(1)} %get-tuple-element.3, f32[128]{0:T(128)S(1)} %get-tuple-element.2), channel_id=1, replica_groups=mesh['dp'=16,'mp'=32] {'mp'}, use_global_device_ids=true, to_apply=%region_6.0 | all-reduce | flops 256 | bytes 2048 | tf_op jit(solution)/shard_map/psum | solution.py:39
  256.8 1.9 fusion.3
  259.0 42.8 %all_to_all.19 = bf16[128,16,128]{0,2,1:T(8,128)(2,1)S(1)} all-to-all(bf16[128,16,128]{0,2,1:T(8,128)(2,1)S(1)} %bitcast.8), channel_id=1, replica_groups=mesh['dp'=16,'mp'=32] {'dp'}, dimensions={1} | all-to-all | bytes 1048576 | tf_op jit(solution)/shard_map/all_to_all | solution.py:28
  301.9 0.3 copy.12
  302.2 102.1 %all-gather.5.cloned.1.call-done = bf16[2048,3968]{1,0:T(8,128)(2,1)} async-done(((bf16[128,3968]{1,0:T(8,128)(2,1)}), bf16[2048,3968]{1,0:T(8,128)(2,1)}) %all-gather.5.cloned.1.call-update) | async-done | bytes 16252944 | tf_op jit(solution)/shard_map/all_gather | solution.py:63
  404.3 8.6 %multiply_reduce_fusion.3 = (f32[3968]{0:T(1024)S(1)}, f32[128]{0:T(128)S(1)}, f32[3968,128]{1,0:T(8,128)S(1)}) fusion(bf16[2048,3968]{1,0:T(8,128)(2,1)} %all-gather.5.cloned.1.call-done, bf16[2048,128]{1,0:T(8,128)(2,1)S(1)} %bitcast.9), kind=kOutput, calls=%fused_computation.14 | convolution fusion | flops 2081894400 | bytes 18825216 | tf_op jit(solution)/shard_map/dot_general | solution.py:62
  412.8 59.8 %psum.66 = f32[3968]{0:T(1024)S(1)} all-reduce(f32[3968]{0:T(1024)S(1)} %get-tuple-element.5), channel_id=1, replica_groups=mesh['dp'=16,'mp'=32] {'dp'}, use_global_device_ids=true, to_apply=%region_10.11 | all-reduce | flops 3968 | bytes 31744 | tf_op jit(solution)/shard_map/psum | solution.py:70
  472.7 0.6 fusion.7
  473.3 51.6 %all-reduce = (f32[128]{0:T(128)S(1)}, f32[]{:T(128)}, f32[128]{0:T(128)S(1)}) all-reduce(f32[128]{0:T(128)S(1)} %get-tuple-element.6, f32[]{:T(128)} %get-tuple-element.15, f32[128]{0:T(128)S(1)} %get-tuple-element.4), channel_id=1, replica_groups=mesh['dp'=16,'mp'=32] {'mp'}, use_global_device_ids=true, to_apply=%region_14.15 | all-reduce | flops 257 | bytes 2056 | tf_op jit(solution)/shard_map/psum | solution.py:72
  525.6 0.6 multiply_reduce_fusion.4
  526.2 2.3 multiply_reduce_fusion
  528.5 52.9 %psum.71 = f32[]{:T(128)} all-reduce(f32[]{:T(128)} %multiply_reduce_fusion.4), channel_id=1, replica_groups=mesh['dp'=16,'mp'=32] {'dp'}, use_global_device_ids=true, to_apply=%region_20.21 | all-reduce | flops 1 | bytes 8 | tf_op jit(solution)/shard_map/psum | solution.py:51
  581.4 98.9 %psum.69 = f32[]{:T(128)} all-reduce(f32[]{:T(128)} %multiply_reduce_fusion), channel_id=1, replica_groups=mesh['dp'=16,'mp'=32] {'dp','mp'}, use_global_device_ids=true, to_apply=%region_16.17 | all-reduce | flops 1 | bytes 8 | tf_op jit(solution)/shard_map/psum | solution.py:80
  681.0 2.5 divide_convert_fusion
  (15 shorter events, 0.4 us)
Async XLA Ops:
  7.2 141.6 %all-gather.3.cloned.1.call-start = ((), (), s32[]{:S(2)}) async-start(), calls=%async_computation.1 | async-start | bytes 17268736 | tf_op jit(solution)/shard_map/all_gather | solution.py:32
  7.9 396.4 %all-gather.5.cloned.1.call-start = ((), (), s32[]{:S(2)}) async-start(), calls=%async_computation.2 | async-start | bytes 17268736 | tf_op jit(solution)/shard_map/all_gather | solution.py:63
  50.4 159.6 %copy-start.2 = (s32[128]{0:T(128)S(1)}, s32[128]{0:T(128)}, u32[]{:S(2)}) copy-start(s32[128]{0:T(128)} %param.9) | copy-start | bytes 1540
  256.8 1.9 copy-start
  404.3 68.4 %copy-start.1 = (f32[3968]{0:T(1024)S(1)}, f32[3968]{0:T(1024)}, u32[]{:S(2)}) copy-start(f32[3968]{0:T(1024)} %param.12) | copy-start | bytes 47620
  404.3 121.9 %copy-start.3 = (f32[128]{0:T(128)S(1)}, f32[128]{0:T(128)}, u32[]{:S(2)}) copy-start(f32[128]{0:T(128)} %param.13) | copy-start | bytes 1540
Sparse Core Ops, SparseCore 0:
  11.2 137.4 all-gather.2
  258.9 145.3 all-gather.4
where the time goes:
time: 691 us; the launch traced here: 690 us
  blocking collectives  442 us (64%)
  waiting for transfers between devices  201 us (29%)
  matrix products  19.9 us (3%)
  between operations  15.5 us (2%)
  other arithmetic  11.5 us (2%)
    all_gather x1, waiting for transfers between devices, per_device(): lax.all_gather(score_grad, 'dp', axis=0, tiled=True)  102 us
    psum x1, blocking collectives, per_device(): square_total = lax.psum(jnp.sum(unclipped * unclipped), ('dp', 'mp'))  98.9 us
    all_gather x1, waiting for transfers between devices, per_device(): lax.all_gather(head_weight, 'dp', axis=1, tiled=True)  98.3 us
    psum x1, blocking collectives, per_device(): row_sums = lax.psum(row_part, 'dp')  59.8 us
    psum x1, blocking collectives, per_device(): total_loss = lax.psum(local_loss, 'dp')  52.9 us
    psum x1, blocking collectives, per_device(): lax.psum((jnp.sum(squared, axis=0), jnp.sum(row_new)), 'mp')  51.6 us
    pmax x1, blocking collectives, per_device(): row_max = lax.pmax(jnp.max(logits, axis=1), 'mp')  50 us
    psum x1, blocking collectives, per_device(): lax.psum((jnp.sum(shifted, axis=1), jnp.sum(shifted * logits, axis=1), jn...  46 us
  transfers between devices with their start and end apart: 2, of which 2 were waited for; matrix products, arithmetic and copies ran while one was open for 0% of the time, Pallas kernels for 0%

commit v1 on v0

v1 whole, which is shorter than its diff:
```python
import jax
import jax.numpy as jnp
from jax import lax
from jax.sharding import Mesh, PartitionSpec as P

D = 2048
V = 126976

penalty = 0.25
decay_rate = 1.0 - 16.0 ** (-0.8)
clip_limit = 1.0

AXES = ("y", "xh", "core", "z", "xl")
DP = ("y", "xh", "core")
MP = ("z", "xl")
CHIPS = ("y", "xh")
PLANE = ("y", "xh", "xl")


def swap_cores(value):
    return lax.ppermute(value, "core", [(0, 1), (1, 0)])


def spread(value, axes):
    count = lax.axis_size(axes)
    return lax.all_to_all(
        jnp.broadcast_to(value[None], (count,) + value.shape), axes, 0, 0
    )


def pieces(value):
    high = lax.reduce_precision(value, 8, 7)
    rest = value - high
    middle = lax.reduce_precision(rest, 8, 7)
    low = rest - middle
    return [part.astype(jnp.bfloat16) for part in (high, middle, low)]


def merge_scores(stats):
    row_max = jnp.max(stats[:, 0], axis=0)
    factor = jnp.exp(stats[:, 0] - row_max[None])
    return jnp.stack(
        [
            row_max,
            jnp.sum(stats[:, 1] * factor, axis=0),
            jnp.sum(stats[:, 2] * factor, axis=0),
            jnp.sum(stats[:, 3], axis=0),
        ]
    )


def per_device(hidden, head_weight, targets, segments, loss_mask, row_state, column_state):
    tok_rows = hidden.shape[0]
    voc_rows, cols = head_weight.shape
    chips = lax.axis_size(CHIPS)
    seg_count = tok_rows * chips * 2 // 32
    chip_rows = voc_rows // chips
    own_rows = chip_rows // 2
    core = lax.axis_index("core")
    chip = lax.axis_index(CHIPS)
    row_start = lax.axis_index(MP) * voc_rows + chip * chip_rows

    info = jnp.stack(
        [
            (targets >> 16).astype(jnp.bfloat16),
            ((targets >> 8) & 255).astype(jnp.bfloat16),
            (targets & 255).astype(jnp.bfloat16),
            segments.astype(jnp.bfloat16),
            loss_mask.astype(jnp.bfloat16),
        ]
        + pieces(column_state)
    )
    info = jnp.concatenate([info, jnp.zeros_like(info)], axis=0)
    head_part = jnp.concatenate(
        [
            head_weight.reshape(chips, chip_rows, cols),
            jnp.broadcast_to(info[None], (chips,) + info.shape),
        ],
        axis=1,
    )
    tall = chip_rows + 16
    wide = D // cols
    head_part = (
        head_part.reshape(chips, tall // wide // 16, wide, 16, cols)
        .transpose(0, 1, 3, 2, 4)
        .reshape(chips, tall // wide, D)
    )
    sent = jnp.concatenate(
        [jnp.broadcast_to(hidden[None], (chips,) + hidden.shape), head_part], axis=1
    )
    got = lax.all_to_all(sent, CHIPS, 0, 0)
    hidden_own = got[:, :tok_rows].reshape(chips * tok_rows, D)
    head_got = (
        got[:, tok_rows:]
        .reshape(chips, tall // wide // 16, 16, wide, cols)
        .transpose(0, 1, 3, 2, 4)
        .reshape(chips, tall, cols)
    )
    head_other = swap_cores(head_got)
    both = jnp.where(
        core == 0,
        jnp.stack([head_got, head_other], axis=1),
        jnp.stack([head_other, head_got], axis=1),
    )
    rows = both[:, :, :chip_rows].transpose(2, 0, 1, 3).reshape(chip_rows, D)
    facts = both[:, :, chip_rows : chip_rows + 8].astype(jnp.float32)

    all_segments = facts[:, :, 3]
    all_masks = facts[:, :, 4]
    own_facts = lax.dynamic_index_in_dim(facts, core, axis=1, keepdims=False)
    own_segments = own_facts[:, 3].reshape(-1)
    own_mask = own_facts[:, 4].reshape(-1)
    own_targets = (
        own_facts[:, 0] * 65536.0 + own_facts[:, 1] * 256.0 + own_facts[:, 2]
    ).reshape(-1).astype(jnp.int32)
    seg_ids = jnp.arange(seg_count, dtype=jnp.int32).astype(jnp.float32)
    counts = jnp.sum(
        jnp.where(
            all_segments.reshape(1, -1) == seg_ids[:, None], all_masks.reshape(1, -1), 0.0
        ),
        axis=1,
    )
    own_counts = jnp.sum(
        jnp.where(own_segments[None, :] == seg_ids[:, None], counts[:, None], 0.0), axis=0
    )
    tok_weight = own_mask / jnp.maximum(own_counts, 1.0) / seg_count
    full_column_state = (facts[:, :, 5] + facts[:, :, 6] + facts[:, :, 7]).reshape(-1)

    logits = lax.dot_general(
        rows, hidden_own, (((1,), (1,)), ((), ())), preferred_element_type=jnp.float32
    )
    target_hit = (
        jnp.arange(chip_rows, dtype=jnp.int32)[:, None] + row_start == own_targets[None, :]
    )
    local_max = jnp.max(logits, axis=0)
    shifted = jnp.exp(logits - local_max[None])
    stats = jnp.stack(
        [
            local_max,
            jnp.sum(shifted, axis=0),
            jnp.sum(shifted * logits, axis=0),
            jnp.sum(jnp.where(target_hit, logits, 0.0), axis=0),
        ]
    )
    hidden_other = swap_cores(hidden_own)
    stats = merge_scores(spread(stats, PLANE))
    row_max, exp_sum, exp_dot, target_logit = merge_scores(spread(stats, "z"))
    log_total = row_max + jnp.log(exp_sum)
    entropy = log_total - exp_dot / exp_sum
    token_loss = log_total - target_logit - penalty * entropy
    local_loss = jnp.sum(tok_weight * token_loss)

    probability = jnp.exp(logits - log_total[None])
    score_grad = (
        tok_weight[None]
        * (
            probability
            - target_hit.astype(jnp.float32)
            + penalty * probability * (logits - log_total[None] + entropy[None])
        )
    ).astype(jnp.bfloat16)
    score_halves = score_grad.reshape(2, own_rows, -1)
    score_own = lax.dynamic_index_in_dim(score_halves, core, axis=0, keepdims=False)
    score_away = lax.dynamic_index_in_dim(score_halves, 1 - core, axis=0, keepdims=False)
    score_other = swap_cores(score_away)
    head_grad = lax.dot_general(
        score_own, hidden_own, (((1,), (0,)), ((), ())), preferred_element_type=jnp.float32
    ) + lax.dot_general(
        score_other, hidden_other, (((1,), (0,)), ((), ())), preferred_element_type=jnp.float32
    )
    squared = head_grad * head_grad
    own_state = lax.dynamic_slice_in_dim(
        row_state, chip * chip_rows + core * own_rows, own_rows, axis=0
    )
    row_new = decay_rate * own_state + (1.0 - decay_rate) * (jnp.sum(squared, axis=1) / D)
    scaled = head_grad * lax.rsqrt(row_new)[:, None]
    tail = jnp.zeros((cols,), jnp.float32).at[0].set(jnp.sum(row_new)).at[1].set(local_loss)
    sums = jnp.concatenate([jnp.sum(squared, axis=0), jnp.sum(scaled * scaled, axis=0), tail])
    sums = lax.psum(sums.reshape(-1, cols), "core")
    total_loss = sums[-1, 1]
    sums = jnp.sum(spread(sums, PLANE), axis=0)
    sums = jnp.sum(spread(sums, "z"), axis=0).reshape(-1)
    column_new = decay_rate * full_column_state + (1.0 - decay_rate) * (sums[:D] / V)
    row_mean = sums[2 * D] / V
    column_scale = lax.rsqrt(column_new)
    square_total = row_mean * jnp.sum(sums[D : 2 * D] * column_scale * column_scale)
    update_rms = jnp.sqrt(square_total / (V * D))
    factor = jnp.sqrt(row_mean) * column_scale / jnp.maximum(1.0, update_rms / clip_limit)
    update = (scaled * factor[None]).astype(jnp.bfloat16)
    update = update.reshape(own_rows, 2 * chips, cols).transpose(1, 0, 2)
    update_step = lax.all_to_all(update, DP, 0, 0).reshape(voc_rows, cols)
    return (update_step, total_loss)


def solution(mesh):
    fine = Mesh(mesh.devices.reshape(4, 2, 2, 16, 2), AXES)
    return jax.shard_map(
        per_device,
        mesh=fine,
        in_specs=(P(DP, None), P(MP, DP), P(DP), P(DP), P(DP), P(MP), P(DP)),
        out_specs=(P(MP, DP), P()),
        check_vma=False,
    )
```

time: 691 us -> 229 us (0.33)
  blocking collectives: 442 us -> 92.8 us
  waiting for transfers between devices: 201 us -> 42.3 us
  starting transfers between devices: 0.08 us -> 47.5 us
  local copies, waits for them, and re-layouts: 0.57 us -> 19.1 us
  between operations: 15.5 us -> 2.42 us
  matrix products: 19.9 us -> 12.2 us
    psum x6 -> x1, blocking collectives: 349 us -> 3.39 us  [per_device(): sums = lax.psum(sums.reshape(-1, cols), 'core')]
    all_gather x2 -> x0, waiting for transfers between devices: 200 us -> none  [the longest x1 102 us: per_device(): lax.all_gather(score_grad, 'dp', axis=0, tiled=True)]
    pmax x1 -> x0, blocking collectives: 50 us -> none  [per_device(): row_max = lax.pmax(jnp.max(logits, axis=1), 'mp')]
    all_to_all x1 -> x3, blocking collectives: 42.8 us -> 89.4 us  [the longest x1 67 us: per_device(): got = lax.all_to_all(sent, CHIPS, 0, 0)]
    all_to_all x0 -> x3, waiting for transfers between devices: none -> 42.3 us  [the longest x2 26 us: spread(): lax.all_to_all(jnp.broadcast_to(value[None], (count,) + value.shape), axe...]
    all_to_all x0 -> x3, starting transfers between devices: none -> 31.5 us  [the longest x2 20.2 us: spread(): lax.all_to_all(jnp.broadcast_to(value[None], (count,) + value.shape), axe...]
    ppermute x0 -> x3, starting transfers between devices: none -> 16 us  [swap_cores(): return lax.ppermute(value, 'core', [(0, 1), (1, 0)])]
    dot_general x2 -> x3, matrix products: 19.9 us -> 12.2 us  [the longest x1 5.21 us: per_device(): lax.dot_general(rows, hidden_own, (((1,), (1,)), ((), ())), preferred_ele...]
  transfers between devices with their start and end apart: 2 -> 6, of which waited for: 2 -> 3; matrix products, arithmetic and copies ran while one was open for 0% -> 10% of each run, Pallas kernels for 0% -> 0%
where the time goes in v1:
time: 229 us; the launch traced here: 228 us
  blocking collectives  92.8 us (41%)
  starting transfers between devices  47.5 us (21%)
  waiting for transfers between devices  42.3 us (18%)
  local copies, waits for them, and re-layouts  19.1 us (8%)
  matrix products  12.2 us (5%)
  other arithmetic  11.7 us (5%)
  between operations  2.42 us (1%)
    all_to_all x1, blocking collectives, per_device(): got = lax.all_to_all(sent, CHIPS, 0, 0)  67 us
    all_to_all x2, waiting for transfers between devices, spread(): lax.all_to_all(jnp.broadcast_to(value[None], (count,) + value.shape), axe...  26 us
    all_to_all x2, blocking collectives, spread(): lax.all_to_all(jnp.broadcast_to(value[None], (count,) + value.shape), axe...  22.4 us
    all_to_all x2, starting transfers between devices, spread(): lax.all_to_all(jnp.broadcast_to(value[None], (count,) + value.shape), axe...  20.2 us
    all_to_all x1, waiting for transfers between devices, per_device(): update_step = lax.all_to_all(update, DP, 0, 0).reshape(voc_rows, cols)  16.4 us
    ppermute x3, starting transfers between devices, swap_cores(): return lax.ppermute(value, 'core', [(0, 1), (1, 0)])  16 us
    all_to_all x1, starting transfers between devices, per_device(): update_step = lax.all_to_all(update, DP, 0, 0).reshape(voc_rows, cols)  11.3 us
    dot_general x1, matrix products, per_device(): lax.dot_general(rows, hidden_own, (((1,), (1,)), ((), ())), preferred_ele...  5.21 us
  transfers between devices with their start and end apart: 6, of which 3 were waited for; matrix products, arithmetic and copies ran while one was open for 10% of the time, Pallas kernels for 0%

profile of v1, /device:TPU:1, one launch (start us, length us, event | category | flops | bytes accessed | tf_op | source)
XLA Modules:
  0.0 228.1 jit_solution(15344421748724962985)
XLA Ops:
  2.7 1.3 pad_maximum_fusion.1
  5.5 0.8 pad_maximum_fusion
  6.4 67.0 %all_to_all.30 = bf16[8,160,2048]{2,1,0:T(8,128)(2,1)S(1)} all-to-all(bf16[8,160,2048]{2,1,0:T(8,128)(2,1)S(1)} %pad_maximum_fusion), channel_id=1, replica_groups=mesh['y'=4,'xh'=2,'core'=2,'z'=16,'xl'=2] {'y','xh'}, dimensions={0} | all-to-all | bytes 10485760 | tf_op jit(solution)/shard_map/all_to_all | solution.py:91
  73.4 2.3 %copy-done = bf16[8,160,2048]{2,1,0:T(8,128)(2,1)} copy-done((bf16[8,160,2048]{2,1,0:T(8,128)(2,1)}, bf16[8,160,2048]{2,1,0:T(8,128)(2,1)S(1)}, u32[]{:S(2)}) %copy-start) | copy-done | bytes 5242904
  77.1 5.2 %collective-permute-start = (bf16[8,512,128]{2,0,1:T(8,128)(2,1)S(1)}, bf16[8,512,128]{2,0,1:T(8,128)(2,1)S(1)}, u32[]{:S(2)}, u32[]{:S(2)}) collective-permute-start(bf16[8,512,128]{2,0,1:T(8,128)(2,1)S(1)} %copy.95), channel_id=1, source_target_pairs={{0,32},{32,0},{1,33},{33,1},{2,34},{34,2},{3,35},{35,3},{4,36},{36... | collective-permute-start | bytes 3145736 | tf_op jit(solution)/shard_map/ppermute | solution.py:21
  83.0 4.7 %slice.134 = bf16[8,128,2048]{2,1,0:T(8,128)(2,1)} slice(bf16[8,160,2048]{2,1,0:T(8,128)(2,1)} %copy-done), slice={[0:8], [0:128], [0:2048]} | slice | bytes 8388608 | tf_op jit(solution)/shard_map/slice | solution.py:92
  87.7 1.9 collective-permute-start.2
  90.2 3.3 %copy.102 = bf16[496,8,2,128]{0,3,2,1:T(8,128)(2,1)} copy(bf16[496,8,2,128]{3,1,0,2:T(8,128)(2,1)S(1)} %slice_bitcast_fusion) | data formatting | bytes 4063232 | tf_op jit(solution)/shard_map/transpose | solution.py:105
  93.6 5.2 %fusion.40 = (f32[1024]{0:T(1024)S(1)}, f32[496,1024]{1,0:T(8,128)S(1)}) fusion(bf16[496,2048]{0,1:T(8,128)(2,1)} %bitcast.150, bf16[1024,2048]{1,0:T(8,128)(2,1)} %bitcast.23), kind=kOutput, calls=%fused_computation.99 | convolution fusion | flops 2080881664 | bytes 8261632 | tf_op jit(solution)/shard_map/dot_general | solution.py:129
  99.5 10.8 %all_to_all.31 = f32[16,4,1024]{2,1,0:T(4,128)S(1)} all-to-all(f32[16,4,1024]{2,1,0:T(4,128)S(1)} %broadcast_in_dim.53), channel_id=1, replica_groups=mesh['y'=4,'xh'=2,'core'=2,'z'=16,'xl'=2] {'y','xh','xl'}, dimensions={0} | all-to-all | bytes 524288 | tf_op jit(solution)/shard_map/all_to_all | solution.py:26
  111.4 14.9 %all-to-all-start.2 = ((f32[16,4,1024]{2,1,0:T(4,128)}), f32[16,4,1024]{2,1,0:T(4,128)S(1)}, u32[]{:S(2)}, u32[]{:S(2)}) async-start(f32[16,4,1024]{2,1,0:T(4,128)} %broadcast_in_dim.54), calls=%async_computation.2 | async-start | bytes 524288 | tf_op jit(solution)/shard_map/all_to_all | solution.py:26
  127.3 11.8 %all-to-all-done.2 = f32[16,4,1024]{2,1,0:T(4,128)S(1)} async-done(((f32[16,4,1024]{2,1,0:T(4,128)}), f32[16,4,1024]{2,1,0:T(4,128)S(1)}, u32[]{:S(2)}, u32[]{:S(2)}) %all-to-all-start.2) | async-done | bytes 262176 | tf_op jit(solution)/shard_map/all_to_all | solution.py:26
  140.8 8.8 %collective-permute-start.1 = (bf16[248,1024]{1,0:T(8,128)(2,1)S(1)}, bf16[248,1024]{1,0:T(8,128)(2,1)S(1)}, u32[]{:S(2)}, u32[]{:S(2)}) collective-permute-start(bf16[248,1024]{1,0:T(8,128)(2,1)S(1)} %dynamic-slice_bitcast_fusion), channel_id=1, source_target_pairs={{0,32},{32,0},{1,33},{33,1},{2,34},{34,2},{3,35},{35,3},{4,36},{36... | collective-permute-start | bytes 1523720 | tf_op jit(solution)/shard_map/ppermute | solution.py:21
  149.7 3.4 %fusion.7 = f32[248,2048]{1,0:T(8,128)S(1)} fusion(bf16[1024,2048]{1,0:T(8,128)(2,1)} %bitcast.23, bf16[2,248,1024]{2,1,0:T(8,128)(2,1)S(1)} %bitcast.149, s32[]{:T(128)S(6)} %select_n.34), kind=kOutput, calls=%fused_computation.22 | convolution fusion | flops 1040187392 | bytes 6733828 | tf_op jit(solution)/shard_map/dot_general | solution.py:166
  153.1 3.6 %multiply_reduce_fusion.3 = (f32[248]{0:T(256)S(1)}, f32[248,2048]{1,0:T(8,128)S(1)}) fusion(f32[248,2048]{1,0:T(8,128)S(1)} %fusion.7, bf16[248,1024]{1,0:T(8,128)(2,1)S(1)} %collective-permute-done.1, bf16[1024,2048]{1,0:T(8,128)(2,1)} %collective-permute-done.2), kind=kOutput, calls=%fused_computation.17 | convolution fusion | flops 1041710848 | bytes 8766432 | tf_op jit(solution)/shard_map/dot_general | solution.py:168
  156.7 1.4 fusion.36
  159.8 3.4 %psum.7 = f32[33,128]{1,0:T(8,128)S(1)} all-reduce(f32[33,128]{1,0:T(8,128)S(1)} %maximum_bitcast_fusion), channel_id=1, replica_groups=mesh['y'=4,'xh'=2,'core'=2,'z'=16,'xl'=2] {'core'}, use_global_device_ids=true, to_apply=%region_19.20 | all-reduce | flops 4224 | bytes 33792 | tf_op jit(solution)/shard_map/psum | solution.py:179
  163.2 11.6 %all_to_all.32 = f32[16,33,128]{2,1,0:T(8,128)S(1)} all-to-all(f32[16,33,128]{2,1,0:T(8,128)S(1)} %broadcast_in_dim.55), channel_id=1, replica_groups=mesh['y'=4,'xh'=2,'core'=2,'z'=16,'xl'=2] {'y','xh','xl'}, dimensions={0} | all-to-all | bytes 540672 | tf_op jit(solution)/shard_map/all_to_all | solution.py:26
  175.5 5.3 %all-to-all-start.4 = ((f32[16,33,128]{2,1,0:T(8,128)}), f32[16,33,128]{2,1,0:T(8,128)S(1)}, u32[]{:S(2)}, u32[]{:S(2)}) async-start(f32[16,33,128]{2,1,0:T(8,128)} %broadcast_in_dim.56), calls=%async_computation.4 | async-start | bytes 655360 | tf_op jit(solution)/shard_map/all_to_all | solution.py:26
  180.9 14.2 %all-to-all-done.4 = f32[16,33,128]{2,1,0:T(8,128)S(1)} async-done(((f32[16,33,128]{2,1,0:T(8,128)}), f32[16,33,128]{2,1,0:T(8,128)S(1)}, u32[]{:S(2)}, u32[]{:S(2)}) %all-to-all-start.4) | async-done | bytes 270368 | tf_op jit(solution)/shard_map/all_to_all | solution.py:26
  197.6 1.3 bitcast_bitcast_fusion
  198.9 11.3 %all-to-all-start.5 = ((bf16[16,248,128]{2,1,0:T(8,128)(2,1)}), bf16[16,248,128]{2,1,0:T(8,128)(2,1)S(1)}, u32[]{:S(2)}, u32[]{:S(2)}) async-start(bf16[16,248,128]{2,1,0:T(8,128)(2,1)} %bitcast_bitcast_fusion), calls=%async_computation.5 | async-start | bytes 2031616 | tf_op jit(solution)/shard_map/all_to_all | solution.py:191
  210.7 16.4 %all-to-all-done.5 = bf16[16,248,128]{2,1,0:T(8,128)(2,1)S(1)} async-done(((bf16[16,248,128]{2,1,0:T(8,128)(2,1)}), bf16[16,248,128]{2,1,0:T(8,128)(2,1)S(1)}, u32[]{:S(2)}, u32[]{:S(2)}) %all-to-all-start.5) | async-done | bytes 1015840 | tf_op jit(solution)/shard_map/all_to_all | solution.py:191
  227.1 1.0 copy.164
  (62 shorter events, 14.7 us)
Async XLA Ops:
  4.0 1.0 copy-start.1
  73.4 2.3 %copy-start = (bf16[8,160,2048]{2,1,0:T(8,128)(2,1)}, bf16[8,160,2048]{2,1,0:T(8,128)(2,1)S(1)}, u32[]{:S(2)}) copy-start(bf16[8,160,2048]{2,1,0:T(8,128)(2,1)S(1)} %all_to_all.30) | copy-start | bytes 15728644
  77.1 12.6 %collective-permute-start = (bf16[8,512,128]{2,0,1:T(8,128)(2,1)S(1)}, bf16[8,512,128]{2,0,1:T(8,128)(2,1)S(1)}, u32[]{:S(2)}, u32[]{:S(2)}) collective-permute-start(bf16[8,512,128]{2,0,1:T(8,128)(2,1)S(1)} %copy.95), channel_id=1, source_target_pairs={{0,32},{32,0},{1,33},{33,1},{2,34},{34,2},{3,35},{35,3},{4,36},{36... | collective-permute-start | bytes 3145736 | tf_op jit(solution)/shard_map/ppermute | solution.py:21
  87.7 65.3 %collective-permute-start.2 = (bf16[1024,2048]{1,0:T(8,128)(2,1)}, bf16[1024,2048]{1,0:T(8,128)(2,1)}, u32[]{:S(2)}, u32[]{:S(2)}) collective-permute-start(bf16[1024,2048]{1,0:T(8,128)(2,1)} %bitcast.23), channel_id=1, source_target_pairs={{0,32},{32,0},{1,33},{33,1},{2,34},{34,2},{3,35},{35,3},{4,36},{36... | collective-permute-start | bytes 12582920 | tf_op jit(solution)/shard_map/ppermute | solution.py:21
  111.4 27.7 %all-to-all-start.2 = ((f32[16,4,1024]{2,1,0:T(4,128)}), f32[16,4,1024]{2,1,0:T(4,128)S(1)}, u32[]{:S(2)}, u32[]{:S(2)}) async-start(f32[16,4,1024]{2,1,0:T(4,128)} %broadcast_in_dim.54), calls=%async_computation.2 | async-start | bytes 524288 | tf_op jit(solution)/shard_map/all_to_all | solution.py:26
  140.8 12.3 %collective-permute-start.1 = (bf16[248,1024]{1,0:T(8,128)(2,1)S(1)}, bf16[248,1024]{1,0:T(8,128)(2,1)S(1)}, u32[]{:S(2)}, u32[]{:S(2)}) collective-permute-start(bf16[248,1024]{1,0:T(8,128)(2,1)S(1)} %dynamic-slice_bitcast_fusion), channel_id=1, source_target_pairs={{0,32},{32,0},{1,33},{33,1},{2,34},{34,2},{3,35},{35,3},{4,36},{36... | collective-permute-start | bytes 1523720 | tf_op jit(solution)/shard_map/ppermute | solution.py:21
  159.4 21.5 %copy-start.2 = (f32[8,2,1,128]{3,0,2,1:T(8,128)S(1)}, f32[8,2,1,128]{3,0,2,1:T(8,128)}, u32[]{:S(2)}) copy-start(f32[8,2,1,128]{3,0,2,1:T(8,128)} %get-tuple-element.52) | copy-start | bytes 24580
  175.5 19.5 %all-to-all-start.4 = ((f32[16,33,128]{2,1,0:T(8,128)}), f32[16,33,128]{2,1,0:T(8,128)S(1)}, u32[]{:S(2)}, u32[]{:S(2)}) async-start(f32[16,33,128]{2,1,0:T(8,128)} %broadcast_in_dim.56), calls=%async_computation.4 | async-start | bytes 655360 | tf_op jit(solution)/shard_map/all_to_all | solution.py:26
  198.9 28.2 %all-to-all-start.5 = ((bf16[16,248,128]{2,1,0:T(8,128)(2,1)}), bf16[16,248,128]{2,1,0:T(8,128)(2,1)S(1)}, u32[]{:S(2)}, u32[]{:S(2)}) async-start(bf16[16,248,128]{2,1,0:T(8,128)(2,1)} %bitcast_bitcast_fusion), calls=%async_computation.5 | async-start | bytes 2031616 | tf_op jit(solution)/shard_map/all_to_all | solution.py:191

commit v2 on v0

v2 whole, which is shorter than its diff:
```python
import jax
import jax.numpy as jnp
from jax import lax
from jax.experimental import pallas as pl
from jax.experimental.pallas import tpu as pltpu
from jax.sharding import Mesh, PartitionSpec as P

D = 2048
V = 126976

penalty = 0.25
decay_rate = 1.0 - 16.0 ** (-0.8)
clip_limit = 1.0

AXES = ("y", "xh", "core", "z", "xl")
DP = ("y", "xh", "core")
MP = ("z", "xl")
CHIPS = ("y", "xh")
PLANE = ("y", "xh", "xl")

PEERS = 8
TOK = 128
COLS = 128
VOC = 3968
CHIP_ROWS = 496
OWN = 248
PAD = 256
TOKENS = 1024
SEGS = 64
STEP = 6 * 128
LAST = 4 * 128
f32 = jnp.float32
bf16 = jnp.bfloat16

params = pltpu.CompilerParams(vmem_limit_bytes=24 * 1024 * 1024)
VMEM = pl.BlockSpec(memory_space=pltpu.VMEM)
SMEM = pl.BlockSpec(memory_space=pltpu.SMEM)


def swap_cores(value):
    return lax.ppermute(value, "core", [(0, 1), (1, 0)])


def trade(value, axes):
    return lax.all_to_all(value, axes, 0, 0)


def pack_kernel(hidden, head, targets, segments, mask, state, out):
    out[0, :TOK, :] = hidden[...]
    for block in range(4):
        height = min(128, CHIP_ROWS - 128 * block)
        out[0, TOK : TOK + height, 128 * block : 128 * block + 128] = head[
            128 * block : 128 * block + height, :
        ]
    row = lax.broadcasted_iota(jnp.int32, (16, 128), 0)
    goal = targets[...]
    value = state[...]
    high = value.astype(bf16).astype(f32)
    rest = value - high
    middle = rest.astype(bf16).astype(f32)
    facts = jnp.zeros((16, 128), f32)
    for place, fact in enumerate(
        [
            (goal >> 16).astype(f32),
            ((goal >> 8) & 255).astype(f32),
            (goal & 255).astype(f32),
            segments[...].astype(f32),
            mask[...].astype(f32),
            high,
            middle,
            rest - middle,
        ]
    ):
        facts = jnp.where(row == place, fact, facts)
    out[0, 2 * TOK - 16 :, LAST - 128 :] = facts.astype(bf16)


def pack(hidden, head, targets, segments, mask, state):
    small = pl.BlockSpec((1, 128), lambda i: (0, 0))
    return pl.pallas_call(
        pack_kernel,
        grid=(PEERS,),
        in_specs=[
            pl.BlockSpec((TOK, LAST), lambda i: (0, 3)),
            pl.BlockSpec((CHIP_ROWS, COLS), lambda i: (i, 0)),
            small,
            small,
            small,
            small,
        ],
        out_specs=pl.BlockSpec((1, 2 * TOK, LAST), lambda i: (i, 0, 0)),
        out_shape=jax.ShapeDtypeStruct((PEERS, 2 * TOK, LAST), bf16),
        compiler_params=params,
        name="pack",
    )(hidden, head, *[x.reshape(1, 128) for x in (targets, segments, mask, state)])


def gather_weight(source, rows, weight):
    def one(q, carry):
        columns = pl.ds(pl.multiple_of(q * 128, 128), 128)
        for block in range(4):
            height = min(128, CHIP_ROWS - 128 * block)
            weight[128 * block : 128 * block + height, columns] = source[
                q, rows : rows + height, 128 * block : 128 * block + 128
            ]
        return carry

    lax.fori_loop(0, PEERS, one, 0)


def half_kernel(place, first, near, far, last, hidden, partial, weight):
    core = place[0]
    odd = place[2]

    def fill(source, rows, index, start, count):
        for i in range(count):
            column = start + i // 2 + 8 * (core if i % 2 == 0 else 1 - core)
            hidden[rows, pl.ds(pl.multiple_of(column * 128, 128), 128)] = source[
                index, :TOK, 128 * i : 128 * i + 128
            ]

    def one(q, carry):
        rows = pl.ds(pl.multiple_of(q * TOK, TOK), TOK)
        fill(first, rows, q, 3 * odd, 6)
        fill(last, rows, q, 6, 4)
        return carry

    def two(q, carry):
        fill(near, pl.ds(pl.multiple_of(q * TOK, TOK), TOK), q, 3 - 3 * odd, 6)
        fill(far, pl.ds(pl.multiple_of((q + 4) * TOK, TOK), TOK), q, 3 - 3 * odd, 6)
        return carry

    lax.fori_loop(0, PEERS, one, 0)
    lax.fori_loop(0, PEERS // 2, two, 0)
    gather_weight(last, TOK, weight)
    for block in range(4):
        tokens = slice(256 * block, 256 * block + 256)
        partial[:, tokens] = lax.dot_general(
            weight[...],
            hidden[tokens, : D // 2],
            (((1,), (1,)), ((), ())),
            preferred_element_type=f32,
        )


def half_call(place, first, near, far, last):
    return pl.pallas_call(
        half_kernel,
        in_specs=[SMEM, VMEM, VMEM, VMEM, VMEM],
        out_specs=[VMEM, VMEM],
        out_shape=[
            jax.ShapeDtypeStruct((TOKENS, D), bf16),
            jax.ShapeDtypeStruct((CHIP_ROWS, TOKENS), f32),
        ],
        scratch_shapes=[pltpu.VMEM((CHIP_ROWS, D // 2), bf16)],
        compiler_params=params,
        cost_estimate=pl.CostEstimate(
            flops=10**11, bytes_accessed=10**8, transcendentals=0
        ),
        name="half",
    )(place, first, near, far, last)


def logits_kernel(
    place, hidden, partial, own, other, logits, stats, tokens, state, weight, facts, counts
):
    step = pl.program_id(0)
    core = place[0]
    row_start = place[1]

    @pl.when(step == 0)
    def _():
        gather_weight(other, 0, weight)
        for q in range(PEERS):
            facts[2 * q + core] = own[q, 2 * TOK - 16 :, LAST - 128 :].astype(f32)
            facts[2 * q + 1 - core] = other[q, TOK - 16 :, LAST - 128 :].astype(f32)
        seg = lax.broadcasted_iota(jnp.int32, (SEGS, 128), 0).astype(f32)
        total = jnp.zeros((SEGS, 128), f32)
        for j in range(2 * PEERS):
            total = total + jnp.where(facts[j, 3:4, :] == seg, facts[j, 4:5, :], 0.0)
            state[j : j + 1, :] = facts[j, 5:6, :] + facts[j, 6:7, :] + facts[j, 7:8, :]
        counts[...] = jnp.broadcast_to(jnp.sum(total, axis=1, keepdims=True), (SEGS, 128))

    scores = partial[...] + lax.dot_general(
        weight[...], hidden[...], (((1,), (1,)), ((), ())), preferred_element_type=f32
    )
    logits[:CHIP_ROWS, :] = scores
    logits[CHIP_ROWS:, :] = jnp.zeros((8, 2 * TOK), f32)
    seg = lax.broadcasted_iota(jnp.int32, (SEGS, 128), 0).astype(f32)
    row = lax.broadcasted_iota(jnp.int32, (CHIP_ROWS, 128), 0) + row_start
    tokens[...] = jnp.zeros_like(tokens)
    for half in range(2):
        part = scores[:, half * 128 : half * 128 + 128]
        q = step * 2 + half
        fact = facts[2 * q + core]
        top = jnp.max(part, axis=0, keepdims=True)
        shifted = jnp.exp(part - top)
        exp_sum = jnp.sum(shifted, axis=0, keepdims=True)
        exp_dot = jnp.sum(shifted * part, axis=0, keepdims=True)
        goal = fact[0:1] * 65536.0 + fact[1:2] * 256.0 + fact[2:3]
        hit = row == goal.astype(jnp.int32)
        target_logit = jnp.sum(jnp.where(hit, part, 0.0), axis=0, keepdims=True)
        own_count = jnp.sum(
            jnp.where(fact[3:4] == seg, counts[...], 0.0), axis=0, keepdims=True
        )
        tok_weight = fact[4:5] / jnp.maximum(own_count, 1.0) / SEGS
        lanes = slice(half * 128, half * 128 + 128)
        tokens[0:1, lanes] = tok_weight
        tokens[1:2, lanes] = goal
        tokens[2:3, lanes] = tok_weight * target_logit
        partial_total = top + jnp.log(exp_sum)
        mean = exp_dot / exp_sum
        for peer in range(16):
            stats[peer, pl.ds(q, 1), :] = partial_total
            stats[peer, pl.ds(8 + q, 1), :] = mean


def logits_call(place, hidden, partial, own, other):
    return pl.pallas_call(
        logits_kernel,
        grid=(4,),
        in_specs=[
            SMEM,
            pl.BlockSpec((2 * TOK, D // 2), lambda i: (i, 1)),
            pl.BlockSpec((CHIP_ROWS, 2 * TOK), lambda i: (0, i)),
            pl.BlockSpec((PEERS, 2 * TOK, LAST), lambda i: (0, 0, 0)),
            pl.BlockSpec((PEERS, TOK, LAST), lambda i: (0, 0, 0)),
        ],
        out_specs=[
            pl.BlockSpec((CHIP_ROWS + 8, 2 * TOK), lambda i: (0, i)),
            pl.BlockSpec((16, 16, 128), lambda i: (0, 0, 0)),
            pl.BlockSpec((8, 2 * TOK), lambda i: (0, i)),
            pl.BlockSpec((16, 128), lambda i: (0, 0)),
        ],
        out_shape=[
            jax.ShapeDtypeStruct((CHIP_ROWS + 8, TOKENS), f32),
            jax.ShapeDtypeStruct((16, 16, 128), f32),
            jax.ShapeDtypeStruct((8, TOKENS), f32),
            jax.ShapeDtypeStruct((16, 128), f32),
        ],
        scratch_shapes=[
            pltpu.VMEM((CHIP_ROWS, D // 2), bf16),
            pltpu.VMEM((16, 16, 128), f32),
            pltpu.VMEM((SEGS, 128), f32),
        ],
        compiler_params=params,
        name="logits",
    )(place, hidden, partial, own, other)


def merged(stats):
    part, mean = stats[:, :8, :], stats[:, 8:, :]
    top = jnp.max(part, axis=0)
    share = jnp.exp(part - top[None])
    total = jnp.sum(share, axis=0)
    return top + jnp.log(total), jnp.sum(share * mean, axis=0) / total


def merge_kernel(stats, out):
    log_total, mean = merged(stats[...])
    out[:, :8, :] = jnp.broadcast_to(log_total[None], (16, 8, 128))
    out[:, 8:, :] = jnp.broadcast_to(mean[None], (16, 8, 128))


def merge_call(stats):
    return pl.pallas_call(
        merge_kernel,
        in_specs=[VMEM],
        out_specs=VMEM,
        out_shape=jax.ShapeDtypeStruct((16, 16, 128), f32),
        compiler_params=params,
        name="merge",
    )(stats)


def score_block(logits, tokens, log_total, entropy, base, row_start, q):
    lanes = slice(q * 128, q * 128 + 128)
    part = logits[pl.ds(pl.multiple_of(base, 8), PAD), lanes]
    row = lax.broadcasted_iota(jnp.int32, (PAD, 128), 0)
    tok_weight = tokens[0:1, lanes]
    goal = tokens[1:2, lanes].astype(jnp.int32)
    hit = (row + (row_start + base) == goal).astype(f32)
    above = part - log_total[q : q + 1, :]
    probability = jnp.exp(above)
    score = tok_weight * (
        probability - hit + penalty * probability * (above + entropy[q : q + 1, :])
    )
    return jnp.where(row < OWN, score, 0.0).astype(bf16)


def away_kernel(place, stats, logits, tokens, score, totals):
    core = place[0]
    log_total, mean = merged(stats[...])
    entropy = log_total - mean
    totals[:8, :] = log_total
    totals[8:, :] = entropy
    for q in range(PEERS):
        score[:, q * 128 : q * 128 + 128] = score_block(
            logits, tokens, log_total, entropy, (1 - core) * OWN, place[1], q
        )


def away_call(place, stats, logits, tokens):
    return pl.pallas_call(
        away_kernel,
        in_specs=[SMEM, VMEM, VMEM, VMEM],
        out_specs=[VMEM, VMEM],
        out_shape=[
            jax.ShapeDtypeStruct((PAD, TOKENS), bf16),
            jax.ShapeDtypeStruct((16, 128), f32),
        ],
        compiler_params=params,
        name="away",
    )(place, stats, logits, tokens)


def own_kernel(place, totals, logits, tokens, hidden, out, score):
    @pl.when(pl.program_id(0) == 0)
    def _():
        for q in range(PEERS):
            score[:, q * 128 : q * 128 + 128] = score_block(
                logits, tokens, totals[:8, :], totals[8:, :], place[0] * OWN, place[1], q
            )

    out[...] = jnp.dot(score[...], hidden[...], preferred_element_type=f32)


def own_call(place, totals, logits, tokens, hidden):
    return pl.pallas_call(
        own_kernel,
        grid=(4,),
        in_specs=[
            SMEM,
            pl.BlockSpec((16, 128), lambda i: (0, 0)),
            pl.BlockSpec((CHIP_ROWS + 8, TOKENS), lambda i: (0, 0)),
            pl.BlockSpec((8, TOKENS), lambda i: (0, 0)),
            pl.BlockSpec((TOKENS, 512), lambda i: (0, i)),
        ],
        out_specs=pl.BlockSpec((PAD, 512), lambda i: (0, i)),
        out_shape=jax.ShapeDtypeStruct((PAD, D), f32),
        scratch_shapes=[pltpu.VMEM((PAD, TOKENS), bf16)],
        compiler_params=params,
        name="own",
    )(place, totals, logits, tokens, hidden)


def split_rows(value):
    high = value.astype(bf16).astype(f32)
    rest = value - high
    middle = rest.astype(bf16).astype(f32)
    return [high, middle, rest - middle]


def join_rows(total, start):
    return total[start : start + 1] + total[start + 1 : start + 2] + total[start + 2 : start + 3]


def grad_kernel(
    place, partial, score, hidden, state, totals, tokens, scaled, sums, grad, table
):
    step = pl.program_id(0)
    value = partial[...] + jnp.dot(score[...], hidden[...], preferred_element_type=f32)
    grad[:, pl.ds(pl.multiple_of(step * 512, 512), 512)] = value

    @pl.when(step == 3)
    def _():
        core = place[0]
        places = [2 * i + core for i in range(8)] + [2 * i + 1 - core for i in range(8)]
        squares = jnp.zeros((PAD, 128), f32)
        for i, j in enumerate(places):
            part = grad[:, 128 * i : 128 * i + 128]
            part = part * part
            squares = squares + part
            table[pl.ds(j, 1), :] = jnp.sum(part, axis=0, keepdims=True)
        row_new = decay_rate * state[...] + (1.0 - decay_rate) * (
            jnp.sum(squares, axis=1, keepdims=True) / D
        )
        scale = jnp.broadcast_to(lax.rsqrt(row_new), (PAD, 128))
        row = lax.broadcasted_iota(jnp.int32, (PAD, 128), 0)
        lane = lax.broadcasted_iota(jnp.int32, (PAD, 128), 1)
        kept = jnp.where(
            (row < OWN) & (lane == 0), jnp.broadcast_to(row_new, (PAD, 128)), 0.0
        )
        row_total = jnp.sum(kept, axis=0, keepdims=True)
        loss = jnp.zeros((1, 128), f32)
        for q in range(PEERS):
            lanes = slice(128 * q, 128 * q + 128)
            loss = loss + (
                tokens[0:1, lanes]
                * (totals[q : q + 1, :] - penalty * totals[8 + q : 9 + q, :])
                * (1.0 / 256.0)
                - tokens[2:3, lanes]
            )
        table[32:48, :] = jnp.zeros((16, 128), f32)
        for i, line in enumerate(split_rows(row_total) + split_rows(loss)):
            table[32 + i : 33 + i, :] = line
        for i, j in enumerate(places):
            part = grad[:, 128 * i : 128 * i + 128] * scale
            scaled[:, pl.ds(pl.multiple_of(j * 128, 128), 128)] = part
            table[pl.ds(16 + j, 1), :] = jnp.sum(part * part, axis=0, keepdims=True)
        sums[...] = jnp.broadcast_to(table[...].astype(bf16)[None], (32, 48, 128))


def grad_call(place, partial, score, hidden, state, totals, tokens):
    return pl.pallas_call(
        grad_kernel,
        grid=(4,),
        in_specs=[
            SMEM,
            pl.BlockSpec((PAD, 512), lambda i: (0, i)),
            pl.BlockSpec((PAD, TOKENS), lambda i: (0, 0)),
            pl.BlockSpec((TOKENS, 512), lambda i: (0, (i + 2) % 4)),
            pl.BlockSpec((PAD, 1), lambda i: (0, 0)),
            pl.BlockSpec((16, 128), lambda i: (0, 0)),
            pl.BlockSpec((8, TOKENS), lambda i: (0, 0)),
        ],
        out_specs=[
            pl.BlockSpec((PAD, D), lambda i: (0, 0)),
            pl.BlockSpec((32, 48, 128), lambda i: (0, 0, 0)),
        ],
        out_shape=[
            jax.ShapeDtypeStruct((PAD, D), f32),
            jax.ShapeDtypeStruct((32, 48, 128), bf16),
        ],
        scratch_shapes=[pltpu.VMEM((PAD, D), f32), pltpu.VMEM((48, 128), f32)],
        compiler_params=params,
        name="grad",
    )(place, partial, score, hidden, state, totals, tokens)


def add_kernel(sums, out):
    total = jnp.sum(sums[...].astype(f32), axis=0)
    lines = split_rows(join_rows(total, 32)) + split_rows(join_rows(total, 35))
    row = lax.broadcasted_iota(jnp.int32, (16, 128), 0)
    tail = jnp.zeros((16, 128), f32)
    for i, line in enumerate(lines):
        tail = jnp.where(row == i, line, tail)
    out[:, :32, :] = jnp.broadcast_to(total[:32].astype(bf16)[None], (16, 32, 128))
    out[:, 32:, :] = jnp.broadcast_to(tail.astype(bf16)[None], (16, 16, 128))


def add_call(sums):
    return pl.pallas_call(
        add_kernel,
        in_specs=[VMEM],
        out_specs=VMEM,
        out_shape=jax.ShapeDtypeStruct((16, 48, 128), bf16),
        compiler_params=params,
        name="add",
    )(sums)


def update_kernel(sums, state, scaled, out, loss):
    total = jnp.sum(sums[...].astype(f32), axis=0)
    column_new = decay_rate * state[...] + (1.0 - decay_rate) * (total[:16] / V)
    column_scale = lax.rsqrt(column_new)
    row_mean = jnp.broadcast_to(jnp.sum(join_rows(total, 32), keepdims=True) / V, (16, 128))
    square_total = jnp.sum(total[16:32] * column_scale * column_scale, keepdims=True)
    square_total = row_mean * jnp.broadcast_to(square_total, (16, 128))
    update_rms = jnp.sqrt(square_total / (V * D))
    factor = jnp.sqrt(row_mean) * column_scale / jnp.maximum(1.0, update_rms / clip_limit)
    for j in range(16):
        out[j] = (scaled[:OWN, 128 * j : 128 * j + 128] * factor[j : j + 1, :]).astype(bf16)
    loss[...] = jnp.broadcast_to(jnp.sum(join_rows(total, 35), keepdims=True), (8, 128))


def update_call(sums, state, scaled):
    return pl.pallas_call(
        update_kernel,
        in_specs=[VMEM] * 3,
        out_specs=[VMEM] * 2,
        out_shape=[
            jax.ShapeDtypeStruct((16, OWN, 128), bf16),
            jax.ShapeDtypeStruct((8, 128), f32),
        ],
        compiler_params=params,
        name="update",
    )(sums, state, scaled)


def per_device(hidden, head_weight, targets, segments, loss_mask, row_state, column_state):
    core = lax.axis_index("core")
    chip = lax.axis_index(CHIPS)
    odd = lax.axis_index("z") % 2
    chip_start = chip * CHIP_ROWS
    place = jnp.stack([core, lax.axis_index(MP) * VOC + chip_start, odd]).astype(jnp.int32)
    own_state = lax.dynamic_slice_in_dim(row_state, chip_start + core * OWN, OWN, axis=0)
    own_state = jnp.concatenate([own_state, jnp.ones((PAD - OWN,), f32)]).reshape(PAD, 1)
    place, own_state, targets = lax.optimization_barrier((place, own_state, targets))

    first = lax.dynamic_slice_in_dim(hidden, odd * STEP, STEP, axis=1)
    first = trade(jnp.broadcast_to(first[None], (PEERS, TOK, STEP)), CHIPS)
    last = pack(hidden, head_weight, targets, segments, loss_mask, column_state)
    last, first = lax.optimization_barrier((last, first))
    last = trade(last, CHIPS)
    near = lax.ppermute(first[:4], "z", [(i, i ^ 1) for i in range(16)])
    far = lax.ppermute(first[4:], "z", [(i, (i + 1 if i % 2 else i - 1) % 16) for i in range(16)])
    head_other = swap_cores(last[:, TOK:, :])
    hidden_own, partial = half_call(place, first, near, far, last)
    logits, stats, tokens, state = logits_call(place, hidden_own, partial, last, head_other)
    stats, hidden_own = lax.optimization_barrier((stats, hidden_own))
    hidden_other = swap_cores(hidden_own)
    stats = merge_call(trade(stats, PLANE))
    stats = trade(stats, "z")
    score_away, totals = away_call(place, stats, logits, tokens)
    score_other = swap_cores(score_away)
    partial = own_call(place, totals, logits, tokens, hidden_own)
    scaled, sums = grad_call(
        place, partial, score_other, hidden_other, own_state, totals, tokens
    )
    sums = add_call(trade(sums, ("y", "xh", "core", "xl")))
    update, loss = update_call(trade(sums, "z"), state, scaled)
    update_step = trade(update, DP).reshape(VOC, COLS)
    return (update_step, loss[0, 0])


def solution(mesh):
    fine = Mesh(mesh.devices.reshape(4, 2, 2, 16, 2), AXES)
    return jax.shard_map(
        per_device,
        mesh=fine,
        in_specs=(P(DP, None), P(MP, DP), P(DP), P(DP), P(DP), P(MP), P(DP)),
        out_specs=(P(MP, DP), P()),
        check_vma=False,
    )
```

time: 691 us -> 194 us (0.28)
  blocking collectives: 442 us -> 62 us
  waiting for transfers between devices: 201 us -> 43.3 us
  starting transfers between devices: 0.08 us -> 52.4 us
  Pallas kernels: 0 us -> 21.4 us
  matrix products: 19.9 us -> 0 us
  between operations: 15.5 us -> 0.88 us
  local copies, waits for them, and re-layouts: 0.57 us -> 12.7 us
  other arithmetic: 11.5 us -> 0.08 us
    psum x6 -> x0, blocking collectives: 349 us -> none  [the longest x1 98.9 us: per_device(): square_total = lax.psum(jnp.sum(unclipped * unclipped), ('dp', 'mp'))]
    all_gather x2 -> x0, waiting for transfers between devices: 200 us -> none  [the longest x1 102 us: per_device(): lax.all_gather(score_grad, 'dp', axis=0, tiled=True)]
    pmax x1 -> x0, blocking collectives: 50 us -> none  [per_device(): row_max = lax.pmax(jnp.max(logits, axis=1), 'mp')]
    all_to_all x0 -> x3, waiting for transfers between devices: none -> 41 us  [trade(): return lax.all_to_all(value, axes, 0, 0)]
    ppermute x0 -> x5, starting transfers between devices: none -> 31.2 us  [the longest x3 16.2 us: swap_cores(): return lax.ppermute(value, 'core', [(0, 1), (1, 0)])]
    pallas_call x0 -> x9, Pallas kernels: none -> 21.4 us  [the longest x1 4.9 us: grad_call(): pl.pallas_call(grad_kernel, grid=(4,), in_specs=[SMEM, pl.BlockSpec((PAD,...]
    all_to_all x0 -> x3, starting transfers between devices: none -> 21.2 us  [trade(): return lax.all_to_all(value, axes, 0, 0)]
    dot_general x2 -> x0, matrix products: 19.9 us -> none  [the longest x1 11.3 us: per_device(): lax.dot_general(section, lax.all_gather(head_weight, 'dp', axis=1, tiled=...]
  transfers between devices with their start and end apart: 2 -> 8, of which waited for: 2 -> 4; matrix products, arithmetic and copies ran while one was open for 0% -> 2% of each run, Pallas kernels for 0% -> 5%
where the time goes in v2:
time: 194 us; the launch traced here: 193 us
  blocking collectives  62 us (32%)
  starting transfers between devices  52.4 us (27%)
  waiting for transfers between devices  43.3 us (22%)
  Pallas kernels  21.4 us (11%)
  local copies, waits for them, and re-layouts  12.7 us (7%)
    all_to_all x4, blocking collectives, trade(): return lax.all_to_all(value, axes, 0, 0)  62 us
    all_to_all x3, waiting for transfers between devices, trade(): return lax.all_to_all(value, axes, 0, 0)  41 us
    all_to_all x3, starting transfers between devices, trade(): return lax.all_to_all(value, axes, 0, 0)  21.2 us
    ppermute x3, starting transfers between devices, swap_cores(): return lax.ppermute(value, 'core', [(0, 1), (1, 0)])  16.2 us
    ppermute x1, starting transfers between devices, per_device(): lax.ppermute(first[4:], 'z', [(i, (i + 1 if i % 2 else i - 1) % 16) for i...  10.2 us
    unnamed x23, local copies, waits for them, and re-layouts  6.41 us
    pallas_call x1, Pallas kernels, grad_call(): pl.pallas_call(grad_kernel, grid=(4,), in_specs=[SMEM, pl.BlockSpec((PAD,...  4.9 us
    ppermute x1, starting transfers between devices, per_device(): near = lax.ppermute(first[:4], 'z', [(i, i ^ 1) for i in range(16)])  4.76 us
  transfers between devices with their start and end apart: 8, of which 4 were waited for; matrix products, arithmetic and copies ran while one was open for 2% of the time, Pallas kernels for 5%

profile of v2, /device:TPU:1, one launch (start us, length us, event | category | flops | bytes accessed | tf_op | source)
XLA Modules:
  0.0 192.8 jit_solution(2286180909487559168)
XLA Ops:
  2.9 7.5 %all-to-all-start = ((bf16[8,128,768]{2,1,0:T(8,128)(2,1)}), bf16[8,128,768]{2,1,0:T(8,128)(2,1)S(1)}, u32[]{:S(2)}, u32[]{:S(2)}) async-start(bf16[8,128,768]{2,1,0:T(8,128)(2,1)} %broadcast_in_dim.2), calls=%async_computation | async-start | bytes 3145728 | tf_op jit(solution)/shard_map/all_to_all | solution.py:45
  11.8 1.3 copy-done
  13.1 16.9 %all-to-all-done.first = bf16[8,128,768]{2,1,0:T(8,128)(2,1)S(1)} async-done(((bf16[8,128,768]{2,1,0:T(8,128)(2,1)}), bf16[8,128,768]{2,1,0:T(8,128)(2,1)S(1)}, u32[]{:S(2)}, u32[]{:S(2)}) %all-to-all-start) | async-done | bytes 1572896 | tf_op jit(solution)/shard_map/all_to_all | solution.py:45
  31.2 4.9 %all-to-all-start.1 = ((bf16[8,256,512]{2,1,0:T(8,128)(2,1)}), bf16[8,256,512]{2,1,0:T(8,128)(2,1)S(1)}, u32[]{:S(2)}, u32[]{:S(2)}) async-start(bf16[8,256,512]{2,1,0:T(8,128)(2,1)} %copy-done), calls=%async_computation.1 | async-start | bytes 4194304 | tf_op jit(solution)/shard_map/all_to_all | solution.py:45
  36.0 2.7 %fusion = (bf16[4,128,768]{2,1,0:T(8,128)(2,1)}, bf16[4,128,768]{2,1,0:T(8,128)(2,1)}) fusion(bf16[8,128,768]{2,1,0:T(8,128)(2,1)} %copy-done.3), kind=kLoop, calls=%fused_computation.2 | loop fusion | bytes 3145728 | tf_op jit(solution)/shard_map/slice | solution.py:497
  38.7 4.8 %collective-permute-start = (bf16[4,128,768]{2,1,0:T(8,128)(2,1)}, bf16[4,128,768]{2,1,0:T(8,128)(2,1)S(1)}, u32[]{:S(2)}, u32[]{:S(2)}) collective-permute-start(bf16[4,128,768]{2,1,0:T(8,128)(2,1)} %get-tuple-element.41), channel_id=1, source_target_pairs={{0,2},{2,0},{4,6},{6,4},{8,10},{10,8},{12,14},{14,12},{16,18},{18,... | collective-permute-start | bytes 2359304 | tf_op jit(solution)/shard_map/ppermute | solution.py:496
  43.4 10.2 %collective-permute-start.1 = (bf16[4,128,768]{2,1,0:T(8,128)(2,1)}, bf16[4,128,768]{2,1,0:T(8,128)(2,1)}, u32[]{:S(2)}, u32[]{:S(2)}) collective-permute-start(bf16[4,128,768]{2,1,0:T(8,128)(2,1)} %get-tuple-element.40), channel_id=1, source_target_pairs={{0,30},{2,4},{4,2},{6,8},{8,6},{10,12},{12,10},{14,16},{16,14},{18... | collective-permute-start | bytes 2359304 | tf_op jit(solution)/shard_map/ppermute | solution.py:497
  53.7 7.7 %all-to-all-done.1.last.own = bf16[8,256,512]{2,1,0:T(8,128)(2,1)S(1)} async-done(((bf16[8,256,512]{2,1,0:T(8,128)(2,1)}), bf16[8,256,512]{2,1,0:T(8,128)(2,1)S(1)}, u32[]{:S(2)}, u32[]{:S(2)}) %all-to-all-start.1) | async-done | bytes 2097184 | tf_op jit(solution)/shard_map/all_to_all | solution.py:45
  61.5 6.1 %collective-permute-start.2 = (bf16[8,128,512]{2,1,0:T(8,128)(2,1)S(1)}, bf16[8,128,512]{2,1,0:T(8,128)(2,1)S(1)}, u32[]{:S(2)}, u32[]{:S(2)}) collective-permute-start(bf16[8,128,512]{2,1,0:T(8,128)(2,1)S(1)} %slice.16), channel_id=1, source_target_pairs={{0,32},{32,0},{1,33},{33,1},{2,34},{34,2},{3,35},{35,3},{4,36},{36... | collective-permute-start | bytes 3145736 | tf_op jit(solution)/shard_map/ppermute | solution.py:41
  67.6 2.3 %collective-permute-done.1.far = bf16[4,128,768]{2,1,0:T(8,128)(2,1)} collective-permute-done((bf16[4,128,768]{2,1,0:T(8,128)(2,1)}, bf16[4,128,768]{2,1,0:T(8,128)(2,1)}, u32[]{:S(2)}, u32[]{:S(2)}) %collective-permute-start.1) | collective-permute-done | bytes 786464 | tf_op jit(solution)/shard_map/ppermute | solution.py:497
  69.9 4.6 %half.1 = (bf16[1024,2048]{1,0:T(8,128)(2,1)}, f32[496,1024]{1,0:T(8,128)S(1)}) custom-call(s32[3]{0:T(128)S(1)} %pad_add_fusion.place, bf16[8,128,768]{2,1,0:T(8,128)(2,1)S(1)} %copy-done.4, bf16[4,128,768]{2,1,0:T(8,128)(2,1)S(1)} %collective-permute-done.near, bf16[4,128,768]{2,1,0:T(8,128)(2,1)} %collective-permute-done.1.far, ...), custom_call_target="tpu_custom_call" | custom-call | flops 99999997952 | bytes 100000000 | tf_op jit(solution)/shard_map/half/pallas_call | solution.py:147
  74.4 4.6 %logits.1 = (f32[504,1024]{1,0:T(8,128)S(1)}, f32[16,16,128]{2,1,0:T(8,128)S(1)}, f32[8,1024]{1,0:T(8,128)S(1)}, f32[16,128]{1,0:T(8,128)S(1)}) custom-call(s32[3]{0:T(128)S(1)} %pad_add_fusion.place, bf16[1024,2048]{1,0:T(8,128)(2,1)} %get-tuple-element.32.hidden, f32[496,1024]{1,0:T(8,128)S(1)} %get-tuple-element.26.partial, ...), custom_call_target="tpu_custom_call" | custom-call | tf_op jit(solution)/shard_map/logits/pallas_call | solution.py:219
  79.1 4.5 %collective-permute-start.4 = (bf16[1024,2048]{1,0:T(8,128)(2,1)}, bf16[1024,2048]{1,0:T(8,128)(2,1)}, u32[]{:S(2)}, u32[]{:S(2)}) collective-permute-start(bf16[1024,2048]{1,0:T(8,128)(2,1)} %get-tuple-element.32.hidden), channel_id=1, source_target_pairs={{0,32},{32,0},{1,33},{33,1},{2,34},{34,2},{3,35},{35,3},{4,36},{36... | collective-permute-start | bytes 12582920 | tf_op jit(solution)/shard_map/ppermute | solution.py:41
  83.6 13.7 %all_to_all.35.stats = f32[16,16,128]{2,1,0:T(8,128)S(1)} all-to-all(f32[16,16,128]{2,1,0:T(8,128)S(1)} %get-tuple-element.28), channel_id=1, replica_groups=mesh['y'=4,'xh'=2,'core'=2,'z'=16,'xl'=2] {'y','xh','xl'}, dimensions={0} | all-to-all | bytes 262144 | tf_op jit(solution)/shard_map/all_to_all | solution.py:45
  97.4 20.2 %all_to_all.36.stats = f32[16,16,128]{2,1,0:T(8,128)S(1)} all-to-all(f32[16,16,128]{2,1,0:T(8,128)S(1)} %merge.1), channel_id=1, replica_groups=mesh['y'=4,'xh'=2,'core'=2,'z'=16,'xl'=2] {'z'}, dimensions={0} | all-to-all | bytes 262144 | tf_op jit(solution)/shard_map/all_to_all | solution.py:45
  118.5 1.4 copy-done.1
  119.9 5.6 %collective-permute-start.3 = (bf16[256,1024]{1,0:T(8,128)(2,1)S(1)}, bf16[256,1024]{1,0:T(8,128)(2,1)S(1)}, u32[]{:S(2)}, u32[]{:S(2)}) collective-permute-start(bf16[256,1024]{1,0:T(8,128)(2,1)S(1)} %get-tuple-element.33), channel_id=1, source_target_pairs={{0,32},{32,0},{1,33},{33,1},{2,34},{34,2},{3,35},{35,3},{4,36},{36... | collective-permute-start | bytes 1572872 | tf_op jit(solution)/shard_map/ppermute | solution.py:41
  125.7 1.6 copy-done.2
  127.3 4.5 %own.1.partial = f32[256,2048]{1,0:T(8,128)S(1)} custom-call(s32[3]{0:T(128)S(1)} %pad_add_fusion.place, f32[16,128]{1,0:T(8,128)S(1)} %get-tuple-element.31.totals, f32[504,1024]{1,0:T(8,128)S(1)} %copy-done.2, f32[8,1024]{1,0:T(8,128)S(1)} %get-tuple-element.30.tokens, bf16[1024,2048]{1,0:T(8,128)(2,1)} %get-tuple-element.32.hidden), custom_call_target="tpu_custom_call" | custom-call | tf_op jit(solution)/shard_map/own/pallas_call | solution.py:329
  131.8 4.9 %grad.1 = (f32[256,2048]{1,0:T(8,128)S(1)}, bf16[32,48,128]{2,1,0:T(8,128)(2,1)S(1)}) custom-call(s32[3]{0:T(128)S(1)} %pad_add_fusion.place, f32[256,2048]{1,0:T(8,128)S(1)} %own.1.partial, bf16[256,1024]{1,0:T(8,128)(2,1)S(1)} %collective-permute-done.3.score, bf16[1024,2048]{1,0:T(8,128)(2,1)} %collective-permute-done.4.hidden, f32[256,1]{1,0:T(8,128)S(1)} %copy.9.state, ...), custom_call_target="tpu_custom_call" | custom-call | tf_op jit(solution)/shard_map/grad/pallas_call | solution.py:405
  136.7 12.6 %all_to_all.37.sums = bf16[32,48,128]{2,1,0:T(8,128)(2,1)S(1)} all-to-all(bf16[32,48,128]{2,1,0:T(8,128)(2,1)S(1)} %get-tuple-element.35), channel_id=1, replica_groups=mesh['y'=4,'xh'=2,'core'=2,'z'=16,'xl'=2] {'y','xh','core','xl'}, dimensions={0} | all-to-all | bytes 786432 | tf_op jit(solution)/shard_map/all_to_all | solution.py:45
  149.3 15.6 %all_to_all.38.sums = bf16[16,48,128]{2,1,0:T(8,128)(2,1)S(1)} all-to-all(bf16[16,48,128]{2,1,0:T(8,128)(2,1)S(1)} %add.36), channel_id=1, replica_groups=mesh['y'=4,'xh'=2,'core'=2,'z'=16,'xl'=2] {'z'}, dimensions={0} | all-to-all | bytes 393216 | tf_op jit(solution)/shard_map/all_to_all | solution.py:45
  166.2 8.8 %all-to-all-start.6 = ((bf16[16,248,128]{2,1,0:T(8,128)(2,1)}), bf16[16,248,128]{2,1,0:T(8,128)(2,1)S(1)}, u32[]{:S(2)}, u32[]{:S(2)}) async-start(bf16[16,248,128]{2,1,0:T(8,128)(2,1)} %get-tuple-element.38), calls=%async_computation.6 | async-start | bytes 2031616 | tf_op jit(solution)/shard_map/all_to_all | solution.py:45
  175.5 16.3 %all-to-all-done.6 = bf16[16,248,128]{2,1,0:T(8,128)(2,1)S(1)} async-done(((bf16[16,248,128]{2,1,0:T(8,128)(2,1)}), bf16[16,248,128]{2,1,0:T(8,128)(2,1)S(1)}, u32[]{:S(2)}, u32[]{:S(2)}) %all-to-all-start.6) | async-done | bytes 1015840 | tf_op jit(solution)/shard_map/all_to_all | solution.py:45
  (37 shorter events, 8.7 us)
Async XLA Ops:
  1.6 9.6 %copy-start.5 = (bf16[3968,128]{1,0:T(8,128)(2,1)S(1)}, bf16[3968,128]{1,0:T(8,128)(2,1)}, u32[]{:S(2)}) copy-start(bf16[3968,128]{1,0:T(8,128)(2,1)} %head.1) | copy-start | bytes 3047428
  1.6 9.6 %copy-start.6 = (bf16[128,2048]{1,0:T(8,128)(2,1)S(1)}, bf16[128,2048]{1,0:T(8,128)(2,1)}, u32[]{:S(2)}) copy-start(bf16[128,2048]{1,0:T(8,128)(2,1)} %hidden.1) | copy-start | bytes 1572868
  1.6 9.6 %copy-start.7 = (s32[128]{0:T(128)S(1)}, s32[128]{0:T(128)}, u32[]{:S(2)}) copy-start(s32[128]{0:T(128)} %param.9) | copy-start | bytes 1540
  1.6 9.6 %copy-start.8 = (s32[128]{0:T(128)S(1)}, s32[128]{0:T(128)}, u32[]{:S(2)}) copy-start(s32[128]{0:T(128)} %param.10) | copy-start | bytes 1540
  1.6 9.6 %copy-start.9 = (s32[128]{0:T(128)S(1)}, s32[128]{0:T(128)}, u32[]{:S(2)}) copy-start(s32[128]{0:T(128)} %param.11) | copy-start | bytes 1540
  1.7 9.6 %copy-start.10 = (f32[128]{0:T(128)S(1)}, f32[128]{0:T(128)}, u32[]{:S(2)}) copy-start(f32[128]{0:T(128)} %param.13) | copy-start | bytes 1540
  2.9 27.1 %all-to-all-start = ((bf16[8,128,768]{2,1,0:T(8,128)(2,1)}), bf16[8,128,768]{2,1,0:T(8,128)(2,1)S(1)}, u32[]{:S(2)}, u32[]{:S(2)}) async-start(bf16[8,128,768]{2,1,0:T(8,128)(2,1)} %broadcast_in_dim.2), calls=%async_computation | async-start | bytes 3145728 | tf_op jit(solution)/shard_map/all_to_all | solution.py:45
  11.7 1.3 copy-start
  30.0 1.1 copy-start.3
  31.2 30.2 %all-to-all-start.1 = ((bf16[8,256,512]{2,1,0:T(8,128)(2,1)}), bf16[8,256,512]{2,1,0:T(8,128)(2,1)S(1)}, u32[]{:S(2)}, u32[]{:S(2)}) async-start(bf16[8,256,512]{2,1,0:T(8,128)(2,1)} %copy-done), calls=%async_computation.1 | async-start | bytes 4194304 | tf_op jit(solution)/shard_map/all_to_all | solution.py:45
  38.7 28.9 %collective-permute-start = (bf16[4,128,768]{2,1,0:T(8,128)(2,1)}, bf16[4,128,768]{2,1,0:T(8,128)(2,1)S(1)}, u32[]{:S(2)}, u32[]{:S(2)}) collective-permute-start(bf16[4,128,768]{2,1,0:T(8,128)(2,1)} %get-tuple-element.41), channel_id=1, source_target_pairs={{0,2},{2,0},{4,6},{6,4},{8,10},{10,8},{12,14},{14,12},{16,18},{18,... | collective-permute-start | bytes 2359304 | tf_op jit(solution)/shard_map/ppermute | solution.py:496
  43.4 26.4 %collective-permute-start.1 = (bf16[4,128,768]{2,1,0:T(8,128)(2,1)}, bf16[4,128,768]{2,1,0:T(8,128)(2,1)}, u32[]{:S(2)}, u32[]{:S(2)}) collective-permute-start(bf16[4,128,768]{2,1,0:T(8,128)(2,1)} %get-tuple-element.40), channel_id=1, source_target_pairs={{0,30},{2,4},{4,2},{6,8},{8,6},{10,12},{12,10},{14,16},{16,14},{18... | collective-permute-start | bytes 2359304 | tf_op jit(solution)/shard_map/ppermute | solution.py:497
  61.4 8.5 %copy-start.4 = (bf16[8,128,768]{2,1,0:T(8,128)(2,1)S(1)}, bf16[8,128,768]{2,1,0:T(8,128)(2,1)}, u32[]{:S(2)}) copy-start(bf16[8,128,768]{2,1,0:T(8,128)(2,1)} %copy-done.3) | copy-start | bytes 4718596
  61.5 13.0 %collective-permute-start.2 = (bf16[8,128,512]{2,1,0:T(8,128)(2,1)S(1)}, bf16[8,128,512]{2,1,0:T(8,128)(2,1)S(1)}, u32[]{:S(2)}, u32[]{:S(2)}) collective-permute-start(bf16[8,128,512]{2,1,0:T(8,128)(2,1)S(1)} %slice.16), channel_id=1, source_target_pairs={{0,32},{32,0},{1,33},{33,1},{2,34},{34,2},{3,35},{35,3},{4,36},{36... | collective-permute-start | bytes 3145736 | tf_op jit(solution)/shard_map/ppermute | solution.py:41
  79.1 52.7 %collective-permute-start.4 = (bf16[1024,2048]{1,0:T(8,128)(2,1)}, bf16[1024,2048]{1,0:T(8,128)(2,1)}, u32[]{:S(2)}, u32[]{:S(2)}) collective-permute-start(bf16[1024,2048]{1,0:T(8,128)(2,1)} %get-tuple-element.32.hidden), channel_id=1, source_target_pairs={{0,32},{32,0},{1,33},{33,1},{2,34},{34,2},{3,35},{35,3},{4,36},{36... | collective-permute-start | bytes 12582920 | tf_op jit(solution)/shard_map/ppermute | solution.py:41
  118.5 1.4 copy-start.1
  119.9 11.8 %collective-permute-start.3 = (bf16[256,1024]{1,0:T(8,128)(2,1)S(1)}, bf16[256,1024]{1,0:T(8,128)(2,1)S(1)}, u32[]{:S(2)}, u32[]{:S(2)}) collective-permute-start(bf16[256,1024]{1,0:T(8,128)(2,1)S(1)} %get-tuple-element.33), channel_id=1, source_target_pairs={{0,32},{32,0},{1,33},{33,1},{2,34},{34,2},{3,35},{35,3},{4,36},{36... | collective-permute-start | bytes 1572872 | tf_op jit(solution)/shard_map/ppermute | solution.py:41
  125.7 1.6 copy-start.2
  166.2 25.7 %all-to-all-start.6 = ((bf16[16,248,128]{2,1,0:T(8,128)(2,1)}), bf16[16,248,128]{2,1,0:T(8,128)(2,1)S(1)}, u32[]{:S(2)}, u32[]{:S(2)}) async-start(bf16[16,248,128]{2,1,0:T(8,128)(2,1)} %get-tuple-element.38), calls=%async_computation.6 | async-start | bytes 2031616 | tf_op jit(solution)/shard_map/all_to_all | solution.py:45

commit v3 on v2

v3 whole, which is shorter than its diff:
```python
import jax
import jax.numpy as jnp
from jax import lax
from jax.experimental import pallas as pl
from jax.experimental.pallas import tpu as pltpu
from jax.sharding import Mesh, PartitionSpec as P

D = 2048
V = 126976

penalty = 0.25
decay_rate = 1.0 - 16.0 ** (-0.8)
clip_limit = 1.0

AXES = ("y", "xh", "core", "z", "xl")
DP = ("y", "xh", "core")
MP = ("z", "xl")
CHIPS = ("y", "xh")
PLANE = ("y", "xh", "xl")

PEERS = 8
TOK = 128
COLS = 128
VOC = 3968
CHIP_ROWS = 496
OWN = 248
PAD = 256
TOKENS = 1024
SEGS = 64
STEP = 6 * 128
LAST = 4 * 128
f32 = jnp.float32
bf16 = jnp.bfloat16

params = pltpu.CompilerParams(vmem_limit_bytes=16 * 1024 * 1024)
large = pltpu.CompilerParams(vmem_limit_bytes=16 * 1024 * 1024)
VMEM = pl.BlockSpec(memory_space=pltpu.VMEM)
SMEM = pl.BlockSpec(memory_space=pltpu.SMEM)
ANY = pl.BlockSpec(memory_space=pl.ANY)
HBM = pl.BlockSpec(memory_space=pltpu.HBM)


def swap_cores(value):
    return lax.ppermute(value, "core", [(0, 1), (1, 0)])


def trade(value, axes):
    return lax.all_to_all(value, axes, 0, 0)


def pack_kernel(hidden, head, targets, segments, mask, state, out):
    out[0, :TOK, :] = hidden[...]
    for block in range(4):
        height = min(128, CHIP_ROWS - 128 * block)
        out[0, TOK : TOK + height, 128 * block : 128 * block + 128] = head[
            128 * block : 128 * block + height, :
        ]
    row = lax.broadcasted_iota(jnp.int32, (16, 128), 0)
    goal = targets[...]
    value = state[...]
    high = value.astype(bf16).astype(f32)
    rest = value - high
    middle = rest.astype(bf16).astype(f32)
    facts = jnp.zeros((16, 128), f32)
    for place, fact in enumerate(
        [
            (goal >> 16).astype(f32),
            ((goal >> 8) & 255).astype(f32),
            (goal & 255).astype(f32),
            segments[...].astype(f32),
            mask[...].astype(f32),
            high,
            middle,
            rest - middle,
        ]
    ):
        facts = jnp.where(row == place, fact, facts)
    out[0, 2 * TOK - 16 :, LAST - 128 :] = facts.astype(bf16)


def pack(hidden, head, targets, segments, mask, state):
    small = pl.BlockSpec((1, 128), lambda i: (0, 0))
    return pl.pallas_call(
        pack_kernel,
        grid=(PEERS,),
        in_specs=[
            pl.BlockSpec((TOK, LAST), lambda i: (0, 3)),
            pl.BlockSpec((CHIP_ROWS, COLS), lambda i: (i, 0)),
            small,
            small,
            small,
            small,
        ],
        out_specs=pl.BlockSpec((1, 2 * TOK, LAST), lambda i: (i, 0, 0)),
        out_shape=pltpu.HBM((PEERS, 2 * TOK, LAST), bf16),
        compiler_params=large,
        name="pack",
    )(hidden, head, *[x.reshape(1, 128) for x in (targets, segments, mask, state)])


def spread_kernel(hidden, out, part, sems):
    start = pl.multiple_of((lax.axis_index("z") % 2) * STEP, STEP)
    copy = pltpu.make_async_copy(hidden.at[:, pl.ds(start, STEP)], part, sems.at[PEERS])
    copy.start()
    copy.wait()
    copies = [pltpu.make_async_copy(part, out.at[q], sems.at[q]) for q in range(PEERS)]
    for copy in copies:
        copy.start()
    for copy in copies:
        copy.wait()


def spread(hidden):
    return pl.pallas_call(
        spread_kernel,
        in_specs=[HBM],
        out_specs=ANY,
        out_shape=pltpu.HBM((PEERS, TOK, STEP), bf16),
        scratch_shapes=[
            pltpu.VMEM((TOK, STEP), bf16),
            pltpu.SemaphoreType.DMA((PEERS + 1,)),
        ],
        compiler_params=params,
        name="spread",
    )(hidden)


def gather_weight(source, q, rows, weight):
    for block in range(4):
        height = min(128, CHIP_ROWS - 128 * block)
        weight[128 * block : 128 * block + height, q * 128 : q * 128 + 128] = source[
            q, rows : rows + height, 128 * block : 128 * block + 128
        ]


def half_kernel(
    place, first, near, far, last, hidden, sent, partial, facts, weight, beside, rest, sems
):
    core = place[0]
    odd = place[2]
    rest_copies = [
        pltpu.make_async_copy(last.at[q], rest.at[q], sems.at[q]) for q in range(PEERS)
    ]
    beside_copies = [
        pltpu.make_async_copy(
            (near if q < 4 else far).at[q % 4], beside.at[q], sems.at[PEERS + q]
        )
        for q in range(PEERS)
    ]
    for copy in rest_copies + beside_copies:
        copy.start()

    def fill(source, q, start, count):
        for i in range(count):
            column = start + i // 2 + 8 * (core if i % 2 == 0 else 1 - core)
            hidden[q * TOK : q * TOK + TOK, pl.ds(pl.multiple_of(column * 128, 128), 128)] = (
                source[q, :TOK, 128 * i : 128 * i + 128]
            )

    for q in range(PEERS):
        fill(first, q, 3 * odd, 6)
    for q in range(PEERS):
        rest_copies[q].wait()
        fill(rest, q, 6, 4)
        gather_weight(rest, q, TOK, weight)
    facts[...] = rest[:, 2 * TOK - 16 :, LAST - 128 :]
    sent_copies = []
    for q in range(PEERS):
        beside_copies[q].wait()
        fill(beside, q, 3 - 3 * odd, 6)
        if q % 2 == 1:
            tokens = slice((q - 1) * TOK, (q + 1) * TOK)
            copy = pltpu.make_async_copy(
                hidden.at[tokens], sent.at[tokens], sems.at[2 * PEERS + q // 2]
            )
            copy.start()
            sent_copies.append(copy)
            partial[:, tokens] = lax.dot_general(
                weight[...],
                hidden[tokens, : D // 2],
                (((1,), (1,)), ((), ())),
                preferred_element_type=f32,
            )
    for copy in sent_copies:
        copy.wait()


def half_call(place, first, near, far, last):
    return pl.pallas_call(
        half_kernel,
        in_specs=[SMEM, VMEM, ANY, ANY, ANY],
        out_specs=[VMEM, HBM, VMEM, VMEM],
        out_shape=[
            jax.ShapeDtypeStruct((TOKENS, D), bf16),
            pltpu.HBM((TOKENS, D), bf16),
            jax.ShapeDtypeStruct((CHIP_ROWS, TOKENS), f32),
            jax.ShapeDtypeStruct((PEERS, 16, 128), bf16),
        ],
        scratch_shapes=[
            pltpu.VMEM((CHIP_ROWS, D // 2), bf16),
            pltpu.VMEM((PEERS, TOK, STEP), bf16),
            pltpu.VMEM((PEERS, 2 * TOK, LAST), bf16),
            pltpu.SemaphoreType.DMA((2 * PEERS + 4,)),
        ],
        compiler_params=params,
        cost_estimate=pl.CostEstimate(
            flops=10**11, bytes_accessed=10**8, transcendentals=0
        ),
        name="half",
    )(place, first, near, far, last)


def logits_kernel(hidden, partial, other, logits, stats, facts, weight, table):
    facts[...] = other[:, TOK - 16 :, LAST - 128 :]
    for q in range(PEERS):
        gather_weight(other, q, 0, weight)
    logits[CHIP_ROWS:, :] = jnp.zeros((8, TOKENS), f32)
    for block in range(4):
        tokens = slice(256 * block, 256 * block + 256)
        scores = partial[:, tokens] + lax.dot_general(
            weight[...],
            hidden[tokens, D // 2 :],
            (((1,), (1,)), ((), ())),
            preferred_element_type=f32,
        )
        logits[:CHIP_ROWS, tokens] = scores
        for half in range(2):
            part = scores[:, half * 128 : half * 128 + 128]
            q = block * 2 + half
            top = jnp.max(part, axis=0, keepdims=True)
            shifted = jnp.exp(part - top)
            exp_sum = jnp.sum(shifted, axis=0, keepdims=True)
            exp_dot = jnp.sum(shifted * part, axis=0, keepdims=True)
            table[q : q + 1, :] = top + jnp.log(exp_sum)
            table[8 + q : 9 + q, :] = exp_dot / exp_sum
    stats[...] = jnp.broadcast_to(table[...][None], (16, 16, 128))


def logits_call(hidden, partial, other):
    return pl.pallas_call(
        logits_kernel,
        in_specs=[VMEM] * 3,
        out_specs=[VMEM] * 3,
        out_shape=[
            jax.ShapeDtypeStruct((CHIP_ROWS + 8, TOKENS), f32),
            jax.ShapeDtypeStruct((16, 16, 128), f32),
            jax.ShapeDtypeStruct((PEERS, 16, 128), bf16),
        ],
        scratch_shapes=[
            pltpu.VMEM((CHIP_ROWS, D // 2), bf16),
            pltpu.VMEM((16, 128), f32),
        ],
        compiler_params=params,
        name="logits",
    )(hidden, partial, other)


def tokens_kernel(place, own_facts, other_facts, logits, tokens, state, facts):
    core = place[0]
    for q in range(PEERS):
        facts[2 * q + core] = own_facts[q].astype(f32)
        facts[2 * q + 1 - core] = other_facts[q].astype(f32)
    seg = lax.broadcasted_iota(jnp.int32, (SEGS, 128), 0).astype(f32)
    total = jnp.zeros((SEGS, 128), f32)
    for j in range(2 * PEERS):
        total = total + jnp.where(facts[j, 3:4, :] == seg, facts[j, 4:5, :], 0.0)
        state[j : j + 1, :] = facts[j, 5:6, :] + facts[j, 6:7, :] + facts[j, 7:8, :]
    counts = jnp.broadcast_to(jnp.sum(total, axis=1, keepdims=True), (SEGS, 128))
    row = lax.broadcasted_iota(jnp.int32, (CHIP_ROWS, 128), 0) + place[1]
    tokens[...] = jnp.zeros_like(tokens)
    for q in range(PEERS):
        lanes = slice(q * 128, q * 128 + 128)
        fact = facts[2 * q + core]
        goal = fact[0:1] * 65536.0 + fact[1:2] * 256.0 + fact[2:3]
        hit = row == goal.astype(jnp.int32)
        target_logit = jnp.sum(
            jnp.where(hit, logits[:CHIP_ROWS, lanes], 0.0), axis=0, keepdims=True
        )
        own_count = jnp.sum(jnp.where(fact[3:4] == seg, counts, 0.0), axis=0, keepdims=True)
        tok_weight = fact[4:5] / jnp.maximum(own_count, 1.0) / SEGS
        tokens[0:1, lanes] = tok_weight
        tokens[1:2, lanes] = goal
        tokens[2:3, lanes] = tok_weight * target_logit


def tokens_call(place, own_facts, other_facts, logits):
    return pl.pallas_call(
        tokens_kernel,
        in_specs=[SMEM] + [VMEM] * 3,
        out_specs=[VMEM] * 2,
        out_shape=[
            jax.ShapeDtypeStruct((8, TOKENS), f32),
            jax.ShapeDtypeStruct((16, 128), f32),
        ],
        scratch_shapes=[pltpu.VMEM((16, 16, 128), f32)],
        compiler_params=params,
        cost_estimate=pl.CostEstimate(
            flops=10**10, bytes_accessed=10**7, transcendentals=0
        ),
        name="tokens",
    )(place, own_facts, other_facts, logits)


def merged(stats):
    part, mean = stats[:, :8, :], stats[:, 8:, :]
    top = jnp.max(part, axis=0)
    share = jnp.exp(part - top[None])
    total = jnp.sum(share, axis=0)
    return top + jnp.log(total), jnp.sum(share * mean, axis=0) / total


def merge_kernel(stats, out):
    log_total, mean = merged(stats[...])
    out[:, :8, :] = jnp.broadcast_to(log_total[None], (16, 8, 128))
    out[:, 8:, :] = jnp.broadcast_to(mean[None], (16, 8, 128))


def merge_call(stats):
    return pl.pallas_call(
        merge_kernel,
        in_specs=[VMEM],
        out_specs=VMEM,
        out_shape=jax.ShapeDtypeStruct((16, 16, 128), f32),
        compiler_params=params,
        name="merge",
    )(stats)


def score_block(logits, tokens, log_total, entropy, base, row_start, q):
    lanes = slice(q * 128, q * 128 + 128)
    part = logits[pl.ds(pl.multiple_of(base, 8), PAD), lanes]
    row = lax.broadcasted_iota(jnp.int32, (PAD, 128), 0)
    tok_weight = tokens[0:1, lanes]
    goal = tokens[1:2, lanes].astype(jnp.int32)
    hit = (row + (row_start + base) == goal).astype(f32)
    above = part - log_total[q : q + 1, :]
    probability = jnp.exp(above)
    score = tok_weight * (
        probability - hit + penalty * probability * (above + entropy[q : q + 1, :])
    )
    return jnp.where(row < OWN, score, 0.0).astype(bf16)


def fetch(source, target, sems):
    copies = []
    for block in range(4):
        tokens = slice(block * 256, block * 256 + 256)
        copy = pltpu.make_async_copy(source.at[tokens], target.at[tokens], sems.at[block])
        copy.start()
        copies.append(copy)
    return copies


def away_kernel(place, stats, logits, tokens, hidden, score, totals, fetched, sems):
    copies = fetch(hidden, fetched, sems)
    core = place[0]
    log_total, mean = merged(stats[...])
    entropy = log_total - mean
    totals[:8, :] = log_total
    totals[8:, :] = entropy
    for q in range(PEERS):
        score[:, q * 128 : q * 128 + 128] = score_block(
            logits, tokens, log_total, entropy, (1 - core) * OWN, place[1], q
        )
    for copy in copies:
        copy.wait()


def away_call(place, stats, logits, tokens, hidden):
    return pl.pallas_call(
        away_kernel,
        in_specs=[SMEM, VMEM, VMEM, VMEM, HBM],
        out_specs=[VMEM] * 3,
        out_shape=[
            jax.ShapeDtypeStruct((PAD, TOKENS), bf16),
            jax.ShapeDtypeStruct((16, 128), f32),
            pltpu.VMEM((TOKENS, D), bf16),
        ],
        scratch_shapes=[pltpu.SemaphoreType.DMA((4,))],
        compiler_params=params,
        name="away",
    )(place, stats, logits, tokens, hidden)


def own_kernel(place, totals, logits, tokens, hidden, other, out, fetched, score, sems):
    copies = fetch(other, fetched, sems)
    for q in range(PEERS):
        score[:, q * 128 : q * 128 + 128] = score_block(
            logits, tokens, totals[:8, :], totals[8:, :], place[0] * OWN, place[1], q
        )
    for block in range(4):
        lanes = slice(block * 512, block * 512 + 512)
        out[:, lanes] = jnp.dot(score[...], hidden[:, lanes], preferred_element_type=f32)
    for copy in copies:
        copy.wait()


def own_call(place, totals, logits, tokens, hidden, other):
    return pl.pallas_call(
        own_kernel,
        in_specs=[SMEM] + [VMEM] * 4 + [HBM],
        out_specs=[VMEM] * 2,
        out_shape=[
            jax.ShapeDtypeStruct((PAD, D), f32),
            pltpu.VMEM((TOKENS, D), bf16),
        ],
        scratch_shapes=[
            pltpu.VMEM((PAD, TOKENS), bf16),
            pltpu.SemaphoreType.DMA((4,)),
        ],
        compiler_params=params,
        name="own",
    )(place, totals, logits, tokens, hidden, other)


def split_rows(value):
    high = value.astype(bf16).astype(f32)
    rest = value - high
    middle = rest.astype(bf16).astype(f32)
    return [high, middle, rest - middle]


def join_rows(total, start):
    return total[start : start + 1] + total[start + 1 : start + 2] + total[start + 2 : start + 3]


def grad_kernel(
    place, partial, score, hidden, state, totals, tokens, scaled, sums, grad, table
):
    core = place[0]
    places = [2 * i + core for i in range(8)] + [2 * i + 1 - core for i in range(8)]
    squares = jnp.zeros((PAD, 128), f32)
    for source in range(4):
        block = (source + 2) % 4
        lanes = slice(block * 512, block * 512 + 512)
        start = source * 512
        value = partial[:, lanes] + jnp.dot(
            score[...], hidden[:, start : start + 512], preferred_element_type=f32
        )
        grad[:, lanes] = value
        for i in range(4):
            part = value[:, 128 * i : 128 * i + 128]
            part = part * part
            squares = squares + part
            table[pl.ds(places[4 * block + i], 1), :] = jnp.sum(part, axis=0, keepdims=True)
    diagonal = lax.broadcasted_iota(jnp.int32, (PAD, PAD), 0) == lax.broadcasted_iota(
        jnp.int32, (PAD, PAD), 1
    )
    old = jnp.sum(jnp.where(diagonal, state[...], 0.0), axis=1, keepdims=True)
    row_new = decay_rate * old + (1.0 - decay_rate) * (
        jnp.sum(squares, axis=1, keepdims=True) / D
    )
    scale = jnp.broadcast_to(lax.rsqrt(row_new), (PAD, 128))
    row = lax.broadcasted_iota(jnp.int32, (PAD, 128), 0)
    lane = lax.broadcasted_iota(jnp.int32, (PAD, 128), 1)
    kept = jnp.where((row < OWN) & (lane == 0), jnp.broadcast_to(row_new, (PAD, 128)), 0.0)
    row_total = jnp.sum(kept, axis=0, keepdims=True)
    loss = jnp.zeros((1, 128), f32)
    for q in range(PEERS):
        lanes = slice(128 * q, 128 * q + 128)
        loss = loss + (
            tokens[0:1, lanes]
            * (totals[q : q + 1, :] - penalty * totals[8 + q : 9 + q, :])
            * (1.0 / 256.0)
            - tokens[2:3, lanes]
        )
    table[32:48, :] = jnp.zeros((16, 128), f32)
    for i, line in enumerate(split_rows(row_total) + split_rows(loss)):
        table[32 + i : 33 + i, :] = line
    for i, j in enumerate(places):
        part = grad[:, 128 * i : 128 * i + 128] * scale
        scaled[:, pl.ds(pl.multiple_of(j * 128, 128), 128)] = part
        table[pl.ds(16 + j, 1), :] = jnp.sum(part * part, axis=0, keepdims=True)
    sums[...] = jnp.broadcast_to(table[...].astype(bf16)[None], (32, 48, 128))


def grad_call(place, partial, score, hidden, state, totals, tokens):
    return pl.pallas_call(
        grad_kernel,
        in_specs=[SMEM] + [VMEM] * 6,
        out_specs=[VMEM] * 2,
        out_shape=[
            jax.ShapeDtypeStruct((PAD, D), f32),
            jax.ShapeDtypeStruct((32, 48, 128), bf16),
        ],
        scratch_shapes=[
            pltpu.VMEM((PAD, D), f32),
            pltpu.VMEM((48, 128), f32),
        ],
        compiler_params=params,
        name="grad",
    )(place, partial, score, hidden, state, totals, tokens)


def add_kernel(sums, out):
    total = jnp.sum(sums[...].astype(f32), axis=0)
    lines = split_rows(join_rows(total, 32)) + split_rows(join_rows(total, 35))
    row = lax.broadcasted_iota(jnp.int32, (16, 128), 0)
    tail = jnp.zeros((16, 128), f32)
    for i, line in enumerate(lines):
        tail = jnp.where(row == i, line, tail)
    out[:, :32, :] = jnp.broadcast_to(total[:32].astype(bf16)[None], (16, 32, 128))
    out[:, 32:, :] = jnp.broadcast_to(tail.astype(bf16)[None], (16, 16, 128))


def add_call(sums):
    return pl.pallas_call(
        add_kernel,
        in_specs=[VMEM],
        out_specs=VMEM,
        out_shape=jax.ShapeDtypeStruct((16, 48, 128), bf16),
        compiler_params=params,
        name="add",
    )(sums)


def update_kernel(sums, state, scaled, out, loss):
    total = jnp.sum(sums[...].astype(f32), axis=0)
    column_new = decay_rate * state[...] + (1.0 - decay_rate) * (total[:16] / V)
    column_scale = lax.rsqrt(column_new)
    row_mean = jnp.broadcast_to(jnp.sum(join_rows(total, 32), keepdims=True) / V, (16, 128))
    square_total = jnp.sum(total[16:32] * column_scale * column_scale, keepdims=True)
    square_total = row_mean * jnp.broadcast_to(square_total, (16, 128))
    update_rms = jnp.sqrt(square_total / (V * D))
    factor = jnp.sqrt(row_mean) * column_scale / jnp.maximum(1.0, update_rms / clip_limit)
    for j in range(16):
        out[j] = (scaled[:OWN, 128 * j : 128 * j + 128] * factor[j : j + 1, :]).astype(bf16)
    loss[...] = jnp.broadcast_to(jnp.sum(join_rows(total, 35), keepdims=True), (8, 128))


def update_call(sums, state, scaled):
    return pl.pallas_call(
        update_kernel,
        in_specs=[VMEM] * 3,
        out_specs=[VMEM] * 2,
        out_shape=[
            jax.ShapeDtypeStruct((16, OWN, 128), bf16),
            jax.ShapeDtypeStruct((8, 128), f32),
        ],
        compiler_params=params,
        name="update",
    )(sums, state, scaled)


def per_device(hidden, head_weight, targets, segments, loss_mask, row_state, column_state):
    core = lax.axis_index("core")
    chip = lax.axis_index(CHIPS)
    odd = lax.axis_index("z") % 2
    chip_start = chip * CHIP_ROWS
    place = jnp.stack([core, lax.axis_index(MP) * VOC + chip_start, odd]).astype(jnp.int32)
    own_state = lax.dynamic_slice_in_dim(row_state, chip_start + core * OWN, OWN, axis=0)
    own_state = jnp.concatenate([own_state, jnp.ones((PAD - OWN,), f32)]).reshape(1, PAD)
    place, own_state, targets = lax.optimization_barrier((place, own_state, targets))

    first = trade(spread(hidden), CHIPS)
    last = pack(hidden, head_weight, targets, segments, loss_mask, column_state)
    last, first = lax.optimization_barrier((last, first))
    last = trade(last, CHIPS)
    near = lax.ppermute(first[:4], "z", [(i, i ^ 1) for i in range(16)])
    far = lax.ppermute(first[4:], "z", [(i, (i + 1 if i % 2 else i - 1) % 16) for i in range(16)])
    head_other = swap_cores(last[:, TOK:, :])
    hidden_own, hidden_sent, partial, own_facts = half_call(place, first, near, far, last)
    logits, stats, other_facts = logits_call(hidden_own, partial, head_other)
    stats, hidden_sent = lax.optimization_barrier((stats, hidden_sent))
    tokens, state = tokens_call(place, own_facts, other_facts, logits)
    hidden_other = swap_cores(hidden_sent)
    stats = merge_call(trade(stats, PLANE))
    stats = trade(stats, "z")
    score_away, totals, hidden_own = away_call(place, stats, logits, tokens, hidden_sent)
    score_other = swap_cores(score_away)
    partial, hidden_other = own_call(
        place, totals, logits, tokens, hidden_own, hidden_other
    )
    scaled, sums = grad_call(
        place, partial, score_other, hidden_other, own_state, totals, tokens
    )
    sums = add_call(trade(sums, ("y", "xh", "core", "xl")))
    update, loss = update_call(trade(sums, "z"), state, scaled)
    update_step = trade(update, DP).reshape(VOC, COLS)
    return (update_step, loss[0, 0])


def solution(mesh):
    fine = Mesh(mesh.devices.reshape(4, 2, 2, 16, 2), AXES)
    return jax.shard_map(
        per_device,
        mesh=fine,
        in_specs=(P(DP, None), P(MP, DP), P(DP), P(DP), P(DP), P(MP), P(DP)),
        out_specs=(P(MP, DP), P()),
        check_vma=False,
    )
```

time: 194 us -> 188 us (0.969)
  blocking collectives: 62 us -> 41.9 us
  starting transfers between devices: 52.4 us -> 62.5 us
  waiting for transfers between devices: 43.3 us -> 52.3 us
  local copies, waits for them, and re-layouts: 12.7 us -> 5.86 us
  Pallas kernels: 21.4 us -> 23.6 us
    all_to_all x4 -> x3, blocking collectives: 62 us -> 41.9 us  [trade(): return lax.all_to_all(value, axes, 0, 0)]
    all_to_all x3 -> x4, waiting for transfers between devices: 41 us -> 51.8 us  [trade(): return lax.all_to_all(value, axes, 0, 0)]
    all_to_all x3 -> x4, starting transfers between devices: 21.2 us -> 30.2 us  [trade(): return lax.all_to_all(value, axes, 0, 0)]
    unnamed x23 -> x15, local copies, waits for them, and re-layouts: 6.41 us -> 2.03 us
    ppermute x1, starting transfers between devices: 4.76 us -> 1.92 us  [per_device(): near = lax.ppermute(first[:4], 'z', [(i, i ^ 1) for i in range(16)])]
    ppermute x1, starting transfers between devices: 10.2 us -> 12.9 us  [per_device(): lax.ppermute(first[4:], 'z', [(i, (i + 1 if i % 2 else i - 1) % 16) for i...]
    pallas_call x1, Pallas kernels: 0.46 us -> 3.11 us  [pack(): pl.pallas_call(pack_kernel, grid=(PEERS,), in_specs=[pl.BlockSpec((TOK, L...]
    ppermute x1, waiting for transfers between devices: 2.29 us -> 0.01 us  [per_device(): lax.ppermute(first[4:], 'z', [(i, (i + 1 if i % 2 else i - 1) % 16) for i...]
  transfers between devices with their start and end apart: 8 -> 9, of which waited for: 4 -> 5; matrix products, arithmetic and copies ran while one was open for 2% -> 2% of each run, Pallas kernels for 5% -> 9%
where the time goes in v3:
time: 188 us; the launch traced here: 187 us
  starting transfers between devices  62.5 us (33%)
  waiting for transfers between devices  52.3 us (28%)
  blocking collectives  41.9 us (22%)
  Pallas kernels  23.6 us (13%)
  local copies, waits for them, and re-layouts  5.86 us (3%)
    all_to_all x4, waiting for transfers between devices, trade(): return lax.all_to_all(value, axes, 0, 0)  51.8 us
    all_to_all x3, blocking collectives, trade(): return lax.all_to_all(value, axes, 0, 0)  41.9 us
    all_to_all x4, starting transfers between devices, trade(): return lax.all_to_all(value, axes, 0, 0)  30.2 us
    ppermute x3, starting transfers between devices, swap_cores(): return lax.ppermute(value, 'core', [(0, 1), (1, 0)])  17.4 us
    ppermute x1, starting transfers between devices, per_device(): lax.ppermute(first[4:], 'z', [(i, (i + 1 if i % 2 else i - 1) % 16) for i...  12.9 us
    pallas_call x1, Pallas kernels, half_call(): pl.pallas_call(half_kernel, in_specs=[SMEM, VMEM, ANY, ANY, ANY], out_spe...  6.33 us
  transfers between devices with their start and end apart: 9, of which 5 were waited for; matrix products, arithmetic and copies ran while one was open for 2% of the time, Pallas kernels for 9%

profile of v3, /device:TPU:1, one launch (start us, length us, event | category | flops | bytes accessed | tf_op | source)
XLA Modules:
  0.0 187.0 jit_solution(5894410834660004146)
XLA Ops:
  3.0 7.6 %all-to-all-start = ((bf16[8,128,768]{2,1,0:T(8,128)(2,1)}), bf16[8,128,768]{2,1,0:T(8,128)(2,1)S(1)}, u32[]{:S(2)}, u32[]{:S(2)}) async-start(bf16[8,128,768]{2,1,0:T(8,128)(2,1)} %spread.1), calls=%async_computation | async-start | bytes 3145728 | tf_op jit(solution)/shard_map/all_to_all | solution.py:48
  11.5 3.1 %pack.1 = bf16[8,256,512]{2,1,0:T(8,128)(2,1)} custom-call(bf16[128,2048]{1,0:T(8,128)(2,1)S(1)} %copy-done.1, bf16[3968,128]{1,0:T(8,128)(2,1)S(1)} %copy-done.2, s32[1,128]{1,0:T(1,128)S(1)} %bitcast.11, s32[1,128]{1,0:T(1,128)S(1)} %bitcast.12, s32[1,128]{1,0:T(1,128)S(1)} %bitcast.13, f32[1,128]{1,0:T(1,128)S(1)} %bitcast.14), custom_call_target="tpu_custom_call" | custom-call | tf_op jit(solution)/shard_map/pack/pallas_call | solution.py:83
  14.6 15.6 %all-to-all-done.first = bf16[8,128,768]{2,1,0:T(8,128)(2,1)S(1)} async-done(((bf16[8,128,768]{2,1,0:T(8,128)(2,1)}), bf16[8,128,768]{2,1,0:T(8,128)(2,1)S(1)}, u32[]{:S(2)}, u32[]{:S(2)}) %all-to-all-start) | async-done | bytes 1572896 | tf_op jit(solution)/shard_map/all_to_all | solution.py:48
  30.3 4.9 %all-to-all-start.1 = ((bf16[8,256,512]{2,1,0:T(8,128)(2,1)}), bf16[8,256,512]{2,1,0:T(8,128)(2,1)}, u32[]{:S(2)}, u32[]{:S(2)}) async-start(bf16[8,256,512]{2,1,0:T(8,128)(2,1)} %pack.1), calls=%async_computation.1 | async-start | bytes 4194304 | tf_op jit(solution)/shard_map/all_to_all | solution.py:48
  36.4 12.9 %collective-permute-start.1 = (bf16[4,128,768]{2,1,0:T(8,128)(2,1)}, bf16[4,128,768]{2,1,0:T(8,128)(2,1)S(1)}, u32[]{:S(2)}, u32[]{:S(2)}) collective-permute-start(bf16[4,128,768]{2,1,0:T(8,128)(2,1)} %get-tuple-element.52), channel_id=1, source_target_pairs={{0,30},{2,4},{4,2},{6,8},{8,6},{10,12},{12,10},{14,16},{16,14},{18... | collective-permute-start | bytes 2359304 | tf_op jit(solution)/shard_map/ppermute | solution.py:560
  49.3 1.9 %collective-permute-start = (bf16[4,128,768]{2,1,0:T(8,128)(2,1)}, bf16[4,128,768]{2,1,0:T(8,128)(2,1)}, u32[]{:S(2)}, u32[]{:S(2)}) collective-permute-start(bf16[4,128,768]{2,1,0:T(8,128)(2,1)} %get-tuple-element.53), channel_id=1, source_target_pairs={{0,2},{2,0},{4,6},{6,4},{8,10},{10,8},{12,14},{14,12},{16,18},{18,... | collective-permute-start | bytes 2359304 | tf_op jit(solution)/shard_map/ppermute | solution.py:559
  51.2 8.7 %all-to-all-done.1.last = bf16[8,256,512]{2,1,0:T(8,128)(2,1)} async-done(((bf16[8,256,512]{2,1,0:T(8,128)(2,1)}), bf16[8,256,512]{2,1,0:T(8,128)(2,1)}, u32[]{:S(2)}, u32[]{:S(2)}) %all-to-all-start.1) | async-done | bytes 2097184 | tf_op jit(solution)/shard_map/all_to_all | solution.py:48
  59.9 1.3 slice.16
  61.2 6.7 %collective-permute-start.2 = (bf16[8,128,512]{2,1,0:T(8,128)(2,1)S(1)}, bf16[8,128,512]{2,1,0:T(8,128)(2,1)S(1)}, u32[]{:S(2)}, u32[]{:S(2)}) collective-permute-start(bf16[8,128,512]{2,1,0:T(8,128)(2,1)S(1)} %slice.16), channel_id=1, source_target_pairs={{0,32},{32,0},{1,33},{33,1},{2,34},{34,2},{3,35},{35,3},{4,36},{36... | collective-permute-start | bytes 3145736 | tf_op jit(solution)/shard_map/ppermute | solution.py:44
  68.3 6.3 %half.1 = (bf16[1024,2048]{1,0:T(8,128)(2,1)S(1)}, bf16[1024,2048]{1,0:T(8,128)(2,1)}, f32[496,1024]{1,0:T(8,128)S(1)}, bf16[8,16,128]{2,1,0:T(8,128)(2,1)S(1)}) custom-call(s32[3]{0:T(128)S(1)} %pad_add_fusion.place, bf16[8,128,768]{2,1,0:T(8,128)(2,1)S(1)} %all-to-all-done.first, bf16[4,128,768]{2,1,0:T(8,128)(2,1)} %collective-permute-done.near, ...), custom_call_target="tpu_custom_call" | custom-call | flops 99999997952 | bytes 100000000 | tf_op jit(solution)/shard_map/half/pallas_call | solution.py:189
  74.7 1.8 logits.1
  76.4 5.0 %collective-permute-start.3 = (bf16[1024,2048]{1,0:T(8,128)(2,1)}, bf16[1024,2048]{1,0:T(8,128)(2,1)}, u32[]{:S(2)}, u32[]{:S(2)}) collective-permute-start(bf16[1024,2048]{1,0:T(8,128)(2,1)} %get-tuple-element.40.hidden), channel_id=1, source_target_pairs={{0,32},{32,0},{1,33},{33,1},{2,34},{34,2},{3,35},{35,3},{4,36},{36... | collective-permute-start | bytes 12582920 | tf_op jit(solution)/shard_map/ppermute | solution.py:44
  81.4 13.6 %all_to_all.35.stats = f32[16,16,128]{2,1,0:T(8,128)S(1)} all-to-all(f32[16,16,128]{2,1,0:T(8,128)S(1)} %get-tuple-element.35), channel_id=1, replica_groups=mesh['y'=4,'xh'=2,'core'=2,'z'=16,'xl'=2] {'y','xh','xl'}, dimensions={0} | all-to-all | bytes 262144 | tf_op jit(solution)/shard_map/all_to_all | solution.py:48
  95.7 8.9 %all-to-all-start.3 = ((f32[16,16,128]{2,1,0:T(8,128)}), f32[16,16,128]{2,1,0:T(8,128)S(1)}, u32[]{:S(2)}, u32[]{:S(2)}) async-start(f32[16,16,128]{2,1,0:T(8,128)} %merge.1), calls=%async_computation.3 | async-start | bytes 262144 | tf_op jit(solution)/shard_map/all_to_all | solution.py:48
  105.6 11.1 %all-to-all-done.3.stats = f32[16,16,128]{2,1,0:T(8,128)S(1)} async-done(((f32[16,16,128]{2,1,0:T(8,128)}), f32[16,16,128]{2,1,0:T(8,128)S(1)}, u32[]{:S(2)}, u32[]{:S(2)}) %all-to-all-start.3) | async-done | bytes 131104 | tf_op jit(solution)/shard_map/all_to_all | solution.py:48
  116.7 2.7 %away.1 = (bf16[256,1024]{1,0:T(8,128)(2,1)S(1)}, f32[16,128]{1,0:T(8,128)S(1)}, bf16[1024,2048]{1,0:T(8,128)(2,1)S(1)}) custom-call(s32[3]{0:T(128)S(1)} %pad_add_fusion.place, f32[16,16,128]{2,1,0:T(8,128)S(1)} %all-to-all-done.3.stats, f32[504,1024]{1,0:T(8,128)S(1)} %get-tuple-element.36.logits, f32[8,1024]{1,0:T(8,128)S(1)} %get-tuple-element.39.tokens, ...), custom_call_target="tpu_custom_call" | custom-call | tf_op jit(solution)/shard_map/away/pallas_call | solution.py:370
  119.5 5.8 %collective-permute-start.4 = (bf16[256,1024]{1,0:T(8,128)(2,1)S(1)}, bf16[256,1024]{1,0:T(8,128)(2,1)S(1)}, u32[]{:S(2)}, u32[]{:S(2)}) collective-permute-start(bf16[256,1024]{1,0:T(8,128)(2,1)S(1)} %get-tuple-element.44), channel_id=1, source_target_pairs={{0,32},{32,0},{1,33},{33,1},{2,34},{34,2},{3,35},{35,3},{4,36},{36... | collective-permute-start | bytes 1572872 | tf_op jit(solution)/shard_map/ppermute | solution.py:44
  125.3 3.1 %own.1 = (f32[256,2048]{1,0:T(8,128)S(1)}, bf16[1024,2048]{1,0:T(8,128)(2,1)S(1)}) custom-call(s32[3]{0:T(128)S(1)} %pad_add_fusion.place, f32[16,128]{1,0:T(8,128)S(1)} %get-tuple-element.41.totals, f32[504,1024]{1,0:T(8,128)S(1)} %get-tuple-element.36.logits, f32[8,1024]{1,0:T(8,128)S(1)} %get-tuple-element.39.tokens, ...), custom_call_target="tpu_custom_call" | custom-call | tf_op jit(solution)/shard_map/own/pallas_call | solution.py:399
  128.4 2.4 %grad.1 = (f32[256,2048]{1,0:T(8,128)S(1)}, bf16[32,48,128]{2,1,0:T(8,128)(2,1)S(1)}) custom-call(s32[3]{0:T(128)S(1)} %pad_add_fusion.place, f32[256,2048]{1,0:T(8,128)S(1)} %get-tuple-element.43.partial, bf16[256,1024]{1,0:T(8,128)(2,1)S(1)} %collective-permute-done.4.score, bf16[1024,2048]{1,0:T(8,128)(2,1)S(1)} %get-tuple-element.45.hidden, ...), custom_call_target="tpu_custom_call" | custom-call | tf_op jit(solution)/shard_map/grad/pallas_call | solution.py:478
  130.8 12.5 %all_to_all.36.sums = bf16[32,48,128]{2,1,0:T(8,128)(2,1)S(1)} all-to-all(bf16[32,48,128]{2,1,0:T(8,128)(2,1)S(1)} %get-tuple-element.47), channel_id=1, replica_groups=mesh['y'=4,'xh'=2,'core'=2,'z'=16,'xl'=2] {'y','xh','core','xl'}, dimensions={0} | all-to-all | bytes 786432 | tf_op jit(solution)/shard_map/all_to_all | solution.py:48
  143.4 15.8 %all_to_all.37.sums = bf16[16,48,128]{2,1,0:T(8,128)(2,1)S(1)} all-to-all(bf16[16,48,128]{2,1,0:T(8,128)(2,1)S(1)} %add.32), channel_id=1, replica_groups=mesh['y'=4,'xh'=2,'core'=2,'z'=16,'xl'=2] {'z'}, dimensions={0} | all-to-all | bytes 393216 | tf_op jit(solution)/shard_map/all_to_all | solution.py:48
  159.2 1.3 update.1
  160.4 8.8 %all-to-all-start.6 = ((bf16[16,248,128]{2,1,0:T(8,128)(2,1)}), bf16[16,248,128]{2,1,0:T(8,128)(2,1)S(1)}, u32[]{:S(2)}, u32[]{:S(2)}) async-start(bf16[16,248,128]{2,1,0:T(8,128)(2,1)} %get-tuple-element.50), calls=%async_computation.6 | async-start | bytes 2031616 | tf_op jit(solution)/shard_map/all_to_all | solution.py:48
  169.7 16.3 %all-to-all-done.6 = bf16[16,248,128]{2,1,0:T(8,128)(2,1)S(1)} async-done(((bf16[16,248,128]{2,1,0:T(8,128)(2,1)}), bf16[16,248,128]{2,1,0:T(8,128)(2,1)S(1)}, u32[]{:S(2)}, u32[]{:S(2)}) %all-to-all-start.6) | async-done | bytes 1015840 | tf_op jit(solution)/shard_map/all_to_all | solution.py:48
  (29 shorter events, 8.1 us)
Async XLA Ops:
  0.6 1.0 copy-start
  2.9 8.6 %copy-start.1 = (bf16[128,2048]{1,0:T(8,128)(2,1)S(1)}, bf16[128,2048]{1,0:T(8,128)(2,1)}, u32[]{:S(2)}) copy-start(bf16[128,2048]{1,0:T(8,128)(2,1)} %hidden.3) | copy-start | bytes 1572868
  2.9 8.5 %copy-start.2 = (bf16[3968,128]{1,0:T(8,128)(2,1)S(1)}, bf16[3968,128]{1,0:T(8,128)(2,1)}, u32[]{:S(2)}) copy-start(bf16[3968,128]{1,0:T(8,128)(2,1)} %head.1) | copy-start | bytes 3047428
  2.9 8.5 %copy-start.3 = (s32[128]{0:T(128)S(1)}, s32[128]{0:T(128)}, u32[]{:S(2)}) copy-start(s32[128]{0:T(128)} %param.9) | copy-start | bytes 1540
  3.0 8.5 %copy-start.4 = (s32[128]{0:T(128)S(1)}, s32[128]{0:T(128)}, u32[]{:S(2)}) copy-start(s32[128]{0:T(128)} %param.10) | copy-start | bytes 1540
  3.0 8.5 %copy-start.5 = (s32[128]{0:T(128)S(1)}, s32[128]{0:T(128)}, u32[]{:S(2)}) copy-start(s32[128]{0:T(128)} %param.11) | copy-start | bytes 1540
  3.0 8.5 %copy-start.6 = (f32[128]{0:T(128)S(1)}, f32[128]{0:T(128)}, u32[]{:S(2)}) copy-start(f32[128]{0:T(128)} %param.13) | copy-start | bytes 1540
  3.0 27.3 %all-to-all-start = ((bf16[8,128,768]{2,1,0:T(8,128)(2,1)}), bf16[8,128,768]{2,1,0:T(8,128)(2,1)S(1)}, u32[]{:S(2)}, u32[]{:S(2)}) async-start(bf16[8,128,768]{2,1,0:T(8,128)(2,1)} %spread.1), calls=%async_computation | async-start | bytes 3145728 | tf_op jit(solution)/shard_map/all_to_all | solution.py:48
  30.3 29.6 %all-to-all-start.1 = ((bf16[8,256,512]{2,1,0:T(8,128)(2,1)}), bf16[8,256,512]{2,1,0:T(8,128)(2,1)}, u32[]{:S(2)}, u32[]{:S(2)}) async-start(bf16[8,256,512]{2,1,0:T(8,128)(2,1)} %pack.1), calls=%async_computation.1 | async-start | bytes 4194304 | tf_op jit(solution)/shard_map/all_to_all | solution.py:48
  36.4 31.5 %collective-permute-start.1 = (bf16[4,128,768]{2,1,0:T(8,128)(2,1)}, bf16[4,128,768]{2,1,0:T(8,128)(2,1)S(1)}, u32[]{:S(2)}, u32[]{:S(2)}) collective-permute-start(bf16[4,128,768]{2,1,0:T(8,128)(2,1)} %get-tuple-element.52), channel_id=1, source_target_pairs={{0,30},{2,4},{4,2},{6,8},{8,6},{10,12},{12,10},{14,16},{16,14},{18... | collective-permute-start | bytes 2359304 | tf_op jit(solution)/shard_map/ppermute | solution.py:560
  49.3 19.1 %collective-permute-start = (bf16[4,128,768]{2,1,0:T(8,128)(2,1)}, bf16[4,128,768]{2,1,0:T(8,128)(2,1)}, u32[]{:S(2)}, u32[]{:S(2)}) collective-permute-start(bf16[4,128,768]{2,1,0:T(8,128)(2,1)} %get-tuple-element.53), channel_id=1, source_target_pairs={{0,2},{2,0},{4,6},{6,4},{8,10},{10,8},{12,14},{14,12},{16,18},{18,... | collective-permute-start | bytes 2359304 | tf_op jit(solution)/shard_map/ppermute | solution.py:559
  61.2 13.5 %collective-permute-start.2 = (bf16[8,128,512]{2,1,0:T(8,128)(2,1)S(1)}, bf16[8,128,512]{2,1,0:T(8,128)(2,1)S(1)}, u32[]{:S(2)}, u32[]{:S(2)}) collective-permute-start(bf16[8,128,512]{2,1,0:T(8,128)(2,1)S(1)} %slice.16), channel_id=1, source_target_pairs={{0,32},{32,0},{1,33},{33,1},{2,34},{34,2},{3,35},{35,3},{4,36},{36... | collective-permute-start | bytes 3145736 | tf_op jit(solution)/shard_map/ppermute | solution.py:44
  76.4 48.8 %collective-permute-start.3 = (bf16[1024,2048]{1,0:T(8,128)(2,1)}, bf16[1024,2048]{1,0:T(8,128)(2,1)}, u32[]{:S(2)}, u32[]{:S(2)}) collective-permute-start(bf16[1024,2048]{1,0:T(8,128)(2,1)} %get-tuple-element.40.hidden), channel_id=1, source_target_pairs={{0,32},{32,0},{1,33},{33,1},{2,34},{34,2},{3,35},{35,3},{4,36},{36... | collective-permute-start | bytes 12582920 | tf_op jit(solution)/shard_map/ppermute | solution.py:44
  95.7 21.0 %all-to-all-start.3 = ((f32[16,16,128]{2,1,0:T(8,128)}), f32[16,16,128]{2,1,0:T(8,128)S(1)}, u32[]{:S(2)}, u32[]{:S(2)}) async-start(f32[16,16,128]{2,1,0:T(8,128)} %merge.1), calls=%async_computation.3 | async-start | bytes 262144 | tf_op jit(solution)/shard_map/all_to_all | solution.py:48
  119.5 8.9 %collective-permute-start.4 = (bf16[256,1024]{1,0:T(8,128)(2,1)S(1)}, bf16[256,1024]{1,0:T(8,128)(2,1)S(1)}, u32[]{:S(2)}, u32[]{:S(2)}) collective-permute-start(bf16[256,1024]{1,0:T(8,128)(2,1)S(1)} %get-tuple-element.44), channel_id=1, source_target_pairs={{0,32},{32,0},{1,33},{33,1},{2,34},{34,2},{3,35},{35,3},{4,36},{36... | collective-permute-start | bytes 1572872 | tf_op jit(solution)/shard_map/ppermute | solution.py:44
  160.4 25.7 %all-to-all-start.6 = ((bf16[16,248,128]{2,1,0:T(8,128)(2,1)}), bf16[16,248,128]{2,1,0:T(8,128)(2,1)S(1)}, u32[]{:S(2)}, u32[]{:S(2)}) async-start(bf16[16,248,128]{2,1,0:T(8,128)(2,1)} %get-tuple-element.50), calls=%async_computation.6 | async-start | bytes 2031616 | tf_op jit(solution)/shard_map/all_to_all | solution.py:48

commit v4 on v3

--- a/solution.py
+++ b/solution.py
@@ -33,7 +33,7 @@
 bf16 = jnp.bfloat16
 
 params = pltpu.CompilerParams(vmem_limit_bytes=16 * 1024 * 1024)
-large = pltpu.CompilerParams(vmem_limit_bytes=16 * 1024 * 1024)
+large = pltpu.CompilerParams(vmem_limit_bytes=63 * 1024 * 1024 + 512 * 1024)
 VMEM = pl.BlockSpec(memory_space=pltpu.VMEM)
 SMEM = pl.BlockSpec(memory_space=pltpu.SMEM)
 ANY = pl.BlockSpec(memory_space=pl.ANY)
@@ -93,7 +93,7 @@
         ],
         out_specs=pl.BlockSpec((1, 2 * TOK, LAST), lambda i: (i, 0, 0)),
         out_shape=pltpu.HBM((PEERS, 2 * TOK, LAST), bf16),
-        compiler_params=large,
+        compiler_params=params,
         name="pack",
     )(hidden, head, *[x.reshape(1, 128) for x in (targets, segments, mask, state)])
 
@@ -120,7 +120,7 @@
             pltpu.VMEM((TOK, STEP), bf16),
             pltpu.SemaphoreType.DMA((PEERS + 1,)),
         ],
-        compiler_params=params,
+        compiler_params=large,
         name="spread",
     )(hidden)
 
@@ -147,8 +147,9 @@
         )
         for q in range(PEERS)
     ]
-    for copy in rest_copies + beside_copies:
-        copy.start()
+    for q in range(PEERS):
+        rest_copies[q].start()
+        beside_copies[q].start()
 
     def fill(source, q, start, count):
         for i in range(count):
@@ -157,15 +158,12 @@
                 source[q, :TOK, 128 * i : 128 * i + 128]
             )
 
+    sent_copies = []
     for q in range(PEERS):
         fill(first, q, 3 * odd, 6)
-    for q in range(PEERS):
         rest_copies[q].wait()
         fill(rest, q, 6, 4)
         gather_weight(rest, q, TOK, weight)
-    facts[...] = rest[:, 2 * TOK - 16 :, LAST - 128 :]
-    sent_copies = []
-    for q in range(PEERS):
         beside_copies[q].wait()
         fill(beside, q, 3 - 3 * odd, 6)
         if q % 2 == 1:
@@ -175,12 +173,15 @@
             )
             copy.start()
             sent_copies.append(copy)
-            partial[:, tokens] = lax.dot_general(
-                weight[...],
-                hidden[tokens, : D // 2],
-                (((1,), (1,)), ((), ())),
-                preferred_element_type=f32,
-            )
+    facts[...] = rest[:, 2 * TOK - 16 :, LAST - 128 :]
+    for block in range(4):
+        tokens = slice(256 * block, 256 * block + 256)
+        partial[:, tokens] = lax.dot_general(
+            weight[...],
+            hidden[tokens, : D // 2],
+            (((1,), (1,)), ((), ())),
+            preferred_element_type=f32,
+        )
     for copy in sent_copies:
         copy.wait()
 
@@ -211,9 +212,9 @@
 
 
 def logits_kernel(hidden, partial, other, logits, stats, facts, weight, table):
-    facts[...] = other[:, TOK - 16 :, LAST - 128 :]
-    for q in range(PEERS):
-        gather_weight(other, q, 0, weight)
+    facts[...] = other[:, 2 * TOK - 16 :, LAST - 128 :]
+    for q in range(PEERS):
+        gather_weight(other, q, TOK, weight)
     logits[CHIP_ROWS:, :] = jnp.zeros((8, TOKENS), f32)
     for block in range(4):
         tokens = slice(256 * block, 256 * block + 256)
@@ -558,9 +559,9 @@
     last = trade(last, CHIPS)
     near = lax.ppermute(first[:4], "z", [(i, i ^ 1) for i in range(16)])
     far = lax.ppermute(first[4:], "z", [(i, (i + 1 if i % 2 else i - 1) % 16) for i in range(16)])
-    head_other = swap_cores(last[:, TOK:, :])
+    last_other = swap_cores(last)
     hidden_own, hidden_sent, partial, own_facts = half_call(place, first, near, far, last)
-    logits, stats, other_facts = logits_call(hidden_own, partial, head_other)
+    logits, stats, other_facts = logits_call(hidden_own, partial, last_other)
     stats, hidden_sent = lax.optimization_barrier((stats, hidden_sent))
     tokens, state = tokens_call(place, own_facts, other_facts, logits)
     hidden_other = swap_cores(hidden_sent)

time: 188 us -> 185 us (0.984)
  local copies, waits for them, and re-layouts: 5.86 us -> 3.54 us
    ppermute x1, starting transfers between devices: 1.92 us -> 5.3 us  [per_device(): near = lax.ppermute(first[:4], 'z', [(i, i ^ 1) for i in range(16)])]
    ppermute x1, starting transfers between devices: 12.9 us -> 10.2 us  [per_device(): lax.ppermute(first[4:], 'z', [(i, (i + 1 if i % 2 else i - 1) % 16) for i...]
  transfers between devices with their start and end apart: 9 -> 9, of which waited for: 5 -> 5; matrix products, arithmetic and copies ran while one was open for 2% -> 1% of each run, Pallas kernels for 9% -> 8%
where the time goes in v4:
time: 185 us; the launch traced here: 184 us
  starting transfers between devices  62.3 us (34%)
  waiting for transfers between devices  52.4 us (28%)
  blocking collectives  41.9 us (23%)
  Pallas kernels  23.2 us (13%)
  local copies, waits for them, and re-layouts  3.54 us (2%)
    all_to_all x4, waiting for transfers between devices, trade(): return lax.all_to_all(value, axes, 0, 0)  51.1 us
    all_to_all x3, blocking collectives, trade(): return lax.all_to_all(value, axes, 0, 0)  41.9 us
    all_to_all x4, starting transfers between devices, trade(): return lax.all_to_all(value, axes, 0, 0)  29.6 us
    ppermute x3, starting transfers between devices, swap_cores(): return lax.ppermute(value, 'core', [(0, 1), (1, 0)])  17.2 us
    ppermute x1, starting transfers between devices, per_device(): lax.ppermute(first[4:], 'z', [(i, (i + 1 if i % 2 else i - 1) % 16) for i...  10.2 us
    ppermute x1, starting transfers between devices, per_device(): near = lax.ppermute(first[:4], 'z', [(i, i ^ 1) for i in range(16)])  5.3 us
    pallas_call x1, Pallas kernels, half_call(): pl.pallas_call(half_kernel, in_specs=[SMEM, VMEM, ANY, ANY, ANY], out_spe...  4.91 us
  transfers between devices with their start and end apart: 9, of which 5 were waited for; matrix products, arithmetic and copies ran while one was open for 1% of the time, Pallas kernels for 8%

profile of v4, /device:TPU:1, one launch (start us, length us, event | category | flops | bytes accessed | tf_op | source)
XLA Modules:
  0.0 184.2 jit_solution(14463604446726450711)
XLA Ops:
  0.6 2.2 %spread.1 = bf16[8,128,768]{2,1,0:T(8,128)(2,1)} custom-call(bf16[128,2048]{1,0:T(8,128)(2,1)} %hidden.3), custom_call_target="tpu_custom_call" | custom-call | tf_op jit(solution)/shard_map/spread/pallas_call | solution.py:114
  2.9 7.6 %all-to-all-start = ((bf16[8,128,768]{2,1,0:T(8,128)(2,1)}), bf16[8,128,768]{2,1,0:T(8,128)(2,1)S(1)}, u32[]{:S(2)}, u32[]{:S(2)}) async-start(bf16[8,128,768]{2,1,0:T(8,128)(2,1)} %spread.1), calls=%async_computation | async-start | bytes 3145728 | tf_op jit(solution)/shard_map/all_to_all | solution.py:48
  11.4 3.1 %pack.1 = bf16[8,256,512]{2,1,0:T(8,128)(2,1)} custom-call(bf16[128,2048]{1,0:T(8,128)(2,1)S(1)} %copy-done, bf16[3968,128]{1,0:T(8,128)(2,1)S(1)} %copy-done.1, s32[1,128]{1,0:T(1,128)S(1)} %bitcast.11, s32[1,128]{1,0:T(1,128)S(1)} %bitcast.12, s32[1,128]{1,0:T(1,128)S(1)} %bitcast.13, f32[1,128]{1,0:T(1,128)S(1)} %bitcast.14), custom_call_target="tpu_custom_call" | custom-call | tf_op jit(solution)/shard_map/pack/pallas_call | solution.py:83
  14.5 15.6 %all-to-all-done.first = bf16[8,128,768]{2,1,0:T(8,128)(2,1)S(1)} async-done(((bf16[8,128,768]{2,1,0:T(8,128)(2,1)}), bf16[8,128,768]{2,1,0:T(8,128)(2,1)S(1)}, u32[]{:S(2)}, u32[]{:S(2)}) %all-to-all-start) | async-done | bytes 1572896 | tf_op jit(solution)/shard_map/all_to_all | solution.py:48
  30.1 4.9 %all-to-all-start.1 = ((bf16[8,256,512]{2,1,0:T(8,128)(2,1)}), bf16[8,256,512]{2,1,0:T(8,128)(2,1)}, u32[]{:S(2)}, u32[]{:S(2)}) async-start(bf16[8,256,512]{2,1,0:T(8,128)(2,1)} %pack.1), calls=%async_computation.1 | async-start | bytes 4194304 | tf_op jit(solution)/shard_map/all_to_all | solution.py:48
  36.3 5.3 %collective-permute-start = (bf16[4,128,768]{2,1,0:T(8,128)(2,1)}, bf16[4,128,768]{2,1,0:T(8,128)(2,1)S(1)}, u32[]{:S(2)}, u32[]{:S(2)}) collective-permute-start(bf16[4,128,768]{2,1,0:T(8,128)(2,1)} %get-tuple-element.53), channel_id=1, source_target_pairs={{0,2},{2,0},{4,6},{6,4},{8,10},{10,8},{12,14},{14,12},{16,18},{18,... | collective-permute-start | bytes 2359304 | tf_op jit(solution)/shard_map/ppermute | solution.py:560
  41.6 10.2 %collective-permute-start.1 = (bf16[4,128,768]{2,1,0:T(8,128)(2,1)}, bf16[4,128,768]{2,1,0:T(8,128)(2,1)}, u32[]{:S(2)}, u32[]{:S(2)}) collective-permute-start(bf16[4,128,768]{2,1,0:T(8,128)(2,1)} %get-tuple-element.52), channel_id=1, source_target_pairs={{0,30},{2,4},{4,2},{6,8},{8,6},{10,12},{12,10},{14,16},{16,14},{18... | collective-permute-start | bytes 2359304 | tf_op jit(solution)/shard_map/ppermute | solution.py:561
  51.8 8.0 %all-to-all-done.1.last = bf16[8,256,512]{2,1,0:T(8,128)(2,1)} async-done(((bf16[8,256,512]{2,1,0:T(8,128)(2,1)}), bf16[8,256,512]{2,1,0:T(8,128)(2,1)}, u32[]{:S(2)}, u32[]{:S(2)}) %all-to-all-start.1) | async-done | bytes 2097184 | tf_op jit(solution)/shard_map/all_to_all | solution.py:48
  59.7 6.7 %collective-permute-start.2 = (bf16[8,256,512]{2,1,0:T(8,128)(2,1)}, bf16[8,256,512]{2,1,0:T(8,128)(2,1)S(1)}, u32[]{:S(2)}, u32[]{:S(2)}) collective-permute-start(bf16[8,256,512]{2,1,0:T(8,128)(2,1)} %all-to-all-done.1.last), channel_id=1, source_target_pairs={{0,32},{32,0},{1,33},{33,1},{2,34},{34,2},{3,35},{35,3},{4,36},{36... | collective-permute-start | bytes 6291464 | tf_op jit(solution)/shard_map/ppermute | solution.py:44
  66.4 1.3 collective-permute-done.1.far
  67.8 4.9 %half.1 = (bf16[1024,2048]{1,0:T(8,128)(2,1)S(1)}, bf16[1024,2048]{1,0:T(8,128)(2,1)}, f32[496,1024]{1,0:T(8,128)S(1)}, bf16[8,16,128]{2,1,0:T(8,128)(2,1)S(1)}) custom-call(s32[3]{0:T(128)S(1)} %pad_add_fusion.place, bf16[8,128,768]{2,1,0:T(8,128)(2,1)S(1)} %all-to-all-done.first, bf16[4,128,768]{2,1,0:T(8,128)(2,1)S(1)} %collective-permute-done.near, ...), custom_call_target="tpu_custom_call" | custom-call | flops 99999997952 | bytes 100000000 | tf_op jit(solution)/shard_map/half/pallas_call | solution.py:190
  72.7 1.8 logits.1
  74.5 4.7 %collective-permute-start.3 = (bf16[1024,2048]{1,0:T(8,128)(2,1)}, bf16[1024,2048]{1,0:T(8,128)(2,1)}, u32[]{:S(2)}, u32[]{:S(2)}) collective-permute-start(bf16[1024,2048]{1,0:T(8,128)(2,1)} %get-tuple-element.40.hidden), channel_id=1, source_target_pairs={{0,32},{32,0},{1,33},{33,1},{2,34},{34,2},{3,35},{35,3},{4,36},{36... | collective-permute-start | bytes 12582920 | tf_op jit(solution)/shard_map/ppermute | solution.py:44
  79.2 13.6 %all_to_all.35.stats = f32[16,16,128]{2,1,0:T(8,128)S(1)} all-to-all(f32[16,16,128]{2,1,0:T(8,128)S(1)} %get-tuple-element.35), channel_id=1, replica_groups=mesh['y'=4,'xh'=2,'core'=2,'z'=16,'xl'=2] {'y','xh','xl'}, dimensions={0} | all-to-all | bytes 262144 | tf_op jit(solution)/shard_map/all_to_all | solution.py:48
  93.5 8.3 %all-to-all-start.3 = ((f32[16,16,128]{2,1,0:T(8,128)}), f32[16,16,128]{2,1,0:T(8,128)S(1)}, u32[]{:S(2)}, u32[]{:S(2)}) async-start(f32[16,16,128]{2,1,0:T(8,128)} %merge.1), calls=%async_computation.3 | async-start | bytes 262144 | tf_op jit(solution)/shard_map/all_to_all | solution.py:48
  102.8 11.1 %all-to-all-done.3.stats = f32[16,16,128]{2,1,0:T(8,128)S(1)} async-done(((f32[16,16,128]{2,1,0:T(8,128)}), f32[16,16,128]{2,1,0:T(8,128)S(1)}, u32[]{:S(2)}, u32[]{:S(2)}) %all-to-all-start.3) | async-done | bytes 131104 | tf_op jit(solution)/shard_map/all_to_all | solution.py:48
  113.9 2.7 %away.1 = (bf16[256,1024]{1,0:T(8,128)(2,1)S(1)}, f32[16,128]{1,0:T(8,128)S(1)}, bf16[1024,2048]{1,0:T(8,128)(2,1)S(1)}) custom-call(s32[3]{0:T(128)S(1)} %pad_add_fusion.place, f32[16,16,128]{2,1,0:T(8,128)S(1)} %all-to-all-done.3.stats, f32[504,1024]{1,0:T(8,128)S(1)} %get-tuple-element.36.logits, f32[8,1024]{1,0:T(8,128)S(1)} %get-tuple-element.39.tokens, ...), custom_call_target="tpu_custom_call" | custom-call | tf_op jit(solution)/shard_map/away/pallas_call | solution.py:371
  116.7 5.8 %collective-permute-start.4 = (bf16[256,1024]{1,0:T(8,128)(2,1)S(1)}, bf16[256,1024]{1,0:T(8,128)(2,1)S(1)}, u32[]{:S(2)}, u32[]{:S(2)}) collective-permute-start(bf16[256,1024]{1,0:T(8,128)(2,1)S(1)} %get-tuple-element.44), channel_id=1, source_target_pairs={{0,32},{32,0},{1,33},{33,1},{2,34},{34,2},{3,35},{35,3},{4,36},{36... | collective-permute-start | bytes 1572872 | tf_op jit(solution)/shard_map/ppermute | solution.py:44
  122.5 3.1 %own.1 = (f32[256,2048]{1,0:T(8,128)S(1)}, bf16[1024,2048]{1,0:T(8,128)(2,1)S(1)}) custom-call(s32[3]{0:T(128)S(1)} %pad_add_fusion.place, f32[16,128]{1,0:T(8,128)S(1)} %get-tuple-element.41.totals, f32[504,1024]{1,0:T(8,128)S(1)} %get-tuple-element.36.logits, f32[8,1024]{1,0:T(8,128)S(1)} %get-tuple-element.39.tokens, ...), custom_call_target="tpu_custom_call" | custom-call | tf_op jit(solution)/shard_map/own/pallas_call | solution.py:400
  125.6 2.4 %grad.1 = (f32[256,2048]{1,0:T(8,128)S(1)}, bf16[32,48,128]{2,1,0:T(8,128)(2,1)S(1)}) custom-call(s32[3]{0:T(128)S(1)} %pad_add_fusion.place, f32[256,2048]{1,0:T(8,128)S(1)} %get-tuple-element.43.partial, bf16[256,1024]{1,0:T(8,128)(2,1)S(1)} %collective-permute-done.4.score, bf16[1024,2048]{1,0:T(8,128)(2,1)S(1)} %get-tuple-element.45.hidden, ...), custom_call_target="tpu_custom_call" | custom-call | tf_op jit(solution)/shard_map/grad/pallas_call | solution.py:479
  128.0 12.5 %all_to_all.36.sums = bf16[32,48,128]{2,1,0:T(8,128)(2,1)S(1)} all-to-all(bf16[32,48,128]{2,1,0:T(8,128)(2,1)S(1)} %get-tuple-element.47), channel_id=1, replica_groups=mesh['y'=4,'xh'=2,'core'=2,'z'=16,'xl'=2] {'y','xh','core','xl'}, dimensions={0} | all-to-all | bytes 786432 | tf_op jit(solution)/shard_map/all_to_all | solution.py:48
  140.6 15.8 %all_to_all.37.sums = bf16[16,48,128]{2,1,0:T(8,128)(2,1)S(1)} all-to-all(bf16[16,48,128]{2,1,0:T(8,128)(2,1)S(1)} %add.32), channel_id=1, replica_groups=mesh['y'=4,'xh'=2,'core'=2,'z'=16,'xl'=2] {'z'}, dimensions={0} | all-to-all | bytes 393216 | tf_op jit(solution)/shard_map/all_to_all | solution.py:48
  157.6 8.8 %all-to-all-start.6 = ((bf16[16,248,128]{2,1,0:T(8,128)(2,1)}), bf16[16,248,128]{2,1,0:T(8,128)(2,1)S(1)}, u32[]{:S(2)}, u32[]{:S(2)}) async-start(bf16[16,248,128]{2,1,0:T(8,128)(2,1)} %get-tuple-element.50), calls=%async_computation.6 | async-start | bytes 2031616 | tf_op jit(solution)/shard_map/all_to_all | solution.py:48
  166.9 16.3 %all-to-all-done.6 = bf16[16,248,128]{2,1,0:T(8,128)(2,1)S(1)} async-done(((bf16[16,248,128]{2,1,0:T(8,128)(2,1)}), bf16[16,248,128]{2,1,0:T(8,128)(2,1)S(1)}, u32[]{:S(2)}, u32[]{:S(2)}) %all-to-all-start.6) | async-done | bytes 1015840 | tf_op jit(solution)/shard_map/all_to_all | solution.py:48
  (26 shorter events, 6.6 us)
Async XLA Ops:
  2.8 8.6 %copy-start = (bf16[128,2048]{1,0:T(8,128)(2,1)S(1)}, bf16[128,2048]{1,0:T(8,128)(2,1)}, u32[]{:S(2)}) copy-start(bf16[128,2048]{1,0:T(8,128)(2,1)} %hidden.3) | copy-start | bytes 1572868
  2.8 8.5 %copy-start.1 = (bf16[3968,128]{1,0:T(8,128)(2,1)S(1)}, bf16[3968,128]{1,0:T(8,128)(2,1)}, u32[]{:S(2)}) copy-start(bf16[3968,128]{1,0:T(8,128)(2,1)} %head.1) | copy-start | bytes 3047428
  2.8 8.5 %copy-start.2 = (s32[128]{0:T(128)S(1)}, s32[128]{0:T(128)}, u32[]{:S(2)}) copy-start(s32[128]{0:T(128)} %param.9) | copy-start | bytes 1540
  2.8 8.5 %copy-start.3 = (s32[128]{0:T(128)S(1)}, s32[128]{0:T(128)}, u32[]{:S(2)}) copy-start(s32[128]{0:T(128)} %param.10) | copy-start | bytes 1540
  2.8 8.5 %copy-start.4 = (s32[128]{0:T(128)S(1)}, s32[128]{0:T(128)}, u32[]{:S(2)}) copy-start(s32[128]{0:T(128)} %param.11) | copy-start | bytes 1540
  2.9 8.5 %copy-start.5 = (f32[128]{0:T(128)S(1)}, f32[128]{0:T(128)}, u32[]{:S(2)}) copy-start(f32[128]{0:T(128)} %param.13) | copy-start | bytes 1540
  2.9 27.3 %all-to-all-start = ((bf16[8,128,768]{2,1,0:T(8,128)(2,1)}), bf16[8,128,768]{2,1,0:T(8,128)(2,1)S(1)}, u32[]{:S(2)}, u32[]{:S(2)}) async-start(bf16[8,128,768]{2,1,0:T(8,128)(2,1)} %spread.1), calls=%async_computation | async-start | bytes 3145728 | tf_op jit(solution)/shard_map/all_to_all | solution.py:48
  30.1 29.6 %all-to-all-start.1 = ((bf16[8,256,512]{2,1,0:T(8,128)(2,1)}), bf16[8,256,512]{2,1,0:T(8,128)(2,1)}, u32[]{:S(2)}, u32[]{:S(2)}) async-start(bf16[8,256,512]{2,1,0:T(8,128)(2,1)} %pack.1), calls=%async_computation.1 | async-start | bytes 4194304 | tf_op jit(solution)/shard_map/all_to_all | solution.py:48
  36.3 30.1 %collective-permute-start = (bf16[4,128,768]{2,1,0:T(8,128)(2,1)}, bf16[4,128,768]{2,1,0:T(8,128)(2,1)S(1)}, u32[]{:S(2)}, u32[]{:S(2)}) collective-permute-start(bf16[4,128,768]{2,1,0:T(8,128)(2,1)} %get-tuple-element.53), channel_id=1, source_target_pairs={{0,2},{2,0},{4,6},{6,4},{8,10},{10,8},{12,14},{14,12},{16,18},{18,... | collective-permute-start | bytes 2359304 | tf_op jit(solution)/shard_map/ppermute | solution.py:560
  41.6 26.2 %collective-permute-start.1 = (bf16[4,128,768]{2,1,0:T(8,128)(2,1)}, bf16[4,128,768]{2,1,0:T(8,128)(2,1)}, u32[]{:S(2)}, u32[]{:S(2)}) collective-permute-start(bf16[4,128,768]{2,1,0:T(8,128)(2,1)} %get-tuple-element.52), channel_id=1, source_target_pairs={{0,30},{2,4},{4,2},{6,8},{8,6},{10,12},{12,10},{14,16},{16,14},{18... | collective-permute-start | bytes 2359304 | tf_op jit(solution)/shard_map/ppermute | solution.py:561
  59.7 12.9 %collective-permute-start.2 = (bf16[8,256,512]{2,1,0:T(8,128)(2,1)}, bf16[8,256,512]{2,1,0:T(8,128)(2,1)S(1)}, u32[]{:S(2)}, u32[]{:S(2)}) collective-permute-start(bf16[8,256,512]{2,1,0:T(8,128)(2,1)} %all-to-all-done.1.last), channel_id=1, source_target_pairs={{0,32},{32,0},{1,33},{33,1},{2,34},{34,2},{3,35},{35,3},{4,36},{36... | collective-permute-start | bytes 6291464 | tf_op jit(solution)/shard_map/ppermute | solution.py:44
  74.5 48.0 %collective-permute-start.3 = (bf16[1024,2048]{1,0:T(8,128)(2,1)}, bf16[1024,2048]{1,0:T(8,128)(2,1)}, u32[]{:S(2)}, u32[]{:S(2)}) collective-permute-start(bf16[1024,2048]{1,0:T(8,128)(2,1)} %get-tuple-element.40.hidden), channel_id=1, source_target_pairs={{0,32},{32,0},{1,33},{33,1},{2,34},{34,2},{3,35},{35,3},{4,36},{36... | collective-permute-start | bytes 12582920 | tf_op jit(solution)/shard_map/ppermute | solution.py:44
  93.5 20.4 %all-to-all-start.3 = ((f32[16,16,128]{2,1,0:T(8,128)}), f32[16,16,128]{2,1,0:T(8,128)S(1)}, u32[]{:S(2)}, u32[]{:S(2)}) async-start(f32[16,16,128]{2,1,0:T(8,128)} %merge.1), calls=%async_computation.3 | async-start | bytes 262144 | tf_op jit(solution)/shard_map/all_to_all | solution.py:48
  116.7 8.9 %collective-permute-start.4 = (bf16[256,1024]{1,0:T(8,128)(2,1)S(1)}, bf16[256,1024]{1,0:T(8,128)(2,1)S(1)}, u32[]{:S(2)}, u32[]{:S(2)}) collective-permute-start(bf16[256,1024]{1,0:T(8,128)(2,1)S(1)} %get-tuple-element.44), channel_id=1, source_target_pairs={{0,32},{32,0},{1,33},{33,1},{2,34},{34,2},{3,35},{35,3},{4,36},{36... | collective-permute-start | bytes 1572872 | tf_op jit(solution)/shard_map/ppermute | solution.py:44
  157.6 25.7 %all-to-all-start.6 = ((bf16[16,248,128]{2,1,0:T(8,128)(2,1)}), bf16[16,248,128]{2,1,0:T(8,128)(2,1)S(1)}, u32[]{:S(2)}, u32[]{:S(2)}) async-start(bf16[16,248,128]{2,1,0:T(8,128)(2,1)} %get-tuple-element.50), calls=%async_computation.6 | async-start | bytes 2031616 | tf_op jit(solution)/shard_map/all_to_all | solution.py:48

commit v5 on v4

--- a/solution.py
+++ b/solution.py
@@ -27,6 +27,7 @@
 PAD = 256
 TOKENS = 1024
 SEGS = 64
+SUMS = 40
 STEP = 6 * 128
 LAST = 4 * 128
 f32 = jnp.float32
@@ -465,14 +466,14 @@
             * (1.0 / 256.0)
             - tokens[2:3, lanes]
         )
-    table[32:48, :] = jnp.zeros((16, 128), f32)
+    table[32:SUMS, :] = jnp.zeros((SUMS - 32, 128), f32)
     for i, line in enumerate(split_rows(row_total) + split_rows(loss)):
         table[32 + i : 33 + i, :] = line
     for i, j in enumerate(places):
         part = grad[:, 128 * i : 128 * i + 128] * scale
         scaled[:, pl.ds(pl.multiple_of(j * 128, 128), 128)] = part
         table[pl.ds(16 + j, 1), :] = jnp.sum(part * part, axis=0, keepdims=True)
-    sums[...] = jnp.broadcast_to(table[...].astype(bf16)[None], (32, 48, 128))
+    sums[...] = jnp.broadcast_to(table[...].astype(bf16)[None], (32, SUMS, 128))
 
 
 def grad_call(place, partial, score, hidden, state, totals, tokens):
@@ -482,11 +483,11 @@
         out_specs=[VMEM] * 2,
         out_shape=[
             jax.ShapeDtypeStruct((PAD, D), f32),
-            jax.ShapeDtypeStruct((32, 48, 128), bf16),
+            jax.ShapeDtypeStruct((32, SUMS, 128), bf16),
         ],
         scratch_shapes=[
             pltpu.VMEM((PAD, D), f32),
-            pltpu.VMEM((48, 128), f32),
+            pltpu.VMEM((SUMS, 128), f32),
         ],
         compiler_params=params,
         name="grad",
@@ -496,12 +497,10 @@
 def add_kernel(sums, out):
     total = jnp.sum(sums[...].astype(f32), axis=0)
     lines = split_rows(join_rows(total, 32)) + split_rows(join_rows(total, 35))
-    row = lax.broadcasted_iota(jnp.int32, (16, 128), 0)
-    tail = jnp.zeros((16, 128), f32)
+    row = lax.broadcasted_iota(jnp.int32, (SUMS, 128), 0)
     for i, line in enumerate(lines):
-        tail = jnp.where(row == i, line, tail)
-    out[:, :32, :] = jnp.broadcast_to(total[:32].astype(bf16)[None], (16, 32, 128))
-    out[:, 32:, :] = jnp.broadcast_to(tail.astype(bf16)[None], (16, 16, 128))
+        total = jnp.where(row == 32 + i, line, total)
+    out[...] = jnp.broadcast_to(total.astype(bf16)[None], (16, SUMS, 128))
 
 
 def add_call(sums):
@@ -509,7 +508,7 @@
         add_kernel,
         in_specs=[VMEM],
         out_specs=VMEM,
-        out_shape=jax.ShapeDtypeStruct((16, 48, 128), bf16),
+        out_shape=jax.ShapeDtypeStruct((16, SUMS, 128), bf16),
         compiler_params=params,
         name="add",
     )(sums)
@@ -553,7 +552,8 @@
     own_state = jnp.concatenate([own_state, jnp.ones((PAD - OWN,), f32)]).reshape(1, PAD)
     place, own_state, targets = lax.optimization_barrier((place, own_state, targets))
 
-    first = trade(spread(hidden), CHIPS)
+    groups = [[4 * y + 2 * xh + (xh ^ k) for y in range(4) for xh in range(2)] for k in range(2)]
+    first = lax.all_to_all(spread(hidden), PLANE, 0, 0, axis_index_groups=groups)
     last = pack(hidden, head_weight, targets, segments, loss_mask, column_state)
     last, first = lax.optimization_barrier((last, first))
     last = trade(last, CHIPS)

time: 185 us -> 183 us (0.989)
    all_to_all x4 -> x3, waiting for transfers between devices: 51.1 us -> 36 us  [trade(): return lax.all_to_all(value, axes, 0, 0)]
    all_to_all x0 -> x1, waiting for transfers between devices: none -> 15.1 us  [per_device(): lax.all_to_all(spread(hidden), PLANE, 0, 0, axis_index_groups=groups)]
    all_to_all x4 -> x3, starting transfers between devices: 29.6 us -> 21.6 us  [trade(): return lax.all_to_all(value, axes, 0, 0)]
    all_to_all x0 -> x1, starting transfers between devices: none -> 7.36 us  [per_device(): lax.all_to_all(spread(hidden), PLANE, 0, 0, axis_index_groups=groups)]
  transfers between devices with their start and end apart: 9 -> 9, of which waited for: 5 -> 5; matrix products, arithmetic and copies ran while one was open for 1% -> 1% of each run, Pallas kernels for 8% -> 9%
where the time goes in v5:
time: 183 us; the launch traced here: 182 us
  starting transfers between devices  61.1 us (33%)
  waiting for transfers between devices  52.2 us (29%)
  blocking collectives  41.2 us (23%)
  Pallas kernels  23.2 us (13%)
  local copies, waits for them, and re-layouts  3.54 us (2%)
    all_to_all x3, blocking collectives, trade(): return lax.all_to_all(value, axes, 0, 0)  41.2 us
    all_to_all x3, waiting for transfers between devices, trade(): return lax.all_to_all(value, axes, 0, 0)  36 us
    all_to_all x3, starting transfers between devices, trade(): return lax.all_to_all(value, axes, 0, 0)  21.6 us
    ppermute x3, starting transfers between devices, swap_cores(): return lax.ppermute(value, 'core', [(0, 1), (1, 0)])  16.8 us
    all_to_all x1, waiting for transfers between devices, per_device(): lax.all_to_all(spread(hidden), PLANE, 0, 0, axis_index_groups=groups)  15.1 us
    ppermute x1, starting transfers between devices, per_device(): lax.ppermute(first[4:], 'z', [(i, (i + 1 if i % 2 else i - 1) % 16) for i...  10.2 us
    all_to_all x1, starting transfers between devices, per_device(): lax.all_to_all(spread(hidden), PLANE, 0, 0, axis_index_groups=groups)  7.36 us
    ppermute x1, starting transfers between devices, per_device(): near = lax.ppermute(first[:4], 'z', [(i, i ^ 1) for i in range(16)])  5.06 us
  transfers between devices with their start and end apart: 9, of which 5 were waited for; matrix products, arithmetic and copies ran while one was open for 1% of the time, Pallas kernels for 9%

profile of v5, /device:TPU:1, one launch (start us, length us, event | category | flops | bytes accessed | tf_op | source)
XLA Modules:
  0.0 182.1 jit_solution(7654157821575228812)
XLA Ops:
  0.6 2.2 %spread.1 = bf16[8,128,768]{2,1,0:T(8,128)(2,1)} custom-call(bf16[128,2048]{1,0:T(8,128)(2,1)} %hidden.3), custom_call_target="tpu_custom_call" | custom-call | tf_op jit(solution)/shard_map/spread/pallas_call | solution.py:115
  2.9 7.4 %all-to-all-start = ((bf16[8,128,768]{2,1,0:T(8,128)(2,1)}), bf16[8,128,768]{2,1,0:T(8,128)(2,1)S(1)}, u32[]{:S(2)}, u32[]{:S(2)}) async-start(bf16[8,128,768]{2,1,0:T(8,128)(2,1)} %spread.1), calls=%async_computation | async-start | bytes 3145728 | tf_op jit(solution)/shard_map/all_to_all | solution.py:556
  11.1 3.1 %pack.1 = bf16[8,256,512]{2,1,0:T(8,128)(2,1)} custom-call(bf16[128,2048]{1,0:T(8,128)(2,1)S(1)} %copy-done, bf16[3968,128]{1,0:T(8,128)(2,1)S(1)} %copy-done.1, s32[1,128]{1,0:T(1,128)S(1)} %bitcast.11, s32[1,128]{1,0:T(1,128)S(1)} %bitcast.12, s32[1,128]{1,0:T(1,128)S(1)} %bitcast.13, f32[1,128]{1,0:T(1,128)S(1)} %bitcast.14), custom_call_target="tpu_custom_call" | custom-call | tf_op jit(solution)/shard_map/pack/pallas_call | solution.py:84
  14.2 15.1 %all-to-all-done.first = bf16[8,128,768]{2,1,0:T(8,128)(2,1)S(1)} async-done(((bf16[8,128,768]{2,1,0:T(8,128)(2,1)}), bf16[8,128,768]{2,1,0:T(8,128)(2,1)S(1)}, u32[]{:S(2)}, u32[]{:S(2)}) %all-to-all-start) | async-done | bytes 1572896 | tf_op jit(solution)/shard_map/all_to_all | solution.py:556
  29.3 5.4 %all-to-all-start.1 = ((bf16[8,256,512]{2,1,0:T(8,128)(2,1)}), bf16[8,256,512]{2,1,0:T(8,128)(2,1)}, u32[]{:S(2)}, u32[]{:S(2)}) async-start(bf16[8,256,512]{2,1,0:T(8,128)(2,1)} %pack.1), calls=%async_computation.1 | async-start | bytes 4194304 | tf_op jit(solution)/shard_map/all_to_all | solution.py:49
  34.7 1.3 fusion
  36.0 5.1 %collective-permute-start = (bf16[4,128,768]{2,1,0:T(8,128)(2,1)}, bf16[4,128,768]{2,1,0:T(8,128)(2,1)S(1)}, u32[]{:S(2)}, u32[]{:S(2)}) collective-permute-start(bf16[4,128,768]{2,1,0:T(8,128)(2,1)} %get-tuple-element.53), channel_id=1, source_target_pairs={{0,2},{2,0},{4,6},{6,4},{8,10},{10,8},{12,14},{14,12},{16,18},{18,... | collective-permute-start | bytes 2359304 | tf_op jit(solution)/shard_map/ppermute | solution.py:560
  41.1 10.2 %collective-permute-start.1 = (bf16[4,128,768]{2,1,0:T(8,128)(2,1)}, bf16[4,128,768]{2,1,0:T(8,128)(2,1)}, u32[]{:S(2)}, u32[]{:S(2)}) collective-permute-start(bf16[4,128,768]{2,1,0:T(8,128)(2,1)} %get-tuple-element.52), channel_id=1, source_target_pairs={{0,30},{2,4},{4,2},{6,8},{8,6},{10,12},{12,10},{14,16},{16,14},{18... | collective-permute-start | bytes 2359304 | tf_op jit(solution)/shard_map/ppermute | solution.py:561
  51.3 8.5 %all-to-all-done.1.last = bf16[8,256,512]{2,1,0:T(8,128)(2,1)} async-done(((bf16[8,256,512]{2,1,0:T(8,128)(2,1)}), bf16[8,256,512]{2,1,0:T(8,128)(2,1)}, u32[]{:S(2)}, u32[]{:S(2)}) %all-to-all-start.1) | async-done | bytes 2097184 | tf_op jit(solution)/shard_map/all_to_all | solution.py:49
  59.7 6.4 %collective-permute-start.2 = (bf16[8,256,512]{2,1,0:T(8,128)(2,1)}, bf16[8,256,512]{2,1,0:T(8,128)(2,1)S(1)}, u32[]{:S(2)}, u32[]{:S(2)}) collective-permute-start(bf16[8,256,512]{2,1,0:T(8,128)(2,1)} %all-to-all-done.1.last), channel_id=1, source_target_pairs={{0,32},{32,0},{1,33},{33,1},{2,34},{34,2},{3,35},{35,3},{4,36},{36... | collective-permute-start | bytes 6291464 | tf_op jit(solution)/shard_map/ppermute | solution.py:45
  67.3 4.9 %half.1 = (bf16[1024,2048]{1,0:T(8,128)(2,1)S(1)}, bf16[1024,2048]{1,0:T(8,128)(2,1)}, f32[496,1024]{1,0:T(8,128)S(1)}, bf16[8,16,128]{2,1,0:T(8,128)(2,1)S(1)}) custom-call(s32[3]{0:T(128)S(1)} %pad_add_fusion.place, bf16[8,128,768]{2,1,0:T(8,128)(2,1)S(1)} %all-to-all-done.first, bf16[4,128,768]{2,1,0:T(8,128)(2,1)S(1)} %collective-permute-done.near, ...), custom_call_target="tpu_custom_call" | custom-call | flops 99999997952 | bytes 100000000 | tf_op jit(solution)/shard_map/half/pallas_call | solution.py:191
  72.2 1.8 logits.1
  74.0 4.7 %collective-permute-start.3 = (bf16[1024,2048]{1,0:T(8,128)(2,1)}, bf16[1024,2048]{1,0:T(8,128)(2,1)}, u32[]{:S(2)}, u32[]{:S(2)}) collective-permute-start(bf16[1024,2048]{1,0:T(8,128)(2,1)} %get-tuple-element.40.hidden), channel_id=1, source_target_pairs={{0,32},{32,0},{1,33},{33,1},{2,34},{34,2},{3,35},{35,3},{4,36},{36... | collective-permute-start | bytes 12582920 | tf_op jit(solution)/shard_map/ppermute | solution.py:45
  78.7 13.6 %all_to_all.35.stats = f32[16,16,128]{2,1,0:T(8,128)S(1)} all-to-all(f32[16,16,128]{2,1,0:T(8,128)S(1)} %get-tuple-element.35), channel_id=1, replica_groups=mesh['y'=4,'xh'=2,'core'=2,'z'=16,'xl'=2] {'y','xh','xl'}, dimensions={0} | all-to-all | bytes 262144 | tf_op jit(solution)/shard_map/all_to_all | solution.py:49
  93.0 8.3 %all-to-all-start.3 = ((f32[16,16,128]{2,1,0:T(8,128)}), f32[16,16,128]{2,1,0:T(8,128)S(1)}, u32[]{:S(2)}, u32[]{:S(2)}) async-start(f32[16,16,128]{2,1,0:T(8,128)} %merge.1), calls=%async_computation.3 | async-start | bytes 262144 | tf_op jit(solution)/shard_map/all_to_all | solution.py:49
  102.3 11.1 %all-to-all-done.3.stats = f32[16,16,128]{2,1,0:T(8,128)S(1)} async-done(((f32[16,16,128]{2,1,0:T(8,128)}), f32[16,16,128]{2,1,0:T(8,128)S(1)}, u32[]{:S(2)}, u32[]{:S(2)}) %all-to-all-start.3) | async-done | bytes 131104 | tf_op jit(solution)/shard_map/all_to_all | solution.py:49
  113.4 2.7 %away.1 = (bf16[256,1024]{1,0:T(8,128)(2,1)S(1)}, f32[16,128]{1,0:T(8,128)S(1)}, bf16[1024,2048]{1,0:T(8,128)(2,1)S(1)}) custom-call(s32[3]{0:T(128)S(1)} %pad_add_fusion.place, f32[16,16,128]{2,1,0:T(8,128)S(1)} %all-to-all-done.3.stats, f32[504,1024]{1,0:T(8,128)S(1)} %get-tuple-element.36.logits, f32[8,1024]{1,0:T(8,128)S(1)} %get-tuple-element.39.tokens, ...), custom_call_target="tpu_custom_call" | custom-call | tf_op jit(solution)/shard_map/away/pallas_call | solution.py:372
  116.2 5.8 %collective-permute-start.4 = (bf16[256,1024]{1,0:T(8,128)(2,1)S(1)}, bf16[256,1024]{1,0:T(8,128)(2,1)S(1)}, u32[]{:S(2)}, u32[]{:S(2)}) collective-permute-start(bf16[256,1024]{1,0:T(8,128)(2,1)S(1)} %get-tuple-element.44), channel_id=1, source_target_pairs={{0,32},{32,0},{1,33},{33,1},{2,34},{34,2},{3,35},{35,3},{4,36},{36... | collective-permute-start | bytes 1572872 | tf_op jit(solution)/shard_map/ppermute | solution.py:45
  121.9 3.1 %own.1 = (f32[256,2048]{1,0:T(8,128)S(1)}, bf16[1024,2048]{1,0:T(8,128)(2,1)S(1)}) custom-call(s32[3]{0:T(128)S(1)} %pad_add_fusion.place, f32[16,128]{1,0:T(8,128)S(1)} %get-tuple-element.41.totals, f32[504,1024]{1,0:T(8,128)S(1)} %get-tuple-element.36.logits, f32[8,1024]{1,0:T(8,128)S(1)} %get-tuple-element.39.tokens, ...), custom_call_target="tpu_custom_call" | custom-call | tf_op jit(solution)/shard_map/own/pallas_call | solution.py:401
  125.0 2.4 %grad.1 = (f32[256,2048]{1,0:T(8,128)S(1)}, bf16[32,40,128]{2,1,0:T(8,128)(2,1)S(1)}) custom-call(s32[3]{0:T(128)S(1)} %pad_add_fusion.place, f32[256,2048]{1,0:T(8,128)S(1)} %get-tuple-element.43.partial, bf16[256,1024]{1,0:T(8,128)(2,1)S(1)} %collective-permute-done.4.score, bf16[1024,2048]{1,0:T(8,128)(2,1)S(1)} %get-tuple-element.45.hidden, ...), custom_call_target="tpu_custom_call" | custom-call | tf_op jit(solution)/shard_map/grad/pallas_call | solution.py:480
  127.5 12.1 %all_to_all.36.sums = bf16[32,40,128]{2,1,0:T(8,128)(2,1)S(1)} all-to-all(bf16[32,40,128]{2,1,0:T(8,128)(2,1)S(1)} %get-tuple-element.47), channel_id=1, replica_groups=mesh['y'=4,'xh'=2,'core'=2,'z'=16,'xl'=2] {'y','xh','core','xl'}, dimensions={0} | all-to-all | bytes 655360 | tf_op jit(solution)/shard_map/all_to_all | solution.py:49
  139.6 15.6 %all_to_all.37.sums = bf16[16,40,128]{2,1,0:T(8,128)(2,1)S(1)} all-to-all(bf16[16,40,128]{2,1,0:T(8,128)(2,1)S(1)} %add.32), channel_id=1, replica_groups=mesh['y'=4,'xh'=2,'core'=2,'z'=16,'xl'=2] {'z'}, dimensions={0} | all-to-all | bytes 327680 | tf_op jit(solution)/shard_map/all_to_all | solution.py:49
  156.4 7.9 %all-to-all-start.6 = ((bf16[16,248,128]{2,1,0:T(8,128)(2,1)}), bf16[16,248,128]{2,1,0:T(8,128)(2,1)S(1)}, u32[]{:S(2)}, u32[]{:S(2)}) async-start(bf16[16,248,128]{2,1,0:T(8,128)(2,1)} %get-tuple-element.50), calls=%async_computation.6 | async-start | bytes 2031616 | tf_op jit(solution)/shard_map/all_to_all | solution.py:49
  164.8 16.3 %all-to-all-done.6 = bf16[16,248,128]{2,1,0:T(8,128)(2,1)S(1)} async-done(((bf16[16,248,128]{2,1,0:T(8,128)(2,1)}), bf16[16,248,128]{2,1,0:T(8,128)(2,1)S(1)}, u32[]{:S(2)}, u32[]{:S(2)}) %all-to-all-start.6) | async-done | bytes 1015840 | tf_op jit(solution)/shard_map/all_to_all | solution.py:49
  (26 shorter events, 6.5 us)
Async XLA Ops:
  2.8 8.3 %copy-start = (bf16[128,2048]{1,0:T(8,128)(2,1)S(1)}, bf16[128,2048]{1,0:T(8,128)(2,1)}, u32[]{:S(2)}) copy-start(bf16[128,2048]{1,0:T(8,128)(2,1)} %hidden.3) | copy-start | bytes 1572868
  2.8 8.3 %copy-start.1 = (bf16[3968,128]{1,0:T(8,128)(2,1)S(1)}, bf16[3968,128]{1,0:T(8,128)(2,1)}, u32[]{:S(2)}) copy-start(bf16[3968,128]{1,0:T(8,128)(2,1)} %head.1) | copy-start | bytes 3047428
  2.8 8.3 %copy-start.2 = (s32[128]{0:T(128)S(1)}, s32[128]{0:T(128)}, u32[]{:S(2)}) copy-start(s32[128]{0:T(128)} %param.9) | copy-start | bytes 1540
  2.8 8.3 %copy-start.3 = (s32[128]{0:T(128)S(1)}, s32[128]{0:T(128)}, u32[]{:S(2)}) copy-start(s32[128]{0:T(128)} %param.10) | copy-start | bytes 1540
  2.8 8.3 %copy-start.4 = (s32[128]{0:T(128)S(1)}, s32[128]{0:T(128)}, u32[]{:S(2)}) copy-start(s32[128]{0:T(128)} %param.11) | copy-start | bytes 1540
  2.9 8.3 %copy-start.5 = (f32[128]{0:T(128)S(1)}, f32[128]{0:T(128)}, u32[]{:S(2)}) copy-start(f32[128]{0:T(128)} %param.13) | copy-start | bytes 1540
  2.9 26.4 %all-to-all-start = ((bf16[8,128,768]{2,1,0:T(8,128)(2,1)}), bf16[8,128,768]{2,1,0:T(8,128)(2,1)S(1)}, u32[]{:S(2)}, u32[]{:S(2)}) async-start(bf16[8,128,768]{2,1,0:T(8,128)(2,1)} %spread.1), calls=%async_computation | async-start | bytes 3145728 | tf_op jit(solution)/shard_map/all_to_all | solution.py:556
  29.3 30.4 %all-to-all-start.1 = ((bf16[8,256,512]{2,1,0:T(8,128)(2,1)}), bf16[8,256,512]{2,1,0:T(8,128)(2,1)}, u32[]{:S(2)}, u32[]{:S(2)}) async-start(bf16[8,256,512]{2,1,0:T(8,128)(2,1)} %pack.1), calls=%async_computation.1 | async-start | bytes 4194304 | tf_op jit(solution)/shard_map/all_to_all | solution.py:49
  36.0 30.1 %collective-permute-start = (bf16[4,128,768]{2,1,0:T(8,128)(2,1)}, bf16[4,128,768]{2,1,0:T(8,128)(2,1)S(1)}, u32[]{:S(2)}, u32[]{:S(2)}) collective-permute-start(bf16[4,128,768]{2,1,0:T(8,128)(2,1)} %get-tuple-element.53), channel_id=1, source_target_pairs={{0,2},{2,0},{4,6},{6,4},{8,10},{10,8},{12,14},{14,12},{16,18},{18,... | collective-permute-start | bytes 2359304 | tf_op jit(solution)/shard_map/ppermute | solution.py:560
  41.1 26.2 %collective-permute-start.1 = (bf16[4,128,768]{2,1,0:T(8,128)(2,1)}, bf16[4,128,768]{2,1,0:T(8,128)(2,1)}, u32[]{:S(2)}, u32[]{:S(2)}) collective-permute-start(bf16[4,128,768]{2,1,0:T(8,128)(2,1)} %get-tuple-element.52), channel_id=1, source_target_pairs={{0,30},{2,4},{4,2},{6,8},{8,6},{10,12},{12,10},{14,16},{16,14},{18... | collective-permute-start | bytes 2359304 | tf_op jit(solution)/shard_map/ppermute | solution.py:561
  59.7 12.5 %collective-permute-start.2 = (bf16[8,256,512]{2,1,0:T(8,128)(2,1)}, bf16[8,256,512]{2,1,0:T(8,128)(2,1)S(1)}, u32[]{:S(2)}, u32[]{:S(2)}) collective-permute-start(bf16[8,256,512]{2,1,0:T(8,128)(2,1)} %all-to-all-done.1.last), channel_id=1, source_target_pairs={{0,32},{32,0},{1,33},{33,1},{2,34},{34,2},{3,35},{35,3},{4,36},{36... | collective-permute-start | bytes 6291464 | tf_op jit(solution)/shard_map/ppermute | solution.py:45
  74.0 47.9 %collective-permute-start.3 = (bf16[1024,2048]{1,0:T(8,128)(2,1)}, bf16[1024,2048]{1,0:T(8,128)(2,1)}, u32[]{:S(2)}, u32[]{:S(2)}) collective-permute-start(bf16[1024,2048]{1,0:T(8,128)(2,1)} %get-tuple-element.40.hidden), channel_id=1, source_target_pairs={{0,32},{32,0},{1,33},{33,1},{2,34},{34,2},{3,35},{35,3},{4,36},{36... | collective-permute-start | bytes 12582920 | tf_op jit(solution)/shard_map/ppermute | solution.py:45
  93.0 20.4 %all-to-all-start.3 = ((f32[16,16,128]{2,1,0:T(8,128)}), f32[16,16,128]{2,1,0:T(8,128)S(1)}, u32[]{:S(2)}, u32[]{:S(2)}) async-start(f32[16,16,128]{2,1,0:T(8,128)} %merge.1), calls=%async_computation.3 | async-start | bytes 262144 | tf_op jit(solution)/shard_map/all_to_all | solution.py:49
  116.2 8.9 %collective-permute-start.4 = (bf16[256,1024]{1,0:T(8,128)(2,1)S(1)}, bf16[256,1024]{1,0:T(8,128)(2,1)S(1)}, u32[]{:S(2)}, u32[]{:S(2)}) collective-permute-start(bf16[256,1024]{1,0:T(8,128)(2,1)S(1)} %get-tuple-element.44), channel_id=1, source_target_pairs={{0,32},{32,0},{1,33},{33,1},{2,34},{34,2},{3,35},{35,3},{4,36},{36... | collective-permute-start | bytes 1572872 | tf_op jit(solution)/shard_map/ppermute | solution.py:45
  156.4 24.7 %all-to-all-start.6 = ((bf16[16,248,128]{2,1,0:T(8,128)(2,1)}), bf16[16,248,128]{2,1,0:T(8,128)(2,1)S(1)}, u32[]{:S(2)}, u32[]{:S(2)}) async-start(bf16[16,248,128]{2,1,0:T(8,128)(2,1)} %get-tuple-element.50), calls=%async_computation.6 | async-start | bytes 2031616 | tf_op jit(solution)/shard_map/all_to_all | solution.py:49

commit v6 on v5

--- a/solution.py
+++ b/solution.py
@@ -139,18 +139,17 @@
 ):
     core = place[0]
     odd = place[2]
-    rest_copies = [
-        pltpu.make_async_copy(last.at[q], rest.at[q], sems.at[q]) for q in range(PEERS)
-    ]
-    beside_copies = [
-        pltpu.make_async_copy(
-            (near if q < 4 else far).at[q % 4], beside.at[q], sems.at[PEERS + q]
-        )
-        for q in range(PEERS)
-    ]
-    for q in range(PEERS):
-        rest_copies[q].start()
-        beside_copies[q].start()
+    pairs = PEERS // 2
+    rest_copies, beside_copies = [], []
+    for i in range(pairs):
+        two = slice(2 * i, 2 * i + 2)
+        copy = pltpu.make_async_copy(last.at[two], rest.at[two], sems.at[i])
+        copy.start()
+        rest_copies.append(copy)
+        source = (near if i < 2 else far).at[slice(2 * (i % 2), 2 * (i % 2) + 2)]
+        copy = pltpu.make_async_copy(source, beside.at[two], sems.at[pairs + i])
+        copy.start()
+        beside_copies.append(copy)
 
     def fill(source, q, start, count):
         for i in range(count):
@@ -162,15 +161,17 @@
     sent_copies = []
     for q in range(PEERS):
         fill(first, q, 3 * odd, 6)
-        rest_copies[q].wait()
+        if q % 2 == 0:
+            rest_copies[q // 2].wait()
         fill(rest, q, 6, 4)
         gather_weight(rest, q, TOK, weight)
-        beside_copies[q].wait()
+        if q % 2 == 0:
+            beside_copies[q // 2].wait()
         fill(beside, q, 3 - 3 * odd, 6)
         if q % 2 == 1:
             tokens = slice((q - 1) * TOK, (q + 1) * TOK)
             copy = pltpu.make_async_copy(
-                hidden.at[tokens], sent.at[tokens], sems.at[2 * PEERS + q // 2]
+                hidden.at[tokens], sent.at[tokens], sems.at[PEERS + q // 2]
             )
             copy.start()
             sent_copies.append(copy)
@@ -202,7 +203,7 @@
             pltpu.VMEM((CHIP_ROWS, D // 2), bf16),
             pltpu.VMEM((PEERS, TOK, STEP), bf16),
             pltpu.VMEM((PEERS, 2 * TOK, LAST), bf16),
-            pltpu.SemaphoreType.DMA((2 * PEERS + 4,)),
+            pltpu.SemaphoreType.DMA((PEERS + 4,)),
         ],
         compiler_params=params,
         cost_estimate=pl.CostEstimate(
@@ -345,8 +346,8 @@
 
 def fetch(source, target, sems):
     copies = []
-    for block in range(4):
-        tokens = slice(block * 256, block * 256 + 256)
+    for block in range(2):
+        tokens = slice(block * 512, block * 512 + 512)
         copy = pltpu.make_async_copy(source.at[tokens], target.at[tokens], sems.at[block])
         copy.start()
         copies.append(copy)
@@ -378,7 +379,7 @@
             jax.ShapeDtypeStruct((16, 128), f32),
             pltpu.VMEM((TOKENS, D), bf16),
         ],
-        scratch_shapes=[pltpu.SemaphoreType.DMA((4,))],
+        scratch_shapes=[pltpu.SemaphoreType.DMA((2,))],
         compiler_params=params,
         name="away",
     )(place, stats, logits, tokens, hidden)
@@ -408,7 +409,7 @@
         ],
         scratch_shapes=[
             pltpu.VMEM((PAD, TOKENS), bf16),
-            pltpu.SemaphoreType.DMA((4,)),
+            pltpu.SemaphoreType.DMA((2,)),
         ],
         compiler_params=params,
         name="own",
@@ -525,7 +526,7 @@
     factor = jnp.sqrt(row_mean) * column_scale / jnp.maximum(1.0, update_rms / clip_limit)
     for j in range(16):
         out[j] = (scaled[:OWN, 128 * j : 128 * j + 128] * factor[j : j + 1, :]).astype(bf16)
-    loss[...] = jnp.broadcast_to(jnp.sum(join_rows(total, 35), keepdims=True), (8, 128))
+    loss[...] = jnp.sum(join_rows(total, 35), keepdims=True)
 
 
 def update_call(sums, state, scaled):
@@ -535,7 +536,7 @@
         out_specs=[VMEM] * 2,
         out_shape=[
             jax.ShapeDtypeStruct((16, OWN, 128), bf16),
-            jax.ShapeDtypeStruct((8, 128), f32),
+            jax.ShapeDtypeStruct((1, 1), f32),
         ],
         compiler_params=params,
         name="update",
@@ -578,7 +579,7 @@
     sums = add_call(trade(sums, ("y", "xh", "core", "xl")))
     update, loss = update_call(trade(sums, "z"), state, scaled)
     update_step = trade(update, DP).reshape(VOC, COLS)
-    return (update_step, loss[0, 0])
+    return (update_step, loss.reshape(()))
 
 
 def solution(mesh):

time: 183 us -> 181 us (0.989)
  blocking collectives: 41.2 us -> 65.4 us
  waiting for transfers between devices: 52.2 us -> 35.8 us
  starting transfers between devices: 61.1 us -> 53.3 us
    all_to_all x3 -> x4, blocking collectives: 41.2 us -> 65.4 us  [trade(): return lax.all_to_all(value, axes, 0, 0)]
    all_to_all x3 -> x2, waiting for transfers between devices: 36 us -> 19.6 us  [trade(): return lax.all_to_all(value, axes, 0, 0)]
    all_to_all x3 -> x2, starting transfers between devices: 21.6 us -> 13.8 us  [trade(): return lax.all_to_all(value, axes, 0, 0)]
  transfers between devices with their start and end apart: 9 -> 8, of which waited for: 5 -> 4; matrix products, arithmetic and copies ran while one was open for 1% -> 1% of each run, Pallas kernels for 9% -> 8%
where the time goes in v6:
time: 181 us
  blocking collectives  65.4 us (36%)
  starting transfers between devices  53.3 us (29%)
  waiting for transfers between devices  35.8 us (20%)
  Pallas kernels  22.2 us (12%)
  local copies, waits for them, and re-layouts  3.01 us (2%)
    all_to_all x4, blocking collectives, trade(): return lax.all_to_all(value, axes, 0, 0)  65.4 us
    all_to_all x2, waiting for transfers between devices, trade(): return lax.all_to_all(value, axes, 0, 0)  19.6 us
    ppermute x3, starting transfers between devices, swap_cores(): return lax.ppermute(value, 'core', [(0, 1), (1, 0)])  16.8 us
    all_to_all x1, waiting for transfers between devices, per_device(): lax.all_to_all(spread(hidden), PLANE, 0, 0, axis_index_groups=groups)  15.1 us
    all_to_all x2, starting transfers between devices, trade(): return lax.all_to_all(value, axes, 0, 0)  13.8 us
    ppermute x1, starting transfers between devices, per_device(): lax.ppermute(first[4:], 'z', [(i, (i + 1 if i % 2 else i - 1) % 16) for i...  10.2 us
    all_to_all x1, starting transfers between devices, per_device(): lax.all_to_all(spread(hidden), PLANE, 0, 0, axis_index_groups=groups)  7.36 us
    ppermute x1, starting transfers between devices, per_device(): near = lax.ppermute(first[:4], 'z', [(i, i ^ 1) for i in range(16)])  5.07 us
  transfers between devices with their start and end apart: 8, of which 4 were waited for; matrix products, arithmetic and copies ran while one was open for 1% of the time, Pallas kernels for 8%

profile of v6, /device:TPU:1, one launch (start us, length us, event | category | flops | bytes accessed | tf_op | source)
XLA Modules:
  0.0 180.6 jit_solution(13923342364263194675)
XLA Ops:
  0.6 2.2 %spread.1 = bf16[8,128,768]{2,1,0:T(8,128)(2,1)} custom-call(bf16[128,2048]{1,0:T(8,128)(2,1)} %hidden.3), custom_call_target="tpu_custom_call" | custom-call | tf_op jit(solution)/shard_map/spread/pallas_call | solution.py:115
  2.9 7.4 %all-to-all-start = ((bf16[8,128,768]{2,1,0:T(8,128)(2,1)}), bf16[8,128,768]{2,1,0:T(8,128)(2,1)S(1)}, u32[]{:S(2)}, u32[]{:S(2)}) async-start(bf16[8,128,768]{2,1,0:T(8,128)(2,1)} %spread.1), calls=%async_computation | async-start | bytes 3145728 | tf_op jit(solution)/shard_map/all_to_all | solution.py:557
  11.1 3.1 %pack.1 = bf16[8,256,512]{2,1,0:T(8,128)(2,1)} custom-call(bf16[128,2048]{1,0:T(8,128)(2,1)S(1)} %copy-done, bf16[3968,128]{1,0:T(8,128)(2,1)S(1)} %copy-done.1, s32[1,128]{1,0:T(1,128)S(1)} %bitcast.11, s32[1,128]{1,0:T(1,128)S(1)} %bitcast.12, s32[1,128]{1,0:T(1,128)S(1)} %bitcast.13, f32[1,128]{1,0:T(1,128)S(1)} %bitcast.14), custom_call_target="tpu_custom_call" | custom-call | tf_op jit(solution)/shard_map/pack/pallas_call | solution.py:84
  14.2 15.1 %all-to-all-done.first = bf16[8,128,768]{2,1,0:T(8,128)(2,1)S(1)} async-done(((bf16[8,128,768]{2,1,0:T(8,128)(2,1)}), bf16[8,128,768]{2,1,0:T(8,128)(2,1)S(1)}, u32[]{:S(2)}, u32[]{:S(2)}) %all-to-all-start) | async-done | bytes 1572896 | tf_op jit(solution)/shard_map/all_to_all | solution.py:557
  29.3 5.4 %all-to-all-start.1 = ((bf16[8,256,512]{2,1,0:T(8,128)(2,1)}), bf16[8,256,512]{2,1,0:T(8,128)(2,1)}, u32[]{:S(2)}, u32[]{:S(2)}) async-start(bf16[8,256,512]{2,1,0:T(8,128)(2,1)} %pack.1), calls=%async_computation.1 | async-start | bytes 4194304 | tf_op jit(solution)/shard_map/all_to_all | solution.py:49
  34.7 1.2 fusion
  36.0 5.1 %collective-permute-start = (bf16[4,128,768]{2,1,0:T(8,128)(2,1)}, bf16[4,128,768]{2,1,0:T(8,128)(2,1)S(1)}, u32[]{:S(2)}, u32[]{:S(2)}) collective-permute-start(bf16[4,128,768]{2,1,0:T(8,128)(2,1)} %get-tuple-element.53), channel_id=1, source_target_pairs={{0,2},{2,0},{4,6},{6,4},{8,10},{10,8},{12,14},{14,12},{16,18},{18,... | collective-permute-start | bytes 2359304 | tf_op jit(solution)/shard_map/ppermute | solution.py:561
  41.1 10.2 %collective-permute-start.1 = (bf16[4,128,768]{2,1,0:T(8,128)(2,1)}, bf16[4,128,768]{2,1,0:T(8,128)(2,1)}, u32[]{:S(2)}, u32[]{:S(2)}) collective-permute-start(bf16[4,128,768]{2,1,0:T(8,128)(2,1)} %get-tuple-element.52), channel_id=1, source_target_pairs={{0,30},{2,4},{4,2},{6,8},{8,6},{10,12},{12,10},{14,16},{16,14},{18... | collective-permute-start | bytes 2359304 | tf_op jit(solution)/shard_map/ppermute | solution.py:562
  51.3 8.5 %all-to-all-done.1.last = bf16[8,256,512]{2,1,0:T(8,128)(2,1)} async-done(((bf16[8,256,512]{2,1,0:T(8,128)(2,1)}), bf16[8,256,512]{2,1,0:T(8,128)(2,1)}, u32[]{:S(2)}, u32[]{:S(2)}) %all-to-all-start.1) | async-done | bytes 2097184 | tf_op jit(solution)/shard_map/all_to_all | solution.py:49
  59.7 6.4 %collective-permute-start.2 = (bf16[8,256,512]{2,1,0:T(8,128)(2,1)}, bf16[8,256,512]{2,1,0:T(8,128)(2,1)S(1)}, u32[]{:S(2)}, u32[]{:S(2)}) collective-permute-start(bf16[8,256,512]{2,1,0:T(8,128)(2,1)} %all-to-all-done.1.last), channel_id=1, source_target_pairs={{0,32},{32,0},{1,33},{33,1},{2,34},{34,2},{3,35},{35,3},{4,36},{36... | collective-permute-start | bytes 6291464 | tf_op jit(solution)/shard_map/ppermute | solution.py:45
  66.1 1.1 collective-permute-done.1.far
  67.3 4.3 %half.1 = (bf16[1024,2048]{1,0:T(8,128)(2,1)S(1)}, bf16[1024,2048]{1,0:T(8,128)(2,1)}, f32[496,1024]{1,0:T(8,128)S(1)}, bf16[8,16,128]{2,1,0:T(8,128)(2,1)S(1)}) custom-call(s32[3]{0:T(128)S(1)} %pad_add_fusion.place, bf16[8,128,768]{2,1,0:T(8,128)(2,1)S(1)} %all-to-all-done.first, bf16[4,128,768]{2,1,0:T(8,128)(2,1)S(1)} %collective-permute-done.near, ...), custom_call_target="tpu_custom_call" | custom-call | flops 99999997952 | bytes 100000000 | tf_op jit(solution)/shard_map/half/pallas_call | solution.py:192
  71.6 1.8 logits.1
  73.4 4.7 %collective-permute-start.3 = (bf16[1024,2048]{1,0:T(8,128)(2,1)}, bf16[1024,2048]{1,0:T(8,128)(2,1)}, u32[]{:S(2)}, u32[]{:S(2)}) collective-permute-start(bf16[1024,2048]{1,0:T(8,128)(2,1)} %get-tuple-element.40.hidden), channel_id=1, source_target_pairs={{0,32},{32,0},{1,33},{33,1},{2,34},{34,2},{3,35},{35,3},{4,36},{36... | collective-permute-start | bytes 12582920 | tf_op jit(solution)/shard_map/ppermute | solution.py:45
  78.1 13.6 %all_to_all.35.stats = f32[16,16,128]{2,1,0:T(8,128)S(1)} all-to-all(f32[16,16,128]{2,1,0:T(8,128)S(1)} %get-tuple-element.35), channel_id=1, replica_groups=mesh['y'=4,'xh'=2,'core'=2,'z'=16,'xl'=2] {'y','xh','xl'}, dimensions={0} | all-to-all | bytes 262144 | tf_op jit(solution)/shard_map/all_to_all | solution.py:49
  92.4 8.4 %all-to-all-start.3 = ((f32[16,16,128]{2,1,0:T(8,128)}), f32[16,16,128]{2,1,0:T(8,128)S(1)}, u32[]{:S(2)}, u32[]{:S(2)}) async-start(f32[16,16,128]{2,1,0:T(8,128)} %merge.1), calls=%async_computation.3 | async-start | bytes 262144 | tf_op jit(solution)/shard_map/all_to_all | solution.py:49
  101.7 11.1 %all-to-all-done.3.stats = f32[16,16,128]{2,1,0:T(8,128)S(1)} async-done(((f32[16,16,128]{2,1,0:T(8,128)}), f32[16,16,128]{2,1,0:T(8,128)S(1)}, u32[]{:S(2)}, u32[]{:S(2)}) %all-to-all-start.3) | async-done | bytes 131104 | tf_op jit(solution)/shard_map/all_to_all | solution.py:49
  112.9 2.8 %away.1 = (bf16[256,1024]{1,0:T(8,128)(2,1)S(1)}, f32[16,128]{1,0:T(8,128)S(1)}, bf16[1024,2048]{1,0:T(8,128)(2,1)S(1)}) custom-call(s32[3]{0:T(128)S(1)} %pad_add_fusion.place, f32[16,16,128]{2,1,0:T(8,128)S(1)} %all-to-all-done.3.stats, f32[504,1024]{1,0:T(8,128)S(1)} %get-tuple-element.36.logits, f32[8,1024]{1,0:T(8,128)S(1)} %get-tuple-element.39.tokens, ...), custom_call_target="tpu_custom_call" | custom-call | tf_op jit(solution)/shard_map/away/pallas_call | solution.py:373
  115.6 5.8 %collective-permute-start.4 = (bf16[256,1024]{1,0:T(8,128)(2,1)S(1)}, bf16[256,1024]{1,0:T(8,128)(2,1)S(1)}, u32[]{:S(2)}, u32[]{:S(2)}) collective-permute-start(bf16[256,1024]{1,0:T(8,128)(2,1)S(1)} %get-tuple-element.44), channel_id=1, source_target_pairs={{0,32},{32,0},{1,33},{33,1},{2,34},{34,2},{3,35},{35,3},{4,36},{36... | collective-permute-start | bytes 1572872 | tf_op jit(solution)/shard_map/ppermute | solution.py:45
  121.4 3.1 %own.1 = (f32[256,2048]{1,0:T(8,128)S(1)}, bf16[1024,2048]{1,0:T(8,128)(2,1)S(1)}) custom-call(s32[3]{0:T(128)S(1)} %pad_add_fusion.place, f32[16,128]{1,0:T(8,128)S(1)} %get-tuple-element.41.totals, f32[504,1024]{1,0:T(8,128)S(1)} %get-tuple-element.36.logits, f32[8,1024]{1,0:T(8,128)S(1)} %get-tuple-element.39.tokens, ...), custom_call_target="tpu_custom_call" | custom-call | tf_op jit(solution)/shard_map/own/pallas_call | solution.py:402
  124.6 2.4 %grad.1 = (f32[256,2048]{1,0:T(8,128)S(1)}, bf16[32,40,128]{2,1,0:T(8,128)(2,1)S(1)}) custom-call(s32[3]{0:T(128)S(1)} %pad_add_fusion.place, f32[256,2048]{1,0:T(8,128)S(1)} %get-tuple-element.43.partial, bf16[256,1024]{1,0:T(8,128)(2,1)S(1)} %collective-permute-done.4.score, bf16[1024,2048]{1,0:T(8,128)(2,1)S(1)} %get-tuple-element.45.hidden, ...), custom_call_target="tpu_custom_call" | custom-call | tf_op jit(solution)/shard_map/grad/pallas_call | solution.py:481
  127.0 12.1 %all_to_all.36.sums = bf16[32,40,128]{2,1,0:T(8,128)(2,1)S(1)} all-to-all(bf16[32,40,128]{2,1,0:T(8,128)(2,1)S(1)} %get-tuple-element.47), channel_id=1, replica_groups=mesh['y'=4,'xh'=2,'core'=2,'z'=16,'xl'=2] {'y','xh','core','xl'}, dimensions={0} | all-to-all | bytes 655360 | tf_op jit(solution)/shard_map/all_to_all | solution.py:49
  139.1 15.6 %all_to_all.37.sums = bf16[16,40,128]{2,1,0:T(8,128)(2,1)S(1)} all-to-all(bf16[16,40,128]{2,1,0:T(8,128)(2,1)S(1)} %add.32), channel_id=1, replica_groups=mesh['y'=4,'xh'=2,'core'=2,'z'=16,'xl'=2] {'z'}, dimensions={0} | all-to-all | bytes 327680 | tf_op jit(solution)/shard_map/all_to_all | solution.py:49
  155.5 24.2 %all_to_all.38 = bf16[16,248,128]{2,1,0:T(8,128)(2,1)S(1)} all-to-all(bf16[16,248,128]{2,1,0:T(8,128)(2,1)S(1)} %get-tuple-element.50), channel_id=1, replica_groups=mesh['y'=4,'xh'=2,'core'=2,'z'=16,'xl'=2] {'y','xh','core'}, dimensions={0} | all-to-all | bytes 2031616 | tf_op jit(solution)/shard_map/all_to_all | solution.py:49
  (24 shorter events, 4.3 us)
Async XLA Ops:
  2.8 8.3 %copy-start = (bf16[128,2048]{1,0:T(8,128)(2,1)S(1)}, bf16[128,2048]{1,0:T(8,128)(2,1)}, u32[]{:S(2)}) copy-start(bf16[128,2048]{1,0:T(8,128)(2,1)} %hidden.3) | copy-start | bytes 1572868
  2.8 8.3 %copy-start.1 = (bf16[3968,128]{1,0:T(8,128)(2,1)S(1)}, bf16[3968,128]{1,0:T(8,128)(2,1)}, u32[]{:S(2)}) copy-start(bf16[3968,128]{1,0:T(8,128)(2,1)} %head.1) | copy-start | bytes 3047428
  2.8 8.3 %copy-start.2 = (s32[128]{0:T(128)S(1)}, s32[128]{0:T(128)}, u32[]{:S(2)}) copy-start(s32[128]{0:T(128)} %param.9) | copy-start | bytes 1540
  2.8 8.3 %copy-start.3 = (s32[128]{0:T(128)S(1)}, s32[128]{0:T(128)}, u32[]{:S(2)}) copy-start(s32[128]{0:T(128)} %param.10) | copy-start | bytes 1540
  2.9 8.3 %copy-start.4 = (s32[128]{0:T(128)S(1)}, s32[128]{0:T(128)}, u32[]{:S(2)}) copy-start(s32[128]{0:T(128)} %param.11) | copy-start | bytes 1540
  2.9 8.3 %copy-start.5 = (f32[128]{0:T(128)S(1)}, f32[128]{0:T(128)}, u32[]{:S(2)}) copy-start(f32[128]{0:T(128)} %param.13) | copy-start | bytes 1540
  2.9 26.4 %all-to-all-start = ((bf16[8,128,768]{2,1,0:T(8,128)(2,1)}), bf16[8,128,768]{2,1,0:T(8,128)(2,1)S(1)}, u32[]{:S(2)}, u32[]{:S(2)}) async-start(bf16[8,128,768]{2,1,0:T(8,128)(2,1)} %spread.1), calls=%async_computation | async-start | bytes 3145728 | tf_op jit(solution)/shard_map/all_to_all | solution.py:557
  29.3 30.4 %all-to-all-start.1 = ((bf16[8,256,512]{2,1,0:T(8,128)(2,1)}), bf16[8,256,512]{2,1,0:T(8,128)(2,1)}, u32[]{:S(2)}, u32[]{:S(2)}) async-start(bf16[8,256,512]{2,1,0:T(8,128)(2,1)} %pack.1), calls=%async_computation.1 | async-start | bytes 4194304 | tf_op jit(solution)/shard_map/all_to_all | solution.py:49
  36.0 30.2 %collective-permute-start = (bf16[4,128,768]{2,1,0:T(8,128)(2,1)}, bf16[4,128,768]{2,1,0:T(8,128)(2,1)S(1)}, u32[]{:S(2)}, u32[]{:S(2)}) collective-permute-start(bf16[4,128,768]{2,1,0:T(8,128)(2,1)} %get-tuple-element.53), channel_id=1, source_target_pairs={{0,2},{2,0},{4,6},{6,4},{8,10},{10,8},{12,14},{14,12},{16,18},{18,... | collective-permute-start | bytes 2359304 | tf_op jit(solution)/shard_map/ppermute | solution.py:561
  41.1 26.2 %collective-permute-start.1 = (bf16[4,128,768]{2,1,0:T(8,128)(2,1)}, bf16[4,128,768]{2,1,0:T(8,128)(2,1)}, u32[]{:S(2)}, u32[]{:S(2)}) collective-permute-start(bf16[4,128,768]{2,1,0:T(8,128)(2,1)} %get-tuple-element.52), channel_id=1, source_target_pairs={{0,30},{2,4},{4,2},{6,8},{8,6},{10,12},{12,10},{14,16},{16,14},{18... | collective-permute-start | bytes 2359304 | tf_op jit(solution)/shard_map/ppermute | solution.py:562
  59.7 11.9 %collective-permute-start.2 = (bf16[8,256,512]{2,1,0:T(8,128)(2,1)}, bf16[8,256,512]{2,1,0:T(8,128)(2,1)S(1)}, u32[]{:S(2)}, u32[]{:S(2)}) collective-permute-start(bf16[8,256,512]{2,1,0:T(8,128)(2,1)} %all-to-all-done.1.last), channel_id=1, source_target_pairs={{0,32},{32,0},{1,33},{33,1},{2,34},{34,2},{3,35},{35,3},{4,36},{36... | collective-permute-start | bytes 6291464 | tf_op jit(solution)/shard_map/ppermute | solution.py:45
  73.4 48.0 %collective-permute-start.3 = (bf16[1024,2048]{1,0:T(8,128)(2,1)}, bf16[1024,2048]{1,0:T(8,128)(2,1)}, u32[]{:S(2)}, u32[]{:S(2)}) collective-permute-start(bf16[1024,2048]{1,0:T(8,128)(2,1)} %get-tuple-element.40.hidden), channel_id=1, source_target_pairs={{0,32},{32,0},{1,33},{33,1},{2,34},{34,2},{3,35},{35,3},{4,36},{36... | collective-permute-start | bytes 12582920 | tf_op jit(solution)/shard_map/ppermute | solution.py:45
  92.4 20.4 %all-to-all-start.3 = ((f32[16,16,128]{2,1,0:T(8,128)}), f32[16,16,128]{2,1,0:T(8,128)S(1)}, u32[]{:S(2)}, u32[]{:S(2)}) async-start(f32[16,16,128]{2,1,0:T(8,128)} %merge.1), calls=%async_computation.3 | async-start | bytes 262144 | tf_op jit(solution)/shard_map/all_to_all | solution.py:49
  115.6 8.9 %collective-permute-start.4 = (bf16[256,1024]{1,0:T(8,128)(2,1)S(1)}, bf16[256,1024]{1,0:T(8,128)(2,1)S(1)}, u32[]{:S(2)}, u32[]{:S(2)}) collective-permute-start(bf16[256,1024]{1,0:T(8,128)(2,1)S(1)} %get-tuple-element.44), channel_id=1, source_target_pairs={{0,32},{32,0},{1,33},{33,1},{2,34},{34,2},{3,35},{35,3},{4,36},{36... | collective-permute-start | bytes 1572872 | tf_op jit(solution)/shard_map/ppermute | solution.py:45

commit v7 on v6

--- a/solution.py
+++ b/solution.py
@@ -28,7 +28,7 @@
 TOKENS = 1024
 SEGS = 64
 SUMS = 40
-STEP = 6 * 128
+STEP = 8 * 128
 LAST = 4 * 128
 f32 = jnp.float32
 bf16 = jnp.bfloat16
@@ -49,11 +49,10 @@
     return lax.all_to_all(value, axes, 0, 0)
 
 
-def pack_kernel(hidden, head, targets, segments, mask, state, out):
-    out[0, :TOK, :] = hidden[...]
+def pack_kernel(head, targets, segments, mask, state, out):
     for block in range(4):
         height = min(128, CHIP_ROWS - 128 * block)
-        out[0, TOK : TOK + height, 128 * block : 128 * block + 128] = head[
+        out[0, :height, 128 * block : 128 * block + 128] = head[
             128 * block : 128 * block + height, :
         ]
     row = lax.broadcasted_iota(jnp.int32, (16, 128), 0)
@@ -76,27 +75,26 @@
         ]
     ):
         facts = jnp.where(row == place, fact, facts)
-    out[0, 2 * TOK - 16 :, LAST - 128 :] = facts.astype(bf16)
-
-
-def pack(hidden, head, targets, segments, mask, state):
+    out[0, TOK - 16 :, LAST - 128 :] = facts.astype(bf16)
+
+
+def pack(head, targets, segments, mask, state):
     small = pl.BlockSpec((1, 128), lambda i: (0, 0))
     return pl.pallas_call(
         pack_kernel,
         grid=(PEERS,),
         in_specs=[
-            pl.BlockSpec((TOK, LAST), lambda i: (0, 3)),
             pl.BlockSpec((CHIP_ROWS, COLS), lambda i: (i, 0)),
             small,
             small,
             small,
             small,
         ],
-        out_specs=pl.BlockSpec((1, 2 * TOK, LAST), lambda i: (i, 0, 0)),
-        out_shape=pltpu.HBM((PEERS, 2 * TOK, LAST), bf16),
+        out_specs=pl.BlockSpec((1, TOK, LAST), lambda i: (i, 0, 0)),
+        out_shape=pltpu.HBM((PEERS, TOK, LAST), bf16),
         compiler_params=params,
         name="pack",
-    )(hidden, head, *[x.reshape(1, 128) for x in (targets, segments, mask, state)])
+    )(head, *[x.reshape(1, 128) for x in (targets, segments, mask, state)])
 
 
 def spread_kernel(hidden, out, part, sems):
@@ -126,11 +124,11 @@
     )(hidden)
 
 
-def gather_weight(source, q, rows, weight):
+def gather_weight(source, q, weight):
     for block in range(4):
         height = min(128, CHIP_ROWS - 128 * block)
         weight[128 * block : 128 * block + height, q * 128 : q * 128 + 128] = source[
-            q, rows : rows + height, 128 * block : 128 * block + 128
+            q, :height, 128 * block : 128 * block + 128
         ]
 
 
@@ -160,14 +158,13 @@
 
     sent_copies = []
     for q in range(PEERS):
-        fill(first, q, 3 * odd, 6)
+        fill(first, q, 4 * odd, 8)
         if q % 2 == 0:
             rest_copies[q // 2].wait()
-        fill(rest, q, 6, 4)
-        gather_weight(rest, q, TOK, weight)
+        gather_weight(rest, q, weight)
         if q % 2 == 0:
             beside_copies[q // 2].wait()
-        fill(beside, q, 3 - 3 * odd, 6)
+        fill(beside, q, 4 - 4 * odd, 8)
         if q % 2 == 1:
             tokens = slice((q - 1) * TOK, (q + 1) * TOK)
             copy = pltpu.make_async_copy(
@@ -175,7 +172,7 @@
             )
             copy.start()
             sent_copies.append(copy)
-    facts[...] = rest[:, 2 * TOK - 16 :, LAST - 128 :]
+    facts[...] = rest[:, TOK - 16 :, LAST - 128 :]
     for block in range(4):
         tokens = slice(256 * block, 256 * block + 256)
         partial[:, tokens] = lax.dot_general(
@@ -202,7 +199,7 @@
         scratch_shapes=[
             pltpu.VMEM((CHIP_ROWS, D // 2), bf16),
             pltpu.VMEM((PEERS, TOK, STEP), bf16),
-            pltpu.VMEM((PEERS, 2 * TOK, LAST), bf16),
+            pltpu.VMEM((PEERS, TOK, LAST), bf16),
             pltpu.SemaphoreType.DMA((PEERS + 4,)),
         ],
         compiler_params=params,
@@ -214,9 +211,9 @@
 
 
 def logits_kernel(hidden, partial, other, logits, stats, facts, weight, table):
-    facts[...] = other[:, 2 * TOK - 16 :, LAST - 128 :]
-    for q in range(PEERS):
-        gather_weight(other, q, TOK, weight)
+    facts[...] = other[:, TOK - 16 :, LAST - 128 :]
+    for q in range(PEERS):
+        gather_weight(other, q, weight)
     logits[CHIP_ROWS:, :] = jnp.zeros((8, TOKENS), f32)
     for block in range(4):
         tokens = slice(256 * block, 256 * block + 256)
@@ -555,7 +552,7 @@
 
     groups = [[4 * y + 2 * xh + (xh ^ k) for y in range(4) for xh in range(2)] for k in range(2)]
     first = lax.all_to_all(spread(hidden), PLANE, 0, 0, axis_index_groups=groups)
-    last = pack(hidden, head_weight, targets, segments, loss_mask, column_state)
+    last = pack(head_weight, targets, segments, loss_mask, column_state)
     last, first = lax.optimization_barrier((last, first))
     last = trade(last, CHIPS)
     near = lax.ppermute(first[:4], "z", [(i, i ^ 1) for i in range(16)])

time: 181 us -> 182 us (level)
  blocking collectives: 65.4 us -> 80.2 us
  starting transfers between devices: 53.3 us -> 44.6 us
  waiting for transfers between devices: 35.8 us -> 32 us
    all_to_all x4 -> x5, blocking collectives: 65.4 us -> 80.2 us  [trade(): return lax.all_to_all(value, axes, 0, 0)]
    all_to_all x2 -> x1, waiting for transfers between devices: 19.6 us -> 11 us  [trade(): return lax.all_to_all(value, axes, 0, 0)]
    all_to_all x2 -> x1, starting transfers between devices: 13.8 us -> 5.97 us  [trade(): return lax.all_to_all(value, axes, 0, 0)]
    all_to_all x1, waiting for transfers between devices: 15.1 us -> 20.9 us  [per_device(): lax.all_to_all(spread(hidden), PLANE, 0, 0, axis_index_groups=groups)]
    ppermute x1, starting transfers between devices: 10.2 us -> 13.9 us  [per_device(): lax.ppermute(first[4:], 'z', [(i, (i + 1 if i % 2 else i - 1) % 16) for i...]
    ppermute x1, starting transfers between devices: 5.07 us -> 1.92 us  [per_device(): near = lax.ppermute(first[:4], 'z', [(i, i ^ 1) for i in range(16)])]
  transfers between devices with their start and end apart: 8 -> 7, of which waited for: 4 -> 2; matrix products, arithmetic and copies ran while one was open for 1% -> 0% of each run, Pallas kernels for 8% -> 8%
where the time goes in v7:
time: 182 us; the launch traced here: 181 us
  blocking collectives  80.2 us (44%)
  starting transfers between devices  44.6 us (25%)
  waiting for transfers between devices  32 us (18%)
  Pallas kernels  21.2 us (12%)
  local copies, waits for them, and re-layouts  2.04 us (1%)
    all_to_all x5, blocking collectives, trade(): return lax.all_to_all(value, axes, 0, 0)  80.2 us
    all_to_all x1, waiting for transfers between devices, per_device(): lax.all_to_all(spread(hidden), PLANE, 0, 0, axis_index_groups=groups)  20.9 us
    ppermute x3, starting transfers between devices, swap_cores(): return lax.ppermute(value, 'core', [(0, 1), (1, 0)])  15.5 us
    ppermute x1, starting transfers between devices, per_device(): lax.ppermute(first[4:], 'z', [(i, (i + 1 if i % 2 else i - 1) % 16) for i...  13.9 us
    all_to_all x1, waiting for transfers between devices, trade(): return lax.all_to_all(value, axes, 0, 0)  11 us
    all_to_all x1, starting transfers between devices, per_device(): lax.all_to_all(spread(hidden), PLANE, 0, 0, axis_index_groups=groups)  7.36 us
    all_to_all x1, starting transfers between devices, trade(): return lax.all_to_all(value, axes, 0, 0)  5.97 us
  transfers between devices with their start and end apart: 7, of which 2 were waited for; matrix products, arithmetic and copies ran while one was open for 0% of the time, Pallas kernels for 8%

profile of v7, /device:TPU:1, one launch (start us, length us, event | category | flops | bytes accessed | tf_op | source)
XLA Modules:
  0.0 180.9 jit_solution(8968197925898032005)
XLA Ops:
  0.6 2.4 %spread.1 = bf16[8,128,1024]{2,1,0:T(8,128)(2,1)} custom-call(bf16[128,2048]{1,0:T(8,128)(2,1)} %hidden.1), custom_call_target="tpu_custom_call" | custom-call | tf_op jit(solution)/shard_map/spread/pallas_call | solution.py:113
  3.1 7.4 %all-to-all-start = ((bf16[8,128,1024]{2,1,0:T(8,128)(2,1)}), bf16[8,128,1024]{2,1,0:T(8,128)(2,1)S(1)}, u32[]{:S(2)}, u32[]{:S(2)}) async-start(bf16[8,128,1024]{2,1,0:T(8,128)(2,1)} %spread.1), calls=%async_computation | async-start | bytes 4194304 | tf_op jit(solution)/shard_map/all_to_all | solution.py:554
  10.4 0.8 dynamic_slice.3
  11.3 2.8 %pack.1 = bf16[8,128,512]{2,1,0:T(8,128)(2,1)} custom-call(bf16[3968,128]{1,0:T(8,128)(2,1)S(1)} %copy-done, s32[1,128]{1,0:T(1,128)S(1)} %bitcast.11, s32[1,128]{1,0:T(1,128)S(1)} %bitcast.12, s32[1,128]{1,0:T(1,128)S(1)} %bitcast.13, f32[1,128]{1,0:T(1,128)S(1)} %bitcast.14), custom_call_target="tpu_custom_call" | custom-call | tf_op jit(solution)/shard_map/pack/pallas_call | solution.py:83
  14.2 20.9 %all-to-all-done.first = bf16[8,128,1024]{2,1,0:T(8,128)(2,1)S(1)} async-done(((bf16[8,128,1024]{2,1,0:T(8,128)(2,1)}), bf16[8,128,1024]{2,1,0:T(8,128)(2,1)S(1)}, u32[]{:S(2)}, u32[]{:S(2)}) %all-to-all-start) | async-done | bytes 2097184 | tf_op jit(solution)/shard_map/all_to_all | solution.py:554
  35.4 13.9 %collective-permute-start.1 = (bf16[4,128,1024]{2,1,0:T(8,128)(2,1)S(1)}, bf16[4,128,1024]{2,1,0:T(8,128)(2,1)S(1)}, u32[]{:S(2)}, u32[]{:S(2)}) collective-permute-start(bf16[4,128,1024]{2,1,0:T(8,128)(2,1)S(1)} %get-tuple-element.52), channel_id=1, source_target_pairs={{0,30},{2,4},{4,2},{6,8},{8,6},{10,12},{12,10},{14,16},{16,14},{18... | collective-permute-start | bytes 3145736 | tf_op jit(solution)/shard_map/ppermute | solution.py:559
  49.3 1.9 %collective-permute-start = (bf16[4,128,1024]{2,1,0:T(8,128)(2,1)S(1)}, bf16[4,128,1024]{2,1,0:T(8,128)(2,1)S(1)}, u32[]{:S(2)}, u32[]{:S(2)}) collective-permute-start(bf16[4,128,1024]{2,1,0:T(8,128)(2,1)S(1)} %get-tuple-element.53), channel_id=1, source_target_pairs={{0,2},{2,0},{4,6},{6,4},{8,10},{10,8},{12,14},{14,12},{16,18},{18,... | collective-permute-start | bytes 3145736 | tf_op jit(solution)/shard_map/ppermute | solution.py:558
  51.2 17.6 %all_to_all.35.last = bf16[8,128,512]{2,1,0:T(8,128)(2,1)S(1)} all-to-all(bf16[8,128,512]{2,1,0:T(8,128)(2,1)S(1)} %copy-done.5), channel_id=1, replica_groups=mesh['y'=4,'xh'=2,'core'=2,'z'=16,'xl'=2] {'y','xh'}, dimensions={0} | all-to-all | bytes 2097152 | tf_op jit(solution)/shard_map/all_to_all | solution.py:49
  68.8 5.1 %collective-permute-start.2 = (bf16[8,128,512]{2,1,0:T(8,128)(2,1)S(1)}, bf16[8,128,512]{2,1,0:T(8,128)(2,1)S(1)}, u32[]{:S(2)}, u32[]{:S(2)}) collective-permute-start(bf16[8,128,512]{2,1,0:T(8,128)(2,1)S(1)} %all_to_all.35.last), channel_id=1, source_target_pairs={{0,32},{32,0},{1,33},{33,1},{2,34},{34,2},{3,35},{35,3},{4,36},{36... | collective-permute-start | bytes 3145736 | tf_op jit(solution)/shard_map/ppermute | solution.py:45
  73.9 3.4 %half.1 = (bf16[1024,2048]{1,0:T(8,128)(2,1)S(1)}, bf16[1024,2048]{1,0:T(8,128)(2,1)}, f32[496,1024]{1,0:T(8,128)S(1)}, bf16[8,16,128]{2,1,0:T(8,128)(2,1)S(1)}) custom-call(s32[3]{0:T(128)S(1)} %pad_add_fusion.place, bf16[8,128,1024]{2,1,0:T(8,128)(2,1)S(1)} %all-to-all-done.first, bf16[4,128,1024]{2,1,0:T(8,128)(2,1)S(1)} %collective-permute-done.near, ...), custom_call_target="tpu_custom_call" | custom-call | flops 99999997952 | bytes 100000000 | tf_op jit(solution)/shard_map/half/pallas_call | solution.py:189
  77.4 1.8 logits.1
  79.1 4.7 %collective-permute-start.3 = (bf16[1024,2048]{1,0:T(8,128)(2,1)}, bf16[1024,2048]{1,0:T(8,128)(2,1)}, u32[]{:S(2)}, u32[]{:S(2)}) collective-permute-start(bf16[1024,2048]{1,0:T(8,128)(2,1)} %get-tuple-element.40.hidden), channel_id=1, source_target_pairs={{0,32},{32,0},{1,33},{33,1},{2,34},{34,2},{3,35},{35,3},{4,36},{36... | collective-permute-start | bytes 12582920 | tf_op jit(solution)/shard_map/ppermute | solution.py:45
  83.9 10.8 %all_to_all.36.stats = f32[16,16,128]{2,1,0:T(8,128)S(1)} all-to-all(f32[16,16,128]{2,1,0:T(8,128)S(1)} %get-tuple-element.35), channel_id=1, replica_groups=mesh['y'=4,'xh'=2,'core'=2,'z'=16,'xl'=2] {'y','xh','xl'}, dimensions={0} | all-to-all | bytes 262144 | tf_op jit(solution)/shard_map/all_to_all | solution.py:49
  95.4 6.0 %all-to-all-start.3 = ((f32[16,16,128]{2,1,0:T(8,128)}), f32[16,16,128]{2,1,0:T(8,128)S(1)}, u32[]{:S(2)}, u32[]{:S(2)}) async-start(f32[16,16,128]{2,1,0:T(8,128)} %merge.1), calls=%async_computation.3 | async-start | bytes 262144 | tf_op jit(solution)/shard_map/all_to_all | solution.py:49
  101.4 0.9 tokens.1
  102.3 11.0 %all-to-all-done.3.stats = f32[16,16,128]{2,1,0:T(8,128)S(1)} async-done(((f32[16,16,128]{2,1,0:T(8,128)}), f32[16,16,128]{2,1,0:T(8,128)S(1)}, u32[]{:S(2)}, u32[]{:S(2)}) %all-to-all-start.3) | async-done | bytes 131104 | tf_op jit(solution)/shard_map/all_to_all | solution.py:49
  113.3 2.8 %away.1 = (bf16[256,1024]{1,0:T(8,128)(2,1)S(1)}, f32[16,128]{1,0:T(8,128)S(1)}, bf16[1024,2048]{1,0:T(8,128)(2,1)S(1)}) custom-call(s32[3]{0:T(128)S(1)} %pad_add_fusion.place, f32[16,16,128]{2,1,0:T(8,128)S(1)} %all-to-all-done.3.stats, f32[504,1024]{1,0:T(8,128)S(1)} %get-tuple-element.36.logits, f32[8,1024]{1,0:T(8,128)S(1)} %get-tuple-element.39.tokens, ...), custom_call_target="tpu_custom_call" | custom-call | tf_op jit(solution)/shard_map/away/pallas_call | solution.py:370
  116.1 5.6 %collective-permute-start.4 = (bf16[256,1024]{1,0:T(8,128)(2,1)S(1)}, bf16[256,1024]{1,0:T(8,128)(2,1)S(1)}, u32[]{:S(2)}, u32[]{:S(2)}) collective-permute-start(bf16[256,1024]{1,0:T(8,128)(2,1)S(1)} %get-tuple-element.44), channel_id=1, source_target_pairs={{0,32},{32,0},{1,33},{33,1},{2,34},{34,2},{3,35},{35,3},{4,36},{36... | collective-permute-start | bytes 1572872 | tf_op jit(solution)/shard_map/ppermute | solution.py:45
  121.8 3.1 %own.1 = (f32[256,2048]{1,0:T(8,128)S(1)}, bf16[1024,2048]{1,0:T(8,128)(2,1)S(1)}) custom-call(s32[3]{0:T(128)S(1)} %pad_add_fusion.place, f32[16,128]{1,0:T(8,128)S(1)} %get-tuple-element.41.totals, f32[504,1024]{1,0:T(8,128)S(1)} %get-tuple-element.36.logits, f32[8,1024]{1,0:T(8,128)S(1)} %get-tuple-element.39.tokens, ...), custom_call_target="tpu_custom_call" | custom-call | tf_op jit(solution)/shard_map/own/pallas_call | solution.py:399
  124.9 2.4 %grad.1 = (f32[256,2048]{1,0:T(8,128)S(1)}, bf16[32,40,128]{2,1,0:T(8,128)(2,1)S(1)}) custom-call(s32[3]{0:T(128)S(1)} %pad_add_fusion.place, f32[256,2048]{1,0:T(8,128)S(1)} %get-tuple-element.43.partial, bf16[256,1024]{1,0:T(8,128)(2,1)S(1)} %collective-permute-done.4.score, bf16[1024,2048]{1,0:T(8,128)(2,1)S(1)} %get-tuple-element.45.hidden, ...), custom_call_target="tpu_custom_call" | custom-call | tf_op jit(solution)/shard_map/grad/pallas_call | solution.py:478
  127.3 12.1 %all_to_all.37.sums = bf16[32,40,128]{2,1,0:T(8,128)(2,1)S(1)} all-to-all(bf16[32,40,128]{2,1,0:T(8,128)(2,1)S(1)} %get-tuple-element.47), channel_id=1, replica_groups=mesh['y'=4,'xh'=2,'core'=2,'z'=16,'xl'=2] {'y','xh','core','xl'}, dimensions={0} | all-to-all | bytes 655360 | tf_op jit(solution)/shard_map/all_to_all | solution.py:49
  139.5 15.5 %all_to_all.38.sums = bf16[16,40,128]{2,1,0:T(8,128)(2,1)S(1)} all-to-all(bf16[16,40,128]{2,1,0:T(8,128)(2,1)S(1)} %add.32), channel_id=1, replica_groups=mesh['y'=4,'xh'=2,'core'=2,'z'=16,'xl'=2] {'z'}, dimensions={0} | all-to-all | bytes 327680 | tf_op jit(solution)/shard_map/all_to_all | solution.py:49
  155.7 24.2 %all_to_all.39 = bf16[16,248,128]{2,1,0:T(8,128)(2,1)S(1)} all-to-all(bf16[16,248,128]{2,1,0:T(8,128)(2,1)S(1)} %get-tuple-element.50), channel_id=1, replica_groups=mesh['y'=4,'xh'=2,'core'=2,'z'=16,'xl'=2] {'y','xh','core'}, dimensions={0} | all-to-all | bytes 2031616 | tf_op jit(solution)/shard_map/all_to_all | solution.py:49
  179.9 1.0 copy.10
  (23 shorter events, 1.9 us)
Async XLA Ops:
  3.0 8.3 %copy-start = (bf16[3968,128]{1,0:T(8,128)(2,1)S(1)}, bf16[3968,128]{1,0:T(8,128)(2,1)}, u32[]{:S(2)}) copy-start(bf16[3968,128]{1,0:T(8,128)(2,1)} %head.1) | copy-start | bytes 3047428
  3.0 8.3 %copy-start.1 = (s32[128]{0:T(128)S(1)}, s32[128]{0:T(128)}, u32[]{:S(2)}) copy-start(s32[128]{0:T(128)} %param.9) | copy-start | bytes 1540
  3.0 8.3 %copy-start.2 = (s32[128]{0:T(128)S(1)}, s32[128]{0:T(128)}, u32[]{:S(2)}) copy-start(s32[128]{0:T(128)} %param.10) | copy-start | bytes 1540
  3.0 8.2 %copy-start.3 = (s32[128]{0:T(128)S(1)}, s32[128]{0:T(128)}, u32[]{:S(2)}) copy-start(s32[128]{0:T(128)} %param.11) | copy-start | bytes 1540
  3.1 8.2 %copy-start.4 = (f32[128]{0:T(128)S(1)}, f32[128]{0:T(128)}, u32[]{:S(2)}) copy-start(f32[128]{0:T(128)} %param.13) | copy-start | bytes 1540
  3.1 32.0 %all-to-all-start = ((bf16[8,128,1024]{2,1,0:T(8,128)(2,1)}), bf16[8,128,1024]{2,1,0:T(8,128)(2,1)S(1)}, u32[]{:S(2)}, u32[]{:S(2)}) async-start(bf16[8,128,1024]{2,1,0:T(8,128)(2,1)} %spread.1), calls=%async_computation | async-start | bytes 4194304 | tf_op jit(solution)/shard_map/all_to_all | solution.py:554
  35.1 16.1 %copy-start.5 = (bf16[8,128,512]{2,1,0:T(8,128)(2,1)S(1)}, bf16[8,128,512]{2,1,0:T(8,128)(2,1)}, u32[]{:S(2)}) copy-start(bf16[8,128,512]{2,1,0:T(8,128)(2,1)} %pack.1) | copy-start | bytes 3145732
  35.4 38.5 %collective-permute-start.1 = (bf16[4,128,1024]{2,1,0:T(8,128)(2,1)S(1)}, bf16[4,128,1024]{2,1,0:T(8,128)(2,1)S(1)}, u32[]{:S(2)}, u32[]{:S(2)}) collective-permute-start(bf16[4,128,1024]{2,1,0:T(8,128)(2,1)S(1)} %get-tuple-element.52), channel_id=1, source_target_pairs={{0,30},{2,4},{4,2},{6,8},{8,6},{10,12},{12,10},{14,16},{16,14},{18... | collective-permute-start | bytes 3145736 | tf_op jit(solution)/shard_map/ppermute | solution.py:559
  49.3 24.6 %collective-permute-start = (bf16[4,128,1024]{2,1,0:T(8,128)(2,1)S(1)}, bf16[4,128,1024]{2,1,0:T(8,128)(2,1)S(1)}, u32[]{:S(2)}, u32[]{:S(2)}) collective-permute-start(bf16[4,128,1024]{2,1,0:T(8,128)(2,1)S(1)} %get-tuple-element.53), channel_id=1, source_target_pairs={{0,2},{2,0},{4,6},{6,4},{8,10},{10,8},{12,14},{14,12},{16,18},{18,... | collective-permute-start | bytes 3145736 | tf_op jit(solution)/shard_map/ppermute | solution.py:558
  68.8 8.6 %collective-permute-start.2 = (bf16[8,128,512]{2,1,0:T(8,128)(2,1)S(1)}, bf16[8,128,512]{2,1,0:T(8,128)(2,1)S(1)}, u32[]{:S(2)}, u32[]{:S(2)}) collective-permute-start(bf16[8,128,512]{2,1,0:T(8,128)(2,1)S(1)} %all_to_all.35.last), channel_id=1, source_target_pairs={{0,32},{32,0},{1,33},{33,1},{2,34},{34,2},{3,35},{35,3},{4,36},{36... | collective-permute-start | bytes 3145736 | tf_op jit(solution)/shard_map/ppermute | solution.py:45
  79.1 42.7 %collective-permute-start.3 = (bf16[1024,2048]{1,0:T(8,128)(2,1)}, bf16[1024,2048]{1,0:T(8,128)(2,1)}, u32[]{:S(2)}, u32[]{:S(2)}) collective-permute-start(bf16[1024,2048]{1,0:T(8,128)(2,1)} %get-tuple-element.40.hidden), channel_id=1, source_target_pairs={{0,32},{32,0},{1,33},{33,1},{2,34},{34,2},{3,35},{35,3},{4,36},{36... | collective-permute-start | bytes 12582920 | tf_op jit(solution)/shard_map/ppermute | solution.py:45
  95.4 18.0 %all-to-all-start.3 = ((f32[16,16,128]{2,1,0:T(8,128)}), f32[16,16,128]{2,1,0:T(8,128)S(1)}, u32[]{:S(2)}, u32[]{:S(2)}) async-start(f32[16,16,128]{2,1,0:T(8,128)} %merge.1), calls=%async_computation.3 | async-start | bytes 262144 | tf_op jit(solution)/shard_map/all_to_all | solution.py:49
  116.1 8.8 %collective-permute-start.4 = (bf16[256,1024]{1,0:T(8,128)(2,1)S(1)}, bf16[256,1024]{1,0:T(8,128)(2,1)S(1)}, u32[]{:S(2)}, u32[]{:S(2)}) collective-permute-start(bf16[256,1024]{1,0:T(8,128)(2,1)S(1)} %get-tuple-element.44), channel_id=1, source_target_pairs={{0,32},{32,0},{1,33},{33,1},{2,34},{34,2},{3,35},{35,3},{4,36},{36... | collective-permute-start | bytes 1572872 | tf_op jit(solution)/shard_map/ppermute | solution.py:45

commit v8 on v6

--- a/solution.py
+++ b/solution.py
@@ -140,16 +140,20 @@
     core = place[0]
     odd = place[2]
     pairs = PEERS // 2
-    rest_copies, beside_copies = [], []
+    rest_copies, beside_copies = [], {}
     for i in range(pairs):
         two = slice(2 * i, 2 * i + 2)
         copy = pltpu.make_async_copy(last.at[two], rest.at[two], sems.at[i])
         copy.start()
         rest_copies.append(copy)
-        source = (near if i < 2 else far).at[slice(2 * (i % 2), 2 * (i % 2) + 2)]
-        copy = pltpu.make_async_copy(source, beside.at[two], sems.at[pairs + i])
+
+    cuts = [(near, 0, 2, 0), (near, 2, 4, 2), (near, 4, 5, 4), (far, 0, 1, 5), (far, 1, 3, 6)]
+    for i, (source, low, high, q) in enumerate(cuts):
+        copy = pltpu.make_async_copy(
+            source.at[low:high], beside.at[q : q + high - low], sems.at[PEERS + i]
+        )
         copy.start()
-        beside_copies.append(copy)
+        beside_copies[q] = copy
 
     def fill(source, q, start, count):
         for i in range(count):
@@ -165,13 +169,13 @@
             rest_copies[q // 2].wait()
         fill(rest, q, 6, 4)
         gather_weight(rest, q, TOK, weight)
-        if q % 2 == 0:
-            beside_copies[q // 2].wait()
+        if q in beside_copies:
+            beside_copies[q].wait()
         fill(beside, q, 3 - 3 * odd, 6)
         if q % 2 == 1:
             tokens = slice((q - 1) * TOK, (q + 1) * TOK)
             copy = pltpu.make_async_copy(
-                hidden.at[tokens], sent.at[tokens], sems.at[PEERS + q // 2]
+                hidden.at[tokens], sent.at[tokens], sems.at[4 + q // 2]
             )
             copy.start()
             sent_copies.append(copy)
@@ -203,7 +207,7 @@
             pltpu.VMEM((CHIP_ROWS, D // 2), bf16),
             pltpu.VMEM((PEERS, TOK, STEP), bf16),
             pltpu.VMEM((PEERS, 2 * TOK, LAST), bf16),
-            pltpu.SemaphoreType.DMA((PEERS + 4,)),
+            pltpu.SemaphoreType.DMA((PEERS + 5,)),
         ],
         compiler_params=params,
         cost_estimate=pl.CostEstimate(
@@ -558,8 +562,8 @@
     last = pack(hidden, head_weight, targets, segments, loss_mask, column_state)
     last, first = lax.optimization_barrier((last, first))
     last = trade(last, CHIPS)
-    near = lax.ppermute(first[:4], "z", [(i, i ^ 1) for i in range(16)])
-    far = lax.ppermute(first[4:], "z", [(i, (i + 1 if i % 2 else i - 1) % 16) for i in range(16)])
+    near = lax.ppermute(first[:5], "z", [(i, i ^ 1) for i in range(16)])
+    far = lax.ppermute(first[5:], "z", [(i, (i + 1 if i % 2 else i - 1) % 16) for i in range(16)])
     last_other = swap_cores(last)
     hidden_own, hidden_sent, partial, own_facts = half_call(place, first, near, far, last)
     logits, stats, other_facts = logits_call(hidden_own, partial, last_other)

time: 181 us -> 181 us (level)
    all_to_all x2, starting transfers between devices: 13.8 us -> 17.4 us  [trade(): return lax.all_to_all(value, axes, 0, 0)]
    ppermute x3, starting transfers between devices: 16.8 us -> 14.3 us  [swap_cores(): return lax.ppermute(value, 'core', [(0, 1), (1, 0)])]
  transfers between devices with their start and end apart: 8 -> 8, of which waited for: 4 -> 3; matrix products, arithmetic and copies ran while one was open for 1% -> 2% of each run, Pallas kernels for 8% -> 8%
where the time goes in v8:
time: 181 us
  blocking collectives  65.4 us (36%)
  starting transfers between devices  54.3 us (30%)
  waiting for transfers between devices  34.1 us (19%)
  Pallas kernels  22.1 us (12%)
  local copies, waits for them, and re-layouts  3.64 us (2%)
    all_to_all x4, blocking collectives, trade(): return lax.all_to_all(value, axes, 0, 0)  65.4 us
    all_to_all x2, waiting for transfers between devices, trade(): return lax.all_to_all(value, axes, 0, 0)  19 us
    all_to_all x2, starting transfers between devices, trade(): return lax.all_to_all(value, axes, 0, 0)  17.4 us
    all_to_all x1, waiting for transfers between devices, per_device(): lax.all_to_all(spread(hidden), PLANE, 0, 0, axis_index_groups=groups)  15.1 us
    ppermute x3, starting transfers between devices, swap_cores(): return lax.ppermute(value, 'core', [(0, 1), (1, 0)])  14.3 us
    ppermute x1, starting transfers between devices, per_device(): lax.ppermute(first[5:], 'z', [(i, (i + 1 if i % 2 else i - 1) % 16) for i...  10.2 us
    all_to_all x1, starting transfers between devices, per_device(): lax.all_to_all(spread(hidden), PLANE, 0, 0, axis_index_groups=groups)  7.36 us
    ppermute x1, starting transfers between devices, per_device(): near = lax.ppermute(first[:5], 'z', [(i, i ^ 1) for i in range(16)])  5.06 us
  transfers between devices with their start and end apart: 8, of which 3 were waited for; matrix products, arithmetic and copies ran while one was open for 2% of the time, Pallas kernels for 8%

profile of v8, /device:TPU:1, one launch (start us, length us, event | category | flops | bytes accessed | tf_op | source)
XLA Modules:
  0.0 180.6 jit_solution(5726721934603572457)
XLA Ops:
  0.6 2.2 %spread.1 = bf16[8,128,768]{2,1,0:T(8,128)(2,1)} custom-call(bf16[128,2048]{1,0:T(8,128)(2,1)} %hidden.3), custom_call_target="tpu_custom_call" | custom-call | tf_op jit(solution)/shard_map/spread/pallas_call | solution.py:115
  2.9 7.4 %all-to-all-start = ((bf16[8,128,768]{2,1,0:T(8,128)(2,1)}), bf16[8,128,768]{2,1,0:T(8,128)(2,1)S(1)}, u32[]{:S(2)}, u32[]{:S(2)}) async-start(bf16[8,128,768]{2,1,0:T(8,128)(2,1)} %spread.1), calls=%async_computation | async-start | bytes 3145728 | tf_op jit(solution)/shard_map/all_to_all | solution.py:561
  11.1 3.1 %pack.1 = bf16[8,256,512]{2,1,0:T(8,128)(2,1)} custom-call(bf16[128,2048]{1,0:T(8,128)(2,1)S(1)} %copy-done, bf16[3968,128]{1,0:T(8,128)(2,1)S(1)} %copy-done.1, s32[1,128]{1,0:T(1,128)S(1)} %bitcast.11, s32[1,128]{1,0:T(1,128)S(1)} %bitcast.12, s32[1,128]{1,0:T(1,128)S(1)} %bitcast.13, f32[1,128]{1,0:T(1,128)S(1)} %bitcast.14), custom_call_target="tpu_custom_call" | custom-call | tf_op jit(solution)/shard_map/pack/pallas_call | solution.py:84
  14.2 15.1 %all-to-all-done.first = bf16[8,128,768]{2,1,0:T(8,128)(2,1)S(1)} async-done(((bf16[8,128,768]{2,1,0:T(8,128)(2,1)}), bf16[8,128,768]{2,1,0:T(8,128)(2,1)S(1)}, u32[]{:S(2)}, u32[]{:S(2)}) %all-to-all-start) | async-done | bytes 1572896 | tf_op jit(solution)/shard_map/all_to_all | solution.py:561
  29.3 5.4 %all-to-all-start.1 = ((bf16[8,256,512]{2,1,0:T(8,128)(2,1)}), bf16[8,256,512]{2,1,0:T(8,128)(2,1)}, u32[]{:S(2)}, u32[]{:S(2)}) async-start(bf16[8,256,512]{2,1,0:T(8,128)(2,1)} %pack.1), calls=%async_computation.1 | async-start | bytes 4194304 | tf_op jit(solution)/shard_map/all_to_all | solution.py:49
  34.7 1.0 slice.6
  35.7 5.1 %collective-permute-start = (bf16[5,128,768]{2,1,0:T(8,128)(2,1)}, bf16[5,128,768]{2,1,0:T(8,128)(2,1)S(1)}, u32[]{:S(2)}, u32[]{:S(2)}) collective-permute-start(bf16[5,128,768]{2,1,0:T(8,128)(2,1)} %slice.6), channel_id=1, source_target_pairs={{0,2},{2,0},{4,6},{6,4},{8,10},{10,8},{12,14},{14,12},{16,18},{18,... | collective-permute-start | bytes 2949128 | tf_op jit(solution)/shard_map/ppermute | solution.py:565
  41.7 10.2 %collective-permute-start.1 = (bf16[3,128,768]{2,1,0:T(8,128)(2,1)}, bf16[3,128,768]{2,1,0:T(8,128)(2,1)}, u32[]{:S(2)}, u32[]{:S(2)}) collective-permute-start(bf16[3,128,768]{2,1,0:T(8,128)(2,1)} %slice.7), channel_id=1, source_target_pairs={{0,30},{2,4},{4,2},{6,8},{8,6},{10,12},{12,10},{14,16},{16,14},{18... | collective-permute-start | bytes 1769480 | tf_op jit(solution)/shard_map/ppermute | solution.py:566
  51.9 7.9 %all-to-all-done.1.last = bf16[8,256,512]{2,1,0:T(8,128)(2,1)} async-done(((bf16[8,256,512]{2,1,0:T(8,128)(2,1)}), bf16[8,256,512]{2,1,0:T(8,128)(2,1)}, u32[]{:S(2)}, u32[]{:S(2)}) %all-to-all-start.1) | async-done | bytes 2097184 | tf_op jit(solution)/shard_map/all_to_all | solution.py:49
  59.8 6.4 %collective-permute-start.2 = (bf16[8,256,512]{2,1,0:T(8,128)(2,1)}, bf16[8,256,512]{2,1,0:T(8,128)(2,1)S(1)}, u32[]{:S(2)}, u32[]{:S(2)}) collective-permute-start(bf16[8,256,512]{2,1,0:T(8,128)(2,1)} %all-to-all-done.1.last), channel_id=1, source_target_pairs={{0,32},{32,0},{1,33},{33,1},{2,34},{34,2},{3,35},{35,3},{4,36},{36... | collective-permute-start | bytes 6291464 | tf_op jit(solution)/shard_map/ppermute | solution.py:45
  66.2 4.4 %half.1 = (bf16[1024,2048]{1,0:T(8,128)(2,1)S(1)}, bf16[1024,2048]{1,0:T(8,128)(2,1)}, f32[496,1024]{1,0:T(8,128)S(1)}, bf16[8,16,128]{2,1,0:T(8,128)(2,1)S(1)}) custom-call(s32[3]{0:T(128)S(1)} %pad_add_fusion.place, bf16[8,128,768]{2,1,0:T(8,128)(2,1)S(1)} %all-to-all-done.first, bf16[5,128,768]{2,1,0:T(8,128)(2,1)S(1)} %collective-permute-done.near, ...), custom_call_target="tpu_custom_call" | custom-call | flops 99999997952 | bytes 100000000 | tf_op jit(solution)/shard_map/half/pallas_call | solution.py:196
  70.5 1.8 logits.1
  72.3 2.2 %collective-permute-start.3 = (bf16[1024,2048]{1,0:T(8,128)(2,1)}, bf16[1024,2048]{1,0:T(8,128)(2,1)}, u32[]{:S(2)}, u32[]{:S(2)}) collective-permute-start(bf16[1024,2048]{1,0:T(8,128)(2,1)} %get-tuple-element.40.hidden), channel_id=1, source_target_pairs={{0,32},{32,0},{1,33},{33,1},{2,34},{34,2},{3,35},{35,3},{4,36},{36... | collective-permute-start | bytes 12582920 | tf_op jit(solution)/shard_map/ppermute | solution.py:45
  74.5 13.6 %all_to_all.35.stats = f32[16,16,128]{2,1,0:T(8,128)S(1)} all-to-all(f32[16,16,128]{2,1,0:T(8,128)S(1)} %get-tuple-element.35), channel_id=1, replica_groups=mesh['y'=4,'xh'=2,'core'=2,'z'=16,'xl'=2] {'y','xh','xl'}, dimensions={0} | all-to-all | bytes 262144 | tf_op jit(solution)/shard_map/all_to_all | solution.py:49
  88.8 11.9 %all-to-all-start.3 = ((f32[16,16,128]{2,1,0:T(8,128)}), f32[16,16,128]{2,1,0:T(8,128)S(1)}, u32[]{:S(2)}, u32[]{:S(2)}) async-start(f32[16,16,128]{2,1,0:T(8,128)} %merge.1), calls=%async_computation.3 | async-start | bytes 262144 | tf_op jit(solution)/shard_map/all_to_all | solution.py:49
  101.7 11.1 %all-to-all-done.3.stats = f32[16,16,128]{2,1,0:T(8,128)S(1)} async-done(((f32[16,16,128]{2,1,0:T(8,128)}), f32[16,16,128]{2,1,0:T(8,128)S(1)}, u32[]{:S(2)}, u32[]{:S(2)}) %all-to-all-start.3) | async-done | bytes 131104 | tf_op jit(solution)/shard_map/all_to_all | solution.py:49
  112.8 2.8 %away.1 = (bf16[256,1024]{1,0:T(8,128)(2,1)S(1)}, f32[16,128]{1,0:T(8,128)S(1)}, bf16[1024,2048]{1,0:T(8,128)(2,1)S(1)}) custom-call(s32[3]{0:T(128)S(1)} %pad_add_fusion.place, f32[16,16,128]{2,1,0:T(8,128)S(1)} %all-to-all-done.3.stats, f32[504,1024]{1,0:T(8,128)S(1)} %get-tuple-element.36.logits, f32[8,1024]{1,0:T(8,128)S(1)} %get-tuple-element.39.tokens, ...), custom_call_target="tpu_custom_call" | custom-call | tf_op jit(solution)/shard_map/away/pallas_call | solution.py:377
  115.6 5.8 %collective-permute-start.4 = (bf16[256,1024]{1,0:T(8,128)(2,1)S(1)}, bf16[256,1024]{1,0:T(8,128)(2,1)S(1)}, u32[]{:S(2)}, u32[]{:S(2)}) collective-permute-start(bf16[256,1024]{1,0:T(8,128)(2,1)S(1)} %get-tuple-element.44), channel_id=1, source_target_pairs={{0,32},{32,0},{1,33},{33,1},{2,34},{34,2},{3,35},{35,3},{4,36},{36... | collective-permute-start | bytes 1572872 | tf_op jit(solution)/shard_map/ppermute | solution.py:45
  121.4 3.1 %own.1 = (f32[256,2048]{1,0:T(8,128)S(1)}, bf16[1024,2048]{1,0:T(8,128)(2,1)S(1)}) custom-call(s32[3]{0:T(128)S(1)} %pad_add_fusion.place, f32[16,128]{1,0:T(8,128)S(1)} %get-tuple-element.41.totals, f32[504,1024]{1,0:T(8,128)S(1)} %get-tuple-element.36.logits, f32[8,1024]{1,0:T(8,128)S(1)} %get-tuple-element.39.tokens, ...), custom_call_target="tpu_custom_call" | custom-call | tf_op jit(solution)/shard_map/own/pallas_call | solution.py:406
  124.5 2.4 %grad.1 = (f32[256,2048]{1,0:T(8,128)S(1)}, bf16[32,40,128]{2,1,0:T(8,128)(2,1)S(1)}) custom-call(s32[3]{0:T(128)S(1)} %pad_add_fusion.place, f32[256,2048]{1,0:T(8,128)S(1)} %get-tuple-element.43.partial, bf16[256,1024]{1,0:T(8,128)(2,1)S(1)} %collective-permute-done.4.score, bf16[1024,2048]{1,0:T(8,128)(2,1)S(1)} %get-tuple-element.45.hidden, ...), custom_call_target="tpu_custom_call" | custom-call | tf_op jit(solution)/shard_map/grad/pallas_call | solution.py:485
  126.9 12.1 %all_to_all.36.sums = bf16[32,40,128]{2,1,0:T(8,128)(2,1)S(1)} all-to-all(bf16[32,40,128]{2,1,0:T(8,128)(2,1)S(1)} %get-tuple-element.47), channel_id=1, replica_groups=mesh['y'=4,'xh'=2,'core'=2,'z'=16,'xl'=2] {'y','xh','core','xl'}, dimensions={0} | all-to-all | bytes 655360 | tf_op jit(solution)/shard_map/all_to_all | solution.py:49
  139.0 15.6 %all_to_all.37.sums = bf16[16,40,128]{2,1,0:T(8,128)(2,1)S(1)} all-to-all(bf16[16,40,128]{2,1,0:T(8,128)(2,1)S(1)} %add.32), channel_id=1, replica_groups=mesh['y'=4,'xh'=2,'core'=2,'z'=16,'xl'=2] {'z'}, dimensions={0} | all-to-all | bytes 327680 | tf_op jit(solution)/shard_map/all_to_all | solution.py:49
  155.4 24.2 %all_to_all.38 = bf16[16,248,128]{2,1,0:T(8,128)(2,1)S(1)} all-to-all(bf16[16,248,128]{2,1,0:T(8,128)(2,1)S(1)} %get-tuple-element.50), channel_id=1, replica_groups=mesh['y'=4,'xh'=2,'core'=2,'z'=16,'xl'=2] {'y','xh','core'}, dimensions={0} | all-to-all | bytes 2031616 | tf_op jit(solution)/shard_map/all_to_all | solution.py:49
  179.6 1.0 copy.10
  (25 shorter events, 4.2 us)
Async XLA Ops:
  2.8 8.3 %copy-start = (bf16[128,2048]{1,0:T(8,128)(2,1)S(1)}, bf16[128,2048]{1,0:T(8,128)(2,1)}, u32[]{:S(2)}) copy-start(bf16[128,2048]{1,0:T(8,128)(2,1)} %hidden.3) | copy-start | bytes 1572868
  2.8 8.3 %copy-start.1 = (bf16[3968,128]{1,0:T(8,128)(2,1)S(1)}, bf16[3968,128]{1,0:T(8,128)(2,1)}, u32[]{:S(2)}) copy-start(bf16[3968,128]{1,0:T(8,128)(2,1)} %head.1) | copy-start | bytes 3047428
  2.8 8.3 %copy-start.2 = (s32[128]{0:T(128)S(1)}, s32[128]{0:T(128)}, u32[]{:S(2)}) copy-start(s32[128]{0:T(128)} %param.9) | copy-start | bytes 1540
  2.8 8.3 %copy-start.3 = (s32[128]{0:T(128)S(1)}, s32[128]{0:T(128)}, u32[]{:S(2)}) copy-start(s32[128]{0:T(128)} %param.10) | copy-start | bytes 1540
  2.8 8.3 %copy-start.4 = (s32[128]{0:T(128)S(1)}, s32[128]{0:T(128)}, u32[]{:S(2)}) copy-start(s32[128]{0:T(128)} %param.11) | copy-start | bytes 1540
  2.9 8.3 %copy-start.5 = (f32[128]{0:T(128)S(1)}, f32[128]{0:T(128)}, u32[]{:S(2)}) copy-start(f32[128]{0:T(128)} %param.13) | copy-start | bytes 1540
  2.9 26.4 %all-to-all-start = ((bf16[8,128,768]{2,1,0:T(8,128)(2,1)}), bf16[8,128,768]{2,1,0:T(8,128)(2,1)S(1)}, u32[]{:S(2)}, u32[]{:S(2)}) async-start(bf16[8,128,768]{2,1,0:T(8,128)(2,1)} %spread.1), calls=%async_computation | async-start | bytes 3145728 | tf_op jit(solution)/shard_map/all_to_all | solution.py:561
  29.3 30.4 %all-to-all-start.1 = ((bf16[8,256,512]{2,1,0:T(8,128)(2,1)}), bf16[8,256,512]{2,1,0:T(8,128)(2,1)}, u32[]{:S(2)}, u32[]{:S(2)}) async-start(bf16[8,256,512]{2,1,0:T(8,128)(2,1)} %pack.1), calls=%async_computation.1 | async-start | bytes 4194304 | tf_op jit(solution)/shard_map/all_to_all | solution.py:49
  35.7 30.4 %collective-permute-start = (bf16[5,128,768]{2,1,0:T(8,128)(2,1)}, bf16[5,128,768]{2,1,0:T(8,128)(2,1)S(1)}, u32[]{:S(2)}, u32[]{:S(2)}) collective-permute-start(bf16[5,128,768]{2,1,0:T(8,128)(2,1)} %slice.6), channel_id=1, source_target_pairs={{0,2},{2,0},{4,6},{6,4},{8,10},{10,8},{12,14},{14,12},{16,18},{18,... | collective-permute-start | bytes 2949128 | tf_op jit(solution)/shard_map/ppermute | solution.py:565
  41.7 24.5 %collective-permute-start.1 = (bf16[3,128,768]{2,1,0:T(8,128)(2,1)}, bf16[3,128,768]{2,1,0:T(8,128)(2,1)}, u32[]{:S(2)}, u32[]{:S(2)}) collective-permute-start(bf16[3,128,768]{2,1,0:T(8,128)(2,1)} %slice.7), channel_id=1, source_target_pairs={{0,30},{2,4},{4,2},{6,8},{8,6},{10,12},{12,10},{14,16},{16,14},{18... | collective-permute-start | bytes 1769480 | tf_op jit(solution)/shard_map/ppermute | solution.py:566
  59.8 10.8 %collective-permute-start.2 = (bf16[8,256,512]{2,1,0:T(8,128)(2,1)}, bf16[8,256,512]{2,1,0:T(8,128)(2,1)S(1)}, u32[]{:S(2)}, u32[]{:S(2)}) collective-permute-start(bf16[8,256,512]{2,1,0:T(8,128)(2,1)} %all-to-all-done.1.last), channel_id=1, source_target_pairs={{0,32},{32,0},{1,33},{33,1},{2,34},{34,2},{3,35},{35,3},{4,36},{36... | collective-permute-start | bytes 6291464 | tf_op jit(solution)/shard_map/ppermute | solution.py:45
  72.3 49.1 %collective-permute-start.3 = (bf16[1024,2048]{1,0:T(8,128)(2,1)}, bf16[1024,2048]{1,0:T(8,128)(2,1)}, u32[]{:S(2)}, u32[]{:S(2)}) collective-permute-start(bf16[1024,2048]{1,0:T(8,128)(2,1)} %get-tuple-element.40.hidden), channel_id=1, source_target_pairs={{0,32},{32,0},{1,33},{33,1},{2,34},{34,2},{3,35},{35,3},{4,36},{36... | collective-permute-start | bytes 12582920 | tf_op jit(solution)/shard_map/ppermute | solution.py:45
  88.8 24.0 %all-to-all-start.3 = ((f32[16,16,128]{2,1,0:T(8,128)}), f32[16,16,128]{2,1,0:T(8,128)S(1)}, u32[]{:S(2)}, u32[]{:S(2)}) async-start(f32[16,16,128]{2,1,0:T(8,128)} %merge.1), calls=%async_computation.3 | async-start | bytes 262144 | tf_op jit(solution)/shard_map/all_to_all | solution.py:49
  115.6 8.9 %collective-permute-start.4 = (bf16[256,1024]{1,0:T(8,128)(2,1)S(1)}, bf16[256,1024]{1,0:T(8,128)(2,1)S(1)}, u32[]{:S(2)}, u32[]{:S(2)}) collective-permute-start(bf16[256,1024]{1,0:T(8,128)(2,1)S(1)} %get-tuple-element.44), channel_id=1, source_target_pairs={{0,32},{32,0},{1,33},{33,1},{2,34},{34,2},{3,35},{35,3},{4,36},{36... | collective-permute-start | bytes 1572872 | tf_op jit(solution)/shard_map/ppermute | solution.py:45
